TPU v7x, 512 devices: a whole 4x8x8 slice. The times are simulated.
512 devices in a mesh: gx: 16 (over z_hi, y), gy: 32 (over x, z_lo, core).
Axes of the slice: x: 4, y: 8, z: 8 (z_hi: 2, z_lo: 4; z = z_hi * 4 + z_lo), core: 2. Of those that a mesh axis runs over, the one named last changes fastest.
Arguments:
- populations: float32 [27, 64, 256, 128], P(None, 'gx', 'gy'), may hold values from 0 to 1, as said below
- cotangent: float32 [27, 64, 256, 128], P(None, 'gx', 'gy'), may hold values from -6 to 6
- porosity: float32 [64, 256, 128], P('gx', 'gy'), may hold values from 0 to 1
- cell_type: int32 [64, 256, 128], P('gx', 'gy'), may hold values from 0 to 4, as said below
- rates: float32 [27], replicated, may hold values from 0.6 to 1.9
- start_step: int32 [1], replicated, may hold values from 0 to 1023
Outputs:
- flow: float32 [27, 64, 256, 128], P(None, 'gx', 'gy')
- adjoint_populations: float32 [27, 64, 256, 128], P(None, 'gx', 'gy')
- sensitivity: float32 [64, 256, 128], P('gx', 'gy')
Inputs may be any that keep to these rules, and one draw needn't show every extreme that they name: `populations`: every population is positive. `cell_type`: 0 fluid, 1 solid, 2 inlet, 3 outlet, 4 wall; fluid cells are the most common type.
All inputs are finite; a program needn't handle non-finite values.
Results may differ from a plain program's by a relative error of at most 0.0003.
Values sent between devices are 32-bit elements; how exact they have to be, the bound alone decides.
No kernel may reach another device: no remote copies, remote signals or barrier semaphores. Data moves between devices by JAX's collectives and lax.ppermute only.
A program may use at most 64 MiB of HBM per device.

v0:
```python
import jax
import jax.numpy as jnp
import numpy as np
from jax import lax
from jax.sharding import PartitionSpec as P

STEPS = 4


line_basis = np.array([[1.0, 1.0, 1.0], [-1.0, 0.0, 1.0], [1.0, -2.0, 1.0]])
line_inverse = line_basis.T / np.array([3.0, 2.0, 6.0])
moment_basis = np.kron(np.kron(line_basis, line_basis), line_basis)
moment_inverse = np.kron(np.kron(line_inverse, line_inverse), line_inverse)
line_weight = np.array([1.0 / 6.0, 2.0 / 3.0, 1.0 / 6.0])
lattice_weight = np.kron(np.kron(line_weight, line_weight), line_weight)
lattice_vel = np.array(
    [[a - 1.0, b - 1.0, d - 1.0] for a in range(3) for b in range(3) for d in range(3)]
)
drag_max = 1.0
ramp_q = 0.1
inlet_speed = 0.3
pulse_period = 64.0


def extended(block, sides, width):
    for axis, dim in sides:
        count = lax.axis_size(axis)
        forward = [(i, i + 1) for i in range(count - 1)]
        forward.append((count - 1, 0))
        backward = [(target, source) for source, target in forward]
        low = lax.ppermute(
            lax.slice_in_dim(block, block.shape[dim] - width, None, axis=dim), axis, forward
        )
        high = lax.ppermute(lax.slice_in_dim(block, 0, width, axis=dim), axis, backward)
        block = jnp.concatenate([low, block, high], axis=dim)
    return block


def collision_matrix(rates):
    scaled = jnp.asarray(moment_inverse, jnp.float32) * rates[None, :]
    return jnp.dot(scaled, jnp.asarray(moment_basis, jnp.float32), precision=lax.Precision.HIGHEST)


def equilibrium(density, speed_x, speed_y, speed_z):
    velocity = jnp.asarray(lattice_vel, jnp.float32)
    weights = jnp.asarray(lattice_weight, jnp.float32)
    along = (
        velocity[:, 0, None, None, None] * speed_x
        + velocity[:, 1, None, None, None] * speed_y
        + velocity[:, 2, None, None, None] * speed_z
    )
    speed_sq = speed_x * speed_x + speed_y * speed_y + speed_z * speed_z
    return (
        weights[:, None, None, None]
        * density
        * (1.0 + 3.0 * along + 4.5 * along * along - 1.5 * speed_sq)
    )


def collide(state_now, gamma, cell_kind, collision, time_value):
    blocks = state_now.reshape((3, 3, 3) + state_now.shape[1:])
    density = jnp.sum(state_now, axis=0)
    speed_x = jnp.sum(blocks[2] - blocks[0], axis=(0, 1)) / density
    speed_y = jnp.sum(blocks[:, 2] - blocks[:, 0], axis=(0, 1)) / density
    speed_z = jnp.sum(blocks[:, :, 2] - blocks[:, :, 0], axis=(0, 1)) / density
    drag_coef = drag_max * ramp_q * (1.0 - gamma) / (ramp_q + gamma)
    damping = jnp.where(cell_kind == 1, 0.0, 1.0 / (1.0 + drag_coef))
    target = equilibrium(density, speed_x * damping, speed_y * damping, speed_z * damping)
    relaxed = state_now - jnp.einsum(
        "ij,jxyz->ixyz", collision, state_now - target, precision=lax.Precision.HIGHEST
    )
    unity = jnp.ones_like(density)
    inlet_eq = equilibrium(
        unity,
        0.0 * unity,
        0.0 * unity,
        inlet_speed * jnp.sin(2.0 * np.pi * time_value / pulse_period) * unity,
    )
    outlet = equilibrium(unity, speed_x, speed_y, speed_z)
    bounce = state_now[::-1]
    kinds = cell_kind[None]
    return jnp.where(
        kinds == 2, inlet_eq, jnp.where(kinds == 3, outlet, jnp.where(kinds == 4, bounce, relaxed))
    )


def shifted_copy(padded, direction):
    size_x = padded.shape[1] - 2
    size_y = padded.shape[2] - 2
    moved = []
    for index in range(27):
        offset_x = direction * int(lattice_vel[index][0])
        offset_y = direction * int(lattice_vel[index][1])
        offset_z = direction * int(lattice_vel[index][2])
        start_x = 1 - offset_x
        start_y = 1 - offset_y
        plane = padded[index, start_x : start_x + size_x, start_y : start_y + size_y]
        moved.append(jnp.roll(plane, offset_z, axis=2))
    return jnp.stack(moved)


def stream(post, direction):
    padded = extended(post, (("gx", 1), ("gy", 2)), 1)
    return shifted_copy(padded, direction)


def step_time(start_step, step):
    return (start_step[0] + step).astype(jnp.float32)


def body(populations, cotangent, porosity, cell_type, rates, start_step):
    collision = collision_matrix(rates)
    cell_kind = cell_type.astype(jnp.float32)
    states = []
    current = populations
    for step in range(STEPS):
        states.append(current)
        post = collide(current, porosity, cell_kind, collision, step_time(start_step, step))
        current = stream(post, 1)
    adjoint = cotangent
    sensitivity = jnp.zeros(porosity.shape, jnp.float32)
    for step in reversed(range(STEPS)):
        pulled = stream(adjoint, -1)
        moment = step_time(start_step, step)

        def local(values, design):
            return collide(values, design, cell_kind, collision, moment)

        _, pullback = jax.vjp(local, states[step], porosity)
        adjoint, design_grad = pullback(pulled)
        sensitivity = sensitivity + design_grad
    return (current, adjoint, sensitivity)


def solution(mesh):
    return jax.shard_map(
        body,
        mesh=mesh,
        in_specs=(
            P(None, "gx", "gy", None),
            P(None, "gx", "gy", None),
            P("gx", "gy", None),
            P("gx", "gy", None),
            P(),
            P(),
        ),
        out_specs=(P(None, "gx", "gy", None), P(None, "gx", "gy", None), P("gx", "gy", None)),
        check_vma=False,
    )
```

profile of v0, /device:TPU:199, one launch (start us, length us, event | category | flops | bytes accessed | tf_op | source)
XLA Modules:
  0.0 251.7 jit_solution(3026583706034859749)
XLA Ops:
  0.6 1.0 fusion.282
  1.7 10.8 %collective-permute-start.17 = (f32[27,1,8,128]{3,2,1,0:T(8,128)S(1)}, f32[27,1,8,128]{3,2,1,0:T(8,128)S(1)}, u32[]{:S(2)}, u32[]{:S(2)}) collective-permute-start(f32[27,1,8,128]{3,2,1,0:T(8,128)S(1)} %get-tuple-element.483), channel_id=1, source_target_pairs={{32,0},{64,32},{96,64},{128,96},{160,128},{192,160},{224,192},{256... | collective-permute-start | bytes 331784 | tf_op jit(solution)/shard_map/ppermute | solution.py:34
  12.5 1.9 collective-permute-start.16
  15.8 0.4 copy-done.7
  16.5 0.5 copy-done.8
  17.2 0.6 copy-done.6
  17.8 0.6 copy-done.5
  18.5 0.5 fusion.23
  19.1 0.6 copy-done.12
  19.7 1.3 fusion.2
  21.3 9.5 %collective-permute-start.1 = (f32[27,1,8,128]{3,2,1,0:T(8,128)S(1)}, f32[27,1,8,128]{3,2,1,0:T(8,128)S(1)}, u32[]{:S(2)}, u32[]{:S(2)}) collective-permute-start(f32[27,1,8,128]{3,2,1,0:T(8,128)S(1)} %get-tuple-element.499), channel_id=1, source_target_pairs={{32,0},{64,32},{96,64},{128,96},{160,128},{192,160},{224,192},{256... | collective-permute-start | bytes 331784 | tf_op jit(solution)/shard_map/ppermute | solution.py:34
  30.9 1.9 collective-permute-start
  33.1 10.3 %collective-permute-done = f32[27,1,8,128]{3,2,1,0:T(8,128)S(1)} collective-permute-done((f32[27,1,8,128]{3,2,1,0:T(8,128)S(1)}, f32[27,1,8,128]{3,2,1,0:T(8,128)S(1)}, u32[]{:S(2)}, u32[]{:S(2)}) %collective-permute-start) | collective-permute-done | bytes 110624 | tf_op jit(solution)/shard_map/ppermute | solution.py:31
  43.7 5.2 %collective-permute-start.3 = (f32[27,6,1,128]{3,2,1,0:T(1,128)S(1)}, f32[27,6,1,128]{3,2,1,0:T(1,128)S(1)}, u32[]{:S(2)}, u32[]{:S(2)}) collective-permute-start(f32[27,6,1,128]{3,2,1,0:T(1,128)S(1)} %get-tuple-element.409), channel_id=1, source_target_pairs={{0,1},{1,2},{2,3},{3,4},{4,5},{5,6},{6,7},{7,8},{8,9},{9,10},{10,1... | collective-permute-start | bytes 248840 | tf_op jit(solution)/shard_map/ppermute | solution.py:31
  48.8 1.9 collective-permute-start.2
  51.4 2.4 collective-permute-start.19
  53.8 7.1 %collective-permute-start.18 = (f32[27,6,1,128]{3,2,1,0:T(1,128)S(1)}, f32[27,6,1,128]{3,2,1,0:T(1,128)S(1)}, u32[]{:S(2)}, u32[]{:S(2)}) collective-permute-start(f32[27,6,1,128]{3,2,1,0:T(1,128)S(1)} %get-tuple-element.397), channel_id=1, source_target_pairs={{0,1},{1,2},{2,3},{3,4},{4,5},{5,6},{6,7},{7,8},{8,9},{9,10},{10,1... | collective-permute-start | bytes 248840 | tf_op jit(solution)/shard_map/ppermute | solution.py:31
  64.2 0.8 fusion.15
  65.0 0.6 fusion.32
  65.6 1.9 collective-permute-start.4
  67.6 9.4 %collective-permute-start.5 = (f32[27,1,8,128]{3,2,1,0:T(8,128)S(1)}, f32[27,1,8,128]{3,2,1,0:T(8,128)S(1)}, u32[]{:S(2)}, u32[]{:S(2)}) collective-permute-start(f32[27,1,8,128]{3,2,1,0:T(8,128)S(1)} %get-tuple-element.496), channel_id=1, source_target_pairs={{32,0},{64,32},{96,64},{128,96},{160,128},{192,160},{224,192},{256... | collective-permute-start | bytes 331784 | tf_op jit(solution)/shard_map/ppermute | solution.py:34
  79.5 1.9 collective-permute-start.6
  81.5 7.5 %collective-permute-start.7 = (f32[27,6,1,128]{3,2,1,0:T(1,128)S(1)}, f32[27,6,1,128]{3,2,1,0:T(1,128)S(1)}, u32[]{:S(2)}, u32[]{:S(2)}) collective-permute-start(f32[27,6,1,128]{3,2,1,0:T(1,128)S(1)} %get-tuple-element.405), channel_id=1, source_target_pairs={{0,1},{1,2},{2,3},{3,4},{4,5},{5,6},{6,7},{7,8},{8,9},{9,10},{10,1... | collective-permute-start | bytes 248840 | tf_op jit(solution)/shard_map/ppermute | solution.py:31
  89.4 1.1 collective-permute-done.7
  94.0 0.8 fusion.13
  94.8 0.6 fusion.44
  95.5 1.9 collective-permute-start.8
  97.4 9.4 %collective-permute-start.9 = (f32[27,1,8,128]{3,2,1,0:T(8,128)S(1)}, f32[27,1,8,128]{3,2,1,0:T(8,128)S(1)}, u32[]{:S(2)}, u32[]{:S(2)}) collective-permute-start(f32[27,1,8,128]{3,2,1,0:T(8,128)S(1)} %get-tuple-element.492), channel_id=1, source_target_pairs={{32,0},{64,32},{96,64},{128,96},{160,128},{192,160},{224,192},{256... | collective-permute-start | bytes 331784 | tf_op jit(solution)/shard_map/ppermute | solution.py:34
  107.1 1.4 collective-permute-done.9
  108.6 1.9 collective-permute-start.10
  110.6 9.5 %collective-permute-start.11 = (f32[27,6,1,128]{3,2,1,0:T(1,128)S(1)}, f32[27,6,1,128]{3,2,1,0:T(1,128)S(1)}, u32[]{:S(2)}, u32[]{:S(2)}) collective-permute-start(f32[27,6,1,128]{3,2,1,0:T(1,128)S(1)} %get-tuple-element.402), channel_id=1, source_target_pairs={{0,1},{1,2},{2,3},{3,4},{4,5},{5,6},{6,7},{7,8},{8,9},{9,10},{10,1... | collective-permute-start | bytes 248840 | tf_op jit(solution)/shard_map/ppermute | solution.py:31
  120.4 1.0 collective-permute-done.11
  124.9 0.8 fusion.9
  125.8 1.0 multiply_reduce_fusion.26
  127.4 1.9 collective-permute-start.20
  129.3 10.1 %collective-permute-start.21 = (f32[27,1,8,128]{3,2,1,0:T(8,128)S(1)}, f32[27,1,8,128]{3,2,1,0:T(8,128)S(1)}, u32[]{:S(2)}, u32[]{:S(2)}) collective-permute-start(f32[27,1,8,128]{3,2,1,0:T(8,128)S(1)} %get-tuple-element.477), channel_id=1, source_target_pairs={{32,0},{64,32},{96,64},{128,96},{160,128},{192,160},{224,192},{256... | collective-permute-start | bytes 331784 | tf_op jit(solution)/shard_map/ppermute | solution.py:34
  139.6 1.5 collective-permute-done.21
  141.2 9.1 %collective-permute-start.22 = (f32[27,6,1,128]{3,2,1,0:T(1,128)S(1)}, f32[27,6,1,128]{3,2,1,0:T(1,128)S(1)}, u32[]{:S(2)}, u32[]{:S(2)}) collective-permute-start(f32[27,6,1,128]{3,2,1,0:T(1,128)S(1)} %get-tuple-element.394), channel_id=1, source_target_pairs={{0,1},{1,2},{2,3},{3,4},{4,5},{5,6},{6,7},{7,8},{8,9},{9,10},{10,1... | collective-permute-start | bytes 248840 | tf_op jit(solution)/shard_map/ppermute | solution.py:31
  150.3 0.8 fusion.11
  151.1 1.9 collective-permute-start.23
  153.3 7.5 %collective-permute-done.23 = f32[27,6,1,128]{3,2,1,0:T(1,128)S(1)} collective-permute-done((f32[27,6,1,128]{3,2,1,0:T(1,128)S(1)}, f32[27,6,1,128]{3,2,1,0:T(1,128)S(1)}, u32[]{:S(2)}, u32[]{:S(2)}) %collective-permute-start.23) | collective-permute-done | bytes 82976 | tf_op jit(solution)/shard_map/ppermute | solution.py:34
  163.4 0.8 fusion.76
  164.3 1.9 collective-permute-start.12
  166.2 11.2 %collective-permute-start.13 = (f32[27,1,8,128]{3,2,1,0:T(8,128)S(1)}, f32[27,1,8,128]{3,2,1,0:T(8,128)S(1)}, u32[]{:S(2)}, u32[]{:S(2)}) collective-permute-start(f32[27,1,8,128]{3,2,1,0:T(8,128)S(1)} %get-tuple-element.488), channel_id=1, source_target_pairs={{32,0},{64,32},{96,64},{128,96},{160,128},{192,160},{224,192},{256... | collective-permute-start | bytes 331784 | tf_op jit(solution)/shard_map/ppermute | solution.py:34
  177.4 0.8 fusion.7
  178.2 1.0 multiply_reduce_fusion.19
  179.9 1.9 collective-permute-start.24
  181.8 9.4 %collective-permute-start.25 = (f32[27,1,8,128]{3,2,1,0:T(8,128)S(1)}, f32[27,1,8,128]{3,2,1,0:T(8,128)S(1)}, u32[]{:S(2)}, u32[]{:S(2)}) collective-permute-start(f32[27,1,8,128]{3,2,1,0:T(8,128)S(1)} %get-tuple-element.473), channel_id=1, source_target_pairs={{32,0},{64,32},{96,64},{128,96},{160,128},{192,160},{224,192},{256... | collective-permute-start | bytes 331784 | tf_op jit(solution)/shard_map/ppermute | solution.py:34
  191.3 2.6 %collective-permute-start.15 = (f32[27,6,1,128]{3,2,1,0:T(1,128)S(1)}, f32[27,6,1,128]{3,2,1,0:T(1,128)S(1)}, u32[]{:S(2)}, u32[]{:S(2)}) collective-permute-start(f32[27,6,1,128]{3,2,1,0:T(1,128)S(1)} %get-tuple-element.399), channel_id=1, source_target_pairs={{0,1},{1,2},{2,3},{3,4},{4,5},{5,6},{6,7},{7,8},{8,9},{9,10},{10,1... | collective-permute-start | bytes 248840 | tf_op jit(solution)/shard_map/ppermute | solution.py:31
  193.9 1.9 collective-permute-start.14
  196.0 1.9 collective-permute-start.27
  197.9 7.8 %collective-permute-start.26 = (f32[27,6,1,128]{3,2,1,0:T(1,128)S(1)}, f32[27,6,1,128]{3,2,1,0:T(1,128)S(1)}, u32[]{:S(2)}, u32[]{:S(2)}) collective-permute-start(f32[27,6,1,128]{3,2,1,0:T(1,128)S(1)} %get-tuple-element.391), channel_id=1, source_target_pairs={{0,1},{1,2},{2,3},{3,4},{4,5},{5,6},{6,7},{7,8},{8,9},{9,10},{10,1... | collective-permute-start | bytes 248840 | tf_op jit(solution)/shard_map/ppermute | solution.py:31
  211.3 0.8 fusion.5
  212.1 1.0 multiply_reduce_fusion.12
  213.7 1.9 collective-permute-start.28
  215.6 9.4 %collective-permute-start.29 = (f32[27,1,8,128]{3,2,1,0:T(8,128)S(1)}, f32[27,1,8,128]{3,2,1,0:T(8,128)S(1)}, u32[]{:S(2)}, u32[]{:S(2)}) collective-permute-start(f32[27,1,8,128]{3,2,1,0:T(8,128)S(1)} %get-tuple-element.469), channel_id=1, source_target_pairs={{32,0},{64,32},{96,64},{128,96},{160,128},{192,160},{224,192},{256... | collective-permute-start | bytes 331784 | tf_op jit(solution)/shard_map/ppermute | solution.py:34
  225.4 1.3 collective-permute-done.29
  226.9 8.2 %collective-permute-start.30 = (f32[27,6,1,128]{3,2,1,0:T(1,128)S(1)}, f32[27,6,1,128]{3,2,1,0:T(1,128)S(1)}, u32[]{:S(2)}, u32[]{:S(2)}) collective-permute-start(f32[27,6,1,128]{3,2,1,0:T(1,128)S(1)} %get-tuple-element.388), channel_id=1, source_target_pairs={{0,1},{1,2},{2,3},{3,4},{4,5},{5,6},{6,7},{7,8},{8,9},{9,10},{10,1... | collective-permute-start | bytes 248840 | tf_op jit(solution)/shard_map/ppermute | solution.py:31
  235.2 1.9 collective-permute-start.31
  237.4 7.5 %collective-permute-done.31 = f32[27,6,1,128]{3,2,1,0:T(1,128)S(1)} collective-permute-done((f32[27,6,1,128]{3,2,1,0:T(1,128)S(1)}, f32[27,6,1,128]{3,2,1,0:T(1,128)S(1)}, u32[]{:S(2)}, u32[]{:S(2)}) %collective-permute-start.31) | collective-permute-done | bytes 82976 | tf_op jit(solution)/shard_map/ppermute | solution.py:34
  247.8 0.8 fusion.3
  248.6 0.9 multiply_reduce_fusion.5
  249.6 0.8 add_add_fusion
  250.6 1.1 bitcast_add_fusion
  (565 shorter events, 29.8 us)
Async XLA Ops:
  0.6 14.8 %copy-start = (f32[27,4,8,128]{3,2,1,0:T(8,128)S(1)}, f32[27,4,8,128]{3,2,1,0:T(8,128)}, u32[]{:S(2)}) copy-start(f32[27,4,8,128]{3,2,1,0:T(8,128)} %param.48) | copy-start | bytes 1327108
  1.7 49.2 %collective-permute-start.17 = (f32[27,1,8,128]{3,2,1,0:T(8,128)S(1)}, f32[27,1,8,128]{3,2,1,0:T(8,128)S(1)}, u32[]{:S(2)}, u32[]{:S(2)}) collective-permute-start(f32[27,1,8,128]{3,2,1,0:T(8,128)S(1)} %get-tuple-element.483), channel_id=1, source_target_pairs={{32,0},{64,32},{96,64},{128,96},{160,128},{192,160},{224,192},{256... | collective-permute-start | bytes 331784 | tf_op jit(solution)/shard_map/ppermute | solution.py:34
  12.5 38.3 %collective-permute-start.16 = (f32[27,1,8,128]{3,2,1,0:T(8,128)S(1)}, f32[27,1,8,128]{3,2,1,0:T(8,128)S(1)}, u32[]{:S(2)}, u32[]{:S(2)}) collective-permute-start(f32[27,1,8,128]{3,2,1,0:T(8,128)S(1)} %get-tuple-element.484), channel_id=1, source_target_pairs={{0,32},{32,64},{64,96},{96,128},{128,160},{160,192},{192,224},{224... | collective-permute-start | bytes 331784 | tf_op jit(solution)/shard_map/ppermute | solution.py:31
  15.5 0.7 copy-start.7
  16.3 0.7 copy-start.8
  16.3 0.7 copy-start.9
  16.3 0.7 copy-start.11
  17.0 0.7 copy-start.6
  17.8 0.7 copy-start.5
  17.8 0.7 copy-start.2
  17.8 0.7 copy-start.3
  17.8 0.7 copy-start.4
  19.0 0.7 copy-start.12
  19.1 0.7 copy-start.13
  21.3 11.5 %copy-start.1 = (f32[27,4,8,128]{3,2,1,0:T(8,128)S(1)}, f32[27,4,8,128]{3,2,1,0:T(8,128)}, u32[]{:S(2)}) copy-start(f32[27,4,8,128]{3,2,1,0:T(8,128)} %param.49) | copy-start | bytes 1327108
  21.3 22.2 %collective-permute-start.1 = (f32[27,1,8,128]{3,2,1,0:T(8,128)S(1)}, f32[27,1,8,128]{3,2,1,0:T(8,128)S(1)}, u32[]{:S(2)}, u32[]{:S(2)}) collective-permute-start(f32[27,1,8,128]{3,2,1,0:T(8,128)S(1)} %get-tuple-element.499), channel_id=1, source_target_pairs={{32,0},{64,32},{96,64},{128,96},{160,128},{192,160},{224,192},{256... | collective-permute-start | bytes 331784 | tf_op jit(solution)/shard_map/ppermute | solution.py:34
  30.9 12.6 %collective-permute-start = (f32[27,1,8,128]{3,2,1,0:T(8,128)S(1)}, f32[27,1,8,128]{3,2,1,0:T(8,128)S(1)}, u32[]{:S(2)}, u32[]{:S(2)}) collective-permute-start(f32[27,1,8,128]{3,2,1,0:T(8,128)S(1)} %get-tuple-element.500), channel_id=1, source_target_pairs={{0,32},{32,64},{64,96},{96,128},{128,160},{160,192},{192,224},{224... | collective-permute-start | bytes 331784 | tf_op jit(solution)/shard_map/ppermute | solution.py:31
  43.7 17.5 %collective-permute-start.3 = (f32[27,6,1,128]{3,2,1,0:T(1,128)S(1)}, f32[27,6,1,128]{3,2,1,0:T(1,128)S(1)}, u32[]{:S(2)}, u32[]{:S(2)}) collective-permute-start(f32[27,6,1,128]{3,2,1,0:T(1,128)S(1)} %get-tuple-element.409), channel_id=1, source_target_pairs={{0,1},{1,2},{2,3},{3,4},{4,5},{5,6},{6,7},{7,8},{8,9},{9,10},{10,1... | collective-permute-start | bytes 248840 | tf_op jit(solution)/shard_map/ppermute | solution.py:31
  48.8 12.0 %collective-permute-start.2 = (f32[27,6,1,128]{3,2,1,0:T(1,128)S(1)}, f32[27,6,1,128]{3,2,1,0:T(1,128)S(1)}, u32[]{:S(2)}, u32[]{:S(2)}) collective-permute-start(f32[27,6,1,128]{3,2,1,0:T(1,128)S(1)} %get-tuple-element.410), channel_id=1, source_target_pairs={{1,0},{2,1},{3,2},{4,3},{5,4},{6,5},{7,6},{8,7},{9,8},{10,9},{11,1... | collective-permute-start | bytes 248840 | tf_op jit(solution)/shard_map/ppermute | solution.py:34
  51.4 25.8 %collective-permute-start.19 = (f32[27,6,1,128]{3,2,1,0:T(1,128)S(1)}, f32[27,6,1,128]{3,2,1,0:T(1,128)S(1)}, u32[]{:S(2)}, u32[]{:S(2)}) collective-permute-start(f32[27,6,1,128]{3,2,1,0:T(1,128)S(1)} %get-tuple-element.396), channel_id=1, source_target_pairs={{1,0},{2,1},{3,2},{4,3},{5,4},{6,5},{7,6},{8,7},{9,8},{10,9},{11,1... | collective-permute-start | bytes 248840 | tf_op jit(solution)/shard_map/ppermute | solution.py:34
  53.8 23.2 %collective-permute-start.18 = (f32[27,6,1,128]{3,2,1,0:T(1,128)S(1)}, f32[27,6,1,128]{3,2,1,0:T(1,128)S(1)}, u32[]{:S(2)}, u32[]{:S(2)}) collective-permute-start(f32[27,6,1,128]{3,2,1,0:T(1,128)S(1)} %get-tuple-element.397), channel_id=1, source_target_pairs={{0,1},{1,2},{2,3},{3,4},{4,5},{5,6},{6,7},{7,8},{8,9},{9,10},{10,1... | collective-permute-start | bytes 248840 | tf_op jit(solution)/shard_map/ppermute | solution.py:31
  65.6 13.7 %collective-permute-start.4 = (f32[27,1,8,128]{3,2,1,0:T(8,128)S(1)}, f32[27,1,8,128]{3,2,1,0:T(8,128)S(1)}, u32[]{:S(2)}, u32[]{:S(2)}) collective-permute-start(f32[27,1,8,128]{3,2,1,0:T(8,128)S(1)} %get-tuple-element.495), channel_id=1, source_target_pairs={{0,32},{32,64},{64,96},{96,128},{128,160},{160,192},{192,224},{224... | collective-permute-start | bytes 331784 | tf_op jit(solution)/shard_map/ppermute | solution.py:31
  67.6 11.8 %collective-permute-start.5 = (f32[27,1,8,128]{3,2,1,0:T(8,128)S(1)}, f32[27,1,8,128]{3,2,1,0:T(8,128)S(1)}, u32[]{:S(2)}, u32[]{:S(2)}) collective-permute-start(f32[27,1,8,128]{3,2,1,0:T(8,128)S(1)} %get-tuple-element.496), channel_id=1, source_target_pairs={{32,0},{64,32},{96,64},{128,96},{160,128},{192,160},{224,192},{256... | collective-permute-start | bytes 331784 | tf_op jit(solution)/shard_map/ppermute | solution.py:34
  79.5 9.7 %collective-permute-start.6 = (f32[27,6,1,128]{3,2,1,0:T(1,128)S(1)}, f32[27,6,1,128]{3,2,1,0:T(1,128)S(1)}, u32[]{:S(2)}, u32[]{:S(2)}) collective-permute-start(f32[27,6,1,128]{3,2,1,0:T(1,128)S(1)} %get-tuple-element.406), channel_id=1, source_target_pairs={{1,0},{2,1},{3,2},{4,3},{5,4},{6,5},{7,6},{8,7},{9,8},{10,9},{11,1... | collective-permute-start | bytes 248840 | tf_op jit(solution)/shard_map/ppermute | solution.py:34
  81.5 9.0 %collective-permute-start.7 = (f32[27,6,1,128]{3,2,1,0:T(1,128)S(1)}, f32[27,6,1,128]{3,2,1,0:T(1,128)S(1)}, u32[]{:S(2)}, u32[]{:S(2)}) collective-permute-start(f32[27,6,1,128]{3,2,1,0:T(1,128)S(1)} %get-tuple-element.405), channel_id=1, source_target_pairs={{0,1},{1,2},{2,3},{3,4},{4,5},{5,6},{6,7},{7,8},{8,9},{9,10},{10,1... | collective-permute-start | bytes 248840 | tf_op jit(solution)/shard_map/ppermute | solution.py:31
  95.5 11.6 %collective-permute-start.8 = (f32[27,1,8,128]{3,2,1,0:T(8,128)S(1)}, f32[27,1,8,128]{3,2,1,0:T(8,128)S(1)}, u32[]{:S(2)}, u32[]{:S(2)}) collective-permute-start(f32[27,1,8,128]{3,2,1,0:T(8,128)S(1)} %get-tuple-element.491), channel_id=1, source_target_pairs={{0,32},{32,64},{64,96},{96,128},{128,160},{160,192},{192,224},{224... | collective-permute-start | bytes 331784 | tf_op jit(solution)/shard_map/ppermute | solution.py:31
  97.4 11.1 %collective-permute-start.9 = (f32[27,1,8,128]{3,2,1,0:T(8,128)S(1)}, f32[27,1,8,128]{3,2,1,0:T(8,128)S(1)}, u32[]{:S(2)}, u32[]{:S(2)}) collective-permute-start(f32[27,1,8,128]{3,2,1,0:T(8,128)S(1)} %get-tuple-element.492), channel_id=1, source_target_pairs={{32,0},{64,32},{96,64},{128,96},{160,128},{192,160},{224,192},{256... | collective-permute-start | bytes 331784 | tf_op jit(solution)/shard_map/ppermute | solution.py:34
  108.6 11.5 %collective-permute-start.10 = (f32[27,6,1,128]{3,2,1,0:T(1,128)S(1)}, f32[27,6,1,128]{3,2,1,0:T(1,128)S(1)}, u32[]{:S(2)}, u32[]{:S(2)}) collective-permute-start(f32[27,6,1,128]{3,2,1,0:T(1,128)S(1)} %get-tuple-element.403), channel_id=1, source_target_pairs={{1,0},{2,1},{3,2},{4,3},{5,4},{6,5},{7,6},{8,7},{9,8},{10,9},{11,1... | collective-permute-start | bytes 248840 | tf_op jit(solution)/shard_map/ppermute | solution.py:34
  110.6 10.8 %collective-permute-start.11 = (f32[27,6,1,128]{3,2,1,0:T(1,128)S(1)}, f32[27,6,1,128]{3,2,1,0:T(1,128)S(1)}, u32[]{:S(2)}, u32[]{:S(2)}) collective-permute-start(f32[27,6,1,128]{3,2,1,0:T(1,128)S(1)} %get-tuple-element.402), channel_id=1, source_target_pairs={{0,1},{1,2},{2,3},{3,4},{4,5},{5,6},{6,7},{7,8},{8,9},{9,10},{10,1... | collective-permute-start | bytes 248840 | tf_op jit(solution)/shard_map/ppermute | solution.py:31
  127.4 12.2 %collective-permute-start.20 = (f32[27,1,8,128]{3,2,1,0:T(8,128)S(1)}, f32[27,1,8,128]{3,2,1,0:T(8,128)S(1)}, u32[]{:S(2)}, u32[]{:S(2)}) collective-permute-start(f32[27,1,8,128]{3,2,1,0:T(8,128)S(1)} %get-tuple-element.476), channel_id=1, source_target_pairs={{0,32},{32,64},{64,96},{96,128},{128,160},{160,192},{192,224},{224... | collective-permute-start | bytes 331784 | tf_op jit(solution)/shard_map/ppermute | solution.py:31
  129.3 11.8 %collective-permute-start.21 = (f32[27,1,8,128]{3,2,1,0:T(8,128)S(1)}, f32[27,1,8,128]{3,2,1,0:T(8,128)S(1)}, u32[]{:S(2)}, u32[]{:S(2)}) collective-permute-start(f32[27,1,8,128]{3,2,1,0:T(8,128)S(1)} %get-tuple-element.477), channel_id=1, source_target_pairs={{32,0},{64,32},{96,64},{128,96},{160,128},{192,160},{224,192},{256... | collective-permute-start | bytes 331784 | tf_op jit(solution)/shard_map/ppermute | solution.py:34
  141.2 11.8 %collective-permute-start.22 = (f32[27,6,1,128]{3,2,1,0:T(1,128)S(1)}, f32[27,6,1,128]{3,2,1,0:T(1,128)S(1)}, u32[]{:S(2)}, u32[]{:S(2)}) collective-permute-start(f32[27,6,1,128]{3,2,1,0:T(1,128)S(1)} %get-tuple-element.394), channel_id=1, source_target_pairs={{0,1},{1,2},{2,3},{3,4},{4,5},{5,6},{6,7},{7,8},{8,9},{9,10},{10,1... | collective-permute-start | bytes 248840 | tf_op jit(solution)/shard_map/ppermute | solution.py:31
  151.1 9.7 %collective-permute-start.23 = (f32[27,6,1,128]{3,2,1,0:T(1,128)S(1)}, f32[27,6,1,128]{3,2,1,0:T(1,128)S(1)}, u32[]{:S(2)}, u32[]{:S(2)}) collective-permute-start(f32[27,6,1,128]{3,2,1,0:T(1,128)S(1)} %get-tuple-element.393), channel_id=1, source_target_pairs={{1,0},{2,1},{3,2},{4,3},{5,4},{6,5},{7,6},{8,7},{9,8},{10,9},{11,1... | collective-permute-start | bytes 248840 | tf_op jit(solution)/shard_map/ppermute | solution.py:34
  164.3 26.9 %collective-permute-start.12 = (f32[27,1,8,128]{3,2,1,0:T(8,128)S(1)}, f32[27,1,8,128]{3,2,1,0:T(8,128)S(1)}, u32[]{:S(2)}, u32[]{:S(2)}) collective-permute-start(f32[27,1,8,128]{3,2,1,0:T(8,128)S(1)} %get-tuple-element.487), channel_id=1, source_target_pairs={{0,32},{32,64},{64,96},{96,128},{128,160},{160,192},{192,224},{224... | collective-permute-start | bytes 331784 | tf_op jit(solution)/shard_map/ppermute | solution.py:31
  166.2 25.0 %collective-permute-start.13 = (f32[27,1,8,128]{3,2,1,0:T(8,128)S(1)}, f32[27,1,8,128]{3,2,1,0:T(8,128)S(1)}, u32[]{:S(2)}, u32[]{:S(2)}) collective-permute-start(f32[27,1,8,128]{3,2,1,0:T(8,128)S(1)} %get-tuple-element.488), channel_id=1, source_target_pairs={{32,0},{64,32},{96,64},{128,96},{160,128},{192,160},{224,192},{256... | collective-permute-start | bytes 331784 | tf_op jit(solution)/shard_map/ppermute | solution.py:34
  179.9 16.0 %collective-permute-start.24 = (f32[27,1,8,128]{3,2,1,0:T(8,128)S(1)}, f32[27,1,8,128]{3,2,1,0:T(8,128)S(1)}, u32[]{:S(2)}, u32[]{:S(2)}) collective-permute-start(f32[27,1,8,128]{3,2,1,0:T(8,128)S(1)} %get-tuple-element.472), channel_id=1, source_target_pairs={{0,32},{32,64},{64,96},{96,128},{128,160},{160,192},{192,224},{224... | collective-permute-start | bytes 331784 | tf_op jit(solution)/shard_map/ppermute | solution.py:31
  181.8 14.1 %collective-permute-start.25 = (f32[27,1,8,128]{3,2,1,0:T(8,128)S(1)}, f32[27,1,8,128]{3,2,1,0:T(8,128)S(1)}, u32[]{:S(2)}, u32[]{:S(2)}) collective-permute-start(f32[27,1,8,128]{3,2,1,0:T(8,128)S(1)} %get-tuple-element.473), channel_id=1, source_target_pairs={{32,0},{64,32},{96,64},{128,96},{160,128},{192,160},{224,192},{256... | collective-permute-start | bytes 331784 | tf_op jit(solution)/shard_map/ppermute | solution.py:34
  191.3 14.6 %collective-permute-start.15 = (f32[27,6,1,128]{3,2,1,0:T(1,128)S(1)}, f32[27,6,1,128]{3,2,1,0:T(1,128)S(1)}, u32[]{:S(2)}, u32[]{:S(2)}) collective-permute-start(f32[27,6,1,128]{3,2,1,0:T(1,128)S(1)} %get-tuple-element.399), channel_id=1, source_target_pairs={{0,1},{1,2},{2,3},{3,4},{4,5},{5,6},{6,7},{7,8},{8,9},{9,10},{10,1... | collective-permute-start | bytes 248840 | tf_op jit(solution)/shard_map/ppermute | solution.py:31
  193.9 11.8 %collective-permute-start.14 = (f32[27,6,1,128]{3,2,1,0:T(1,128)S(1)}, f32[27,6,1,128]{3,2,1,0:T(1,128)S(1)}, u32[]{:S(2)}, u32[]{:S(2)}) collective-permute-start(f32[27,6,1,128]{3,2,1,0:T(1,128)S(1)} %get-tuple-element.400), channel_id=1, source_target_pairs={{1,0},{2,1},{3,2},{4,3},{5,4},{6,5},{7,6},{8,7},{9,8},{10,9},{11,1... | collective-permute-start | bytes 248840 | tf_op jit(solution)/shard_map/ppermute | solution.py:34
  196.0 12.3 %collective-permute-start.27 = (f32[27,6,1,128]{3,2,1,0:T(1,128)S(1)}, f32[27,6,1,128]{3,2,1,0:T(1,128)S(1)}, u32[]{:S(2)}, u32[]{:S(2)}) collective-permute-start(f32[27,6,1,128]{3,2,1,0:T(1,128)S(1)} %get-tuple-element.390), channel_id=1, source_target_pairs={{1,0},{2,1},{3,2},{4,3},{5,4},{6,5},{7,6},{8,7},{9,8},{10,9},{11,1... | collective-permute-start | bytes 248840 | tf_op jit(solution)/shard_map/ppermute | solution.py:34
  197.9 10.2 %collective-permute-start.26 = (f32[27,6,1,128]{3,2,1,0:T(1,128)S(1)}, f32[27,6,1,128]{3,2,1,0:T(1,128)S(1)}, u32[]{:S(2)}, u32[]{:S(2)}) collective-permute-start(f32[27,6,1,128]{3,2,1,0:T(1,128)S(1)} %get-tuple-element.391), channel_id=1, source_target_pairs={{0,1},{1,2},{2,3},{3,4},{4,5},{5,6},{6,7},{7,8},{8,9},{9,10},{10,1... | collective-permute-start | bytes 248840 | tf_op jit(solution)/shard_map/ppermute | solution.py:31
  213.7 11.7 %collective-permute-start.28 = (f32[27,1,8,128]{3,2,1,0:T(8,128)S(1)}, f32[27,1,8,128]{3,2,1,0:T(8,128)S(1)}, u32[]{:S(2)}, u32[]{:S(2)}) collective-permute-start(f32[27,1,8,128]{3,2,1,0:T(8,128)S(1)} %get-tuple-element.468), channel_id=1, source_target_pairs={{0,32},{32,64},{64,96},{96,128},{128,160},{160,192},{192,224},{224... | collective-permute-start | bytes 331784 | tf_op jit(solution)/shard_map/ppermute | solution.py:31
  215.6 11.1 %collective-permute-start.29 = (f32[27,1,8,128]{3,2,1,0:T(8,128)S(1)}, f32[27,1,8,128]{3,2,1,0:T(8,128)S(1)}, u32[]{:S(2)}, u32[]{:S(2)}) collective-permute-start(f32[27,1,8,128]{3,2,1,0:T(8,128)S(1)} %get-tuple-element.469), channel_id=1, source_target_pairs={{32,0},{64,32},{96,64},{128,96},{160,128},{192,160},{224,192},{256... | collective-permute-start | bytes 331784 | tf_op jit(solution)/shard_map/ppermute | solution.py:34
  226.9 10.2 %collective-permute-start.30 = (f32[27,6,1,128]{3,2,1,0:T(1,128)S(1)}, f32[27,6,1,128]{3,2,1,0:T(1,128)S(1)}, u32[]{:S(2)}, u32[]{:S(2)}) collective-permute-start(f32[27,6,1,128]{3,2,1,0:T(1,128)S(1)} %get-tuple-element.388), channel_id=1, source_target_pairs={{0,1},{1,2},{2,3},{3,4},{4,5},{5,6},{6,7},{7,8},{8,9},{9,10},{10,1... | collective-permute-start | bytes 248840 | tf_op jit(solution)/shard_map/ppermute | solution.py:31
  235.2 2.2 copy-start.10
  235.2 9.7 %collective-permute-start.31 = (f32[27,6,1,128]{3,2,1,0:T(1,128)S(1)}, f32[27,6,1,128]{3,2,1,0:T(1,128)S(1)}, u32[]{:S(2)}, u32[]{:S(2)}) collective-permute-start(f32[27,6,1,128]{3,2,1,0:T(1,128)S(1)} %get-tuple-element.387), channel_id=1, source_target_pairs={{1,0},{2,1},{3,2},{4,3},{5,4},{6,5},{7,6},{8,7},{9,8},{10,9},{11,1... | collective-permute-start | bytes 248840 | tf_op jit(solution)/shard_map/ppermute | solution.py:34
where the time goes:
time: 253 us; the launch traced here: 252 us
  starting transfers between devices  167 us (66%)
  waiting for transfers between devices  32.4 us (13%)
  other arithmetic  25 us (10%)
  local copies, waits for them, and re-layouts  16.1 us (6%)
  matrix products  7.21 us (3%)
  between operations  3.74 us (1%)
    ppermute x16, starting transfers between devices, extended(): lax.ppermute(lax.slice_in_dim(block, 0, width, axis=dim), axis, backward)  94.9 us
    ppermute x16, starting transfers between devices, extended(): lax.ppermute(lax.slice_in_dim(block, block.shape[dim] - width, None, axis...  72.3 us
    ppermute x16, waiting for transfers between devices, extended(): lax.ppermute(lax.slice_in_dim(block, 0, width, axis=dim), axis, backward)  19.4 us
    ppermute x16, waiting for transfers between devices, extended(): lax.ppermute(lax.slice_in_dim(block, block.shape[dim] - width, None, axis...  12.9 us
    slice x144, local copies, waits for them, and re-layouts, shifted_copy(): moved.append(jnp.roll(plane, offset_z, axis=2))  10.4 us
    unnamed x142, other arithmetic  10.1 us
    dot_general x8, matrix products, collide(): jnp.einsum('ij,jxyz->ixyz', collision, state_now - target, precision=lax....  7.08 us
  transfers between devices with their start and end apart: 32, of which 11 were waited for; matrix products, arithmetic and copies ran while one was open for 7% of the time, Pallas kernels for 0%

commit v1 on v0

v1 whole, which is shorter than its diff:
```python
import jax
import jax.numpy as jnp
import numpy as np
from jax import lax
from jax.experimental import pallas as pl
from jax.experimental.pallas import tpu as pltpu
from jax.sharding import PartitionSpec as P

DRAG_MAX = 1.0
RAMP_Q = 0.1
INLET_SPEED = 0.3
PULSE_PERIOD = 64

NX, NY, LANES = 4, 8, 128
HALO = 3
PLANES = NX + 2 * HALO
ROWS = 3 * NY
VMEM_LIMIT = 48 * 1024 * 1024

SCALE = [
    float(s)
    for s in np.kron(np.kron([1 / 3, 1 / 2, 1 / 6], [1 / 3, 1 / 2, 1 / 6]), [1 / 3, 1 / 2, 1 / 6])
]
VEL = [(a - 1, b - 1, d - 1) for a in range(3) for b in range(3) for d in range(3)]
ODD = [(c[0] == 0) ^ (c[1] == 0) ^ (c[2] == 0) for c in VEL]


def reach(component, side, width, direction):
    if direction == 0:
        return width
    inward = -side * direction
    return max(0, width - (0 if component == inward else 1 if component == 0 else 2))


def member_reach(field, i, axis, side):
    _, _, width, direction = field
    return reach(VEL[i][axis] if direction else 0, side, width, direction)


def plan_x(fields, side):
    places = {}
    for field in fields:
        for layer in range(1, field[2] + 1):
            for i in range(field[1]):
                if member_reach(field, i, 0, side) >= layer:
                    places[field[0], i, layer] = len(places)
    return places, len(places)


def plan_y(fields, side):
    entries, start = [], 0
    for field in fields:
        for plane in range(-field[2], NX + field[2]):
            for i in range(field[1]):
                if plane < 0 and member_reach(field, i, 0, -1) < -plane:
                    continue
                if plane >= NX and member_reach(field, i, 0, 1) < plane - NX + 1:
                    continue
                rows = member_reach(field, i, 1, side)
                if rows:
                    entries.append((field[0], i, plane, start, rows))
                    start += rows
    return entries, -(-start // 8) * 8


FIRST = (("post", 27, 3, 1), ("adjoint", 27, 1, -1), ("cell", 2, 2, 0))
SECOND = (("adjoint", 27, 3, -1), ("post", 27, 1, 1), ("speed", 4, 2, 0))
PLAN_X = {(f, s): plan_x(f, s) for f in (FIRST, SECOND) for s in (-1, 1)}
PLAN_Y = {(f, s): plan_y(f, s) for f in (FIRST, SECOND) for s in (-1, 1)}


def pack_x(fields, side, read, out):
    for (name, i, layer), place in PLAN_X[fields, side][0].items():
        out[place] = read(name, i, layer - 1 if side > 0 else NX - layer)


def halo_tile(fields, from_low, from_high, name, i, plane):
    if plane < 0:
        return from_low, PLAN_X[fields, -1][0][name, i, -plane]
    return from_high, PLAN_X[fields, 1][0][name, i, plane - NX + 1]


def pack_y(fields, side, own, from_low, from_high, out):
    for name, i, plane, start, rows in PLAN_Y[fields, side][0]:
        first = 0 if side > 0 else NY - rows
        if 0 <= plane < NX:
            out[start : start + rows] = own(name, i, plane, first, rows)
        else:
            ref, place = halo_tile(fields, from_low, from_high, name, i, plane)
            out[start : start + rows] = ref[place, first : first + rows]


def unpack(fields, wide, from_x, from_y):
    for side, ref in zip((-1, 1), from_x):
        for (name, i, layer), place in PLAN_X[fields, side][0].items():
            plane = NX - 1 + layer if side > 0 else -layer
            wide[name][i, plane + HALO, NY : 2 * NY] = ref[place]
    for side, ref in zip((-1, 1), from_y):
        for name, i, plane, start, rows in PLAN_Y[fields, side][0]:
            first = 2 * NY if side > 0 else NY - rows
            wide[name][i, plane + HALO, first : first + rows] = ref[start : start + rows]


def moments(f):
    v = list(f)
    for stride in (9, 3, 1):
        for i in range(27):
            if (i // stride) % 3 == 0:
                a, b, c = v[i], v[i + stride], v[i + 2 * stride]
                s = (a + c) + b
                v[i], v[i + stride], v[i + 2 * stride] = s, c - a, s - 3.0 * b
    return v


def moments_transposed(m):
    v = list(m)
    for stride in (9, 3, 1):
        for i in range(27):
            if (i // stride) % 3 == 0:
                s, d, q = v[i], v[i + stride], v[i + 2 * stride]
                t = s + q
                v[i], v[i + stride], v[i + 2 * stride] = t - d, s - (q + q), t + d
    return v


def rate_of(rates, i, relaxing, even, odd):
    return jnp.where(relaxing, rates[i], odd if ODD[i] else even)


def kinds_of(kind):
    relaxing = kind < 1.5
    even = jnp.where((kind > 1.5) & (kind < 3.5), 1.0, 0.0)
    odd = jnp.where(kind > 3.5, 2.0, even)
    return relaxing, even, odd


def collide(f, kappa, kind, rates, inlet):
    m = moments(f)
    relaxing, even, odd = kinds_of(kind)
    rho = m[0]
    inverse = 1.0 / rho
    ux, uy, uz = m[9] * inverse, m[3] * inverse, m[1] * inverse
    vx, vy = kappa * ux, kappa * uy
    vz = jnp.where((kind > 1.5) & (kind < 2.5), inlet, kappa * uz)
    den = jnp.where(relaxing, rho, 1.0)
    jx, jy, jz = den * vx, den * vy, den * vz
    xy, xz, yz = jx * vy, jx * vz, jy * vz
    xx, yy, zz = 3.0 * (jx * vx), 3.0 * (jy * vy), 3.0 * (jz * vz)
    x2, y2, z2 = xx - den, yy - den, zz - den
    e = [None] * 27
    e[0] = den
    e[18], e[6], e[2] = x2, y2, z2
    e[24], e[20], e[8] = -(x2 + yy), -(x2 + zz), -(y2 + zz)
    e[26] = (x2 + yy) + zz
    e[9], e[15], e[11], e[17] = jx, -jx, -jx, jx
    e[3], e[21], e[5], e[23] = jy, -jy, -jy, jy
    e[1], e[19], e[7], e[25] = jz, -jz, -jz, jz
    e[12], e[14] = xy, -xy
    e[10], e[16] = xz, -xz
    e[4], e[22] = yz, -yz
    out = []
    for i in range(27):
        rate = rate_of(rates, i, relaxing, even, odd)
        gap = -m[i] if e[i] is None else e[i] - m[i]
        out.append(SCALE[i] * (m[i] + rate * gap))
    return moments_transposed(out), (ux, uy, uz, inverse, rho)


def collide_back(h, kappa, kind, rates, speed, rho=None):
    y = moments(h)
    relaxing, even, odd = kinds_of(kind)
    ux, uy, uz, inverse = speed
    w, z = [], []
    for i in range(27):
        yi = SCALE[i] * y[i]
        wi = rate_of(rates, i, relaxing, even, odd) * yi
        w.append(wi)
        z.append(yi - wi)
    vx, vy, vz = kappa * ux, kappa * uy, kappa * uz
    w222 = w[26]
    a_x = (w[18] - w[24]) - (w[20] - w222)
    a_y = (w[6] - w[24]) - (w[8] - w222)
    a_z = (w[2] - w[20]) - (w[8] - w222)
    b_x = (w[9] - w[15]) - (w[11] - w[17])
    b_y = (w[3] - w[21]) - (w[5] - w[23])
    b_z = (w[1] - w[19]) - (w[7] - w[25])
    c_xy, c_xz, c_yz = w[12] - w[14], w[10] - w[16], w[4] - w[22]
    base = ((w[0] - w[18]) - (w[6] + w[2])) + ((w[24] + w[20]) + (w[8] - w222))
    p_x, p_y, p_z = 3.0 * (a_x * vx), 3.0 * (a_y * vy), 3.0 * (a_z * vz)
    q_x, q_y, q_z = c_xy * vy + c_xz * vz, c_xy * vx + c_yz * vz, c_xz * vx + c_yz * vy
    r_x, r_y, r_z = b_x + p_x, b_y + p_y, b_z + p_z
    value = base + vx * (r_x + 0.5 * q_x) + vy * (r_y + 0.5 * q_y) + vz * (r_z + 0.5 * q_z)
    g_x, g_y, g_z = r_x + p_x + q_x, r_y + p_y + q_y, r_z + p_z + q_z
    factor = jnp.where(relaxing, kappa, kappa * inverse)
    along = ux * g_x + uy * g_y + uz * g_z
    z[0] = z[0] + (jnp.where(relaxing, value, 0.0) - factor * along)
    z[9] = z[9] + factor * g_x
    z[3] = z[3] + factor * g_y
    z[1] = z[1] + factor * g_z
    return moments_transposed(z), None if rho is None else rho * along


def turned(value, shift):
    return value if shift == 0 else pltpu.roll(value, shift % LANES, axis=1)


def pulled(wide, plane, row, direction):
    tiles = []
    for i, (cx, cy, cz) in enumerate(VEL):
        tile = wide[i, plane - direction * cx, pl.ds(row - direction * cy, NY)]
        tiles.append(turned(tile, direction * cz))
    return tiles


def inlet_speed(start, step):
    time = jnp.full((NY, LANES), (start[0] + step) % PULSE_PERIOD, jnp.int32).astype(jnp.float32)
    return INLET_SPEED * jnp.sin(time * (2.0 * np.pi / PULSE_PERIOD))


def kappa_of(porosity, kind):
    damping = (RAMP_Q + porosity) / (
        RAMP_Q * (1.0 + DRAG_MAX) + (1.0 - DRAG_MAX * RAMP_Q) * porosity
    )
    return jnp.where(kind < 0.5, damping, jnp.where((kind > 2.5) & (kind < 3.5), 1.0, 0.0))


def first_kernel(rates, start, populations, cotangent, porosity, cell_type, post, cell, speed, to_low, to_high):
    inlet = inlet_speed(start, 0)

    def plane_step(plane, carry):
        kind = cell_type[plane].astype(jnp.float32)
        kappa = kappa_of(porosity[plane], kind)
        cell[0, plane] = kappa
        cell[1, plane] = kind
        out, values = collide([populations[i, plane] for i in range(27)], kappa, kind, rates, inlet)
        for i in range(27):
            post[i, plane] = out[i]
        for i in range(5):
            speed[i, plane] = values[i]
        return carry

    lax.fori_loop(0, NX, plane_step, 0)
    sources = {"post": post, "adjoint": cotangent, "cell": cell}

    def read(name, i, plane):
        return sources[name][i, plane]

    pack_x(FIRST, 1, read, to_low)
    pack_x(FIRST, -1, read, to_high)


def second_kernel(post, cotangent, cell, from_low, from_high, to_low, to_high):
    sources = {"post": post, "adjoint": cotangent, "cell": cell}

    def own(name, i, plane, first, rows):
        return sources[name][i, plane, first : first + rows]

    pack_y(FIRST, 1, own, from_low, from_high, to_low)
    pack_y(FIRST, -1, own, from_low, from_high, to_high)


def third_kernel(
    rates, start, post, cotangent, cell, low_x, high_x, low_y, high_y,
    last_post, adjoint, wide_cell, speed_one, speed_two, gain, to_low, to_high,
    wide_post, next_post, wide_adjoint,
):
    for i in range(27):
        wide_post[i, HALO : HALO + NX, NY : 2 * NY] = post[i]
        wide_adjoint[i, HALO : HALO + NX, NY : 2 * NY] = cotangent[i]
    for i in range(2):
        wide_cell[i, HALO : HALO + NX, NY : 2 * NY] = cell[i]
    wide = {"post": wide_post, "adjoint": wide_adjoint, "cell": wide_cell}
    unpack(FIRST, wide, (low_x, high_x), (low_y, high_y))

    def forward(step, source, target, speed, width):
        inlet = inlet_speed(start, step)

        def body(n, carry):
            plane = n // 2 + (HALO - width)
            row = (n % 2) * NY + NY // 2
            here = pl.ds(row, NY)
            f = pulled(source, plane, row, 1)
            out, values = collide(f, wide_cell[0, plane, here], wide_cell[1, plane, here], rates, inlet)
            for i in range(27):
                target[i, plane, here] = out[i]
            for i in range(5):
                speed[i, plane, here] = values[i]
            return carry

        lax.fori_loop(0, 2 * (NX + 2 * width), body, 0)

    forward(1, wide_post, next_post, speed_one, 2)
    forward(2, next_post, wide_post, speed_two, 1)
    inlet = inlet_speed(start, 3)

    def last(n, carry):
        plane = n + HALO
        here = pl.ds(NY, NY)
        kappa, kind = wide_cell[0, plane, here], wide_cell[1, plane, here]
        out, values = collide(pulled(wide_post, plane, NY, 1), kappa, kind, rates, inlet)
        for i in range(27):
            last_post[i, n] = out[i]
        back, grad = collide_back(
            pulled(wide_adjoint, plane, NY, -1), kappa, kind, rates, values[:4], values[4]
        )
        for i in range(27):
            adjoint[i, n] = back[i]
        gain[n] = grad
        return carry

    lax.fori_loop(0, NX, last, 0)

    def read(name, i, plane):
        if name == "speed":
            return speed_two[i, plane + HALO, NY : 2 * NY]
        return {"post": last_post, "adjoint": adjoint}[name][i, plane]

    pack_x(SECOND, 1, read, to_low)
    pack_x(SECOND, -1, read, to_high)


def fourth_kernel(post, adjoint, speed, from_low, from_high, to_low, to_high):
    def own(name, i, plane, first, rows):
        if name == "speed":
            return speed[i, plane + HALO, NY + first : NY + first + rows]
        return {"post": post, "adjoint": adjoint}[name][i, plane, first : first + rows]

    pack_y(SECOND, 1, own, from_low, from_high, to_low)
    pack_y(SECOND, -1, own, from_low, from_high, to_high)


def fifth_kernel(
    rates, post, adjoint, wide_cell, speed_zero, speed_one, speed_two, gain, porosity,
    low_x, high_x, low_y, high_y,
    flow, first_adjoint, sensitivity,
    wide_post, wide_adjoint, next_adjoint, wide_speed, gains,
):
    for i in range(27):
        wide_post[i, HALO : HALO + NX, NY : 2 * NY] = post[i]
        wide_adjoint[i, HALO : HALO + NX, NY : 2 * NY] = adjoint[i]
    wide_speed[...] = speed_two[...]
    wide = {"post": wide_post, "adjoint": wide_adjoint, "speed": wide_speed}
    unpack(SECOND, wide, (low_x, high_x), (low_y, high_y))

    def back(source, target, speed, width, place):
        def body(n, carry):
            plane = n // 2 + (HALO - width)
            row = (n % 2) * NY + NY // 2
            here = pl.ds(row, NY)
            h = pulled(source, plane, row, -1)
            values = [speed[i, plane, here] for i in range(5)]
            out, grad = collide_back(
                h, wide_cell[0, plane, here], wide_cell[1, plane, here], rates, values[:4], values[4]
            )
            for i in range(27):
                target[i, plane, here] = out[i]
            gains[place, plane, here] = grad
            return carry

        lax.fori_loop(0, 2 * (NX + 2 * width), body, 0)

    back(wide_adjoint, next_adjoint, wide_speed, 2, 0)
    back(next_adjoint, wide_adjoint, speed_one, 1, 1)

    def last(n, carry):
        plane = n + HALO
        here = pl.ds(NY, NY)
        kappa, kind = wide_cell[0, plane, here], wide_cell[1, plane, here]
        values = [speed_zero[i, n] for i in range(5)]
        out, grad = collide_back(
            pulled(wide_adjoint, plane, NY, -1), kappa, kind, rates, values[:4], values[4]
        )
        for i in range(27):
            first_adjoint[i, n] = out[i]
        total = ((gain[n] + gains[0, plane, here]) + gains[1, plane, here]) + grad
        ramp = RAMP_Q * (1.0 + DRAG_MAX) + (1.0 - DRAG_MAX * RAMP_Q) * porosity[n]
        slope = (DRAG_MAX * RAMP_Q * (1.0 + RAMP_Q)) / (ramp * ramp)
        sensitivity[n] = jnp.where(kind < 0.5, slope * total, 0.0)
        tiles = pulled(wide_post, plane, NY, 1)
        for i in range(27):
            flow[i, n] = tiles[i]
        return carry

    lax.fori_loop(0, NX, last, 0)


def f32(*shape):
    return jax.ShapeDtypeStruct(shape, jnp.float32)


def call(kernel, scalars, arrays, outs, scratch=()):
    smem = pl.BlockSpec(memory_space=pltpu.SMEM)
    vmem = pl.BlockSpec(memory_space=pltpu.VMEM)
    return pl.pallas_call(
        kernel,
        out_shape=tuple(f32(*s) for s in outs),
        in_specs=[smem] * len(scalars) + [vmem] * len(arrays),
        out_specs=tuple(vmem for _ in outs),
        scratch_shapes=[pltpu.VMEM(s, jnp.float32) for s in scratch],
        compiler_params=pltpu.CompilerParams(vmem_limit_bytes=VMEM_LIMIT),
        name=kernel.__name__,
    )(*scalars, *arrays)


def exchange(axis, to_low, to_high):
    count = lax.axis_size(axis)
    up = [(i, (i + 1) % count) for i in range(count)]
    down = [(b, a) for a, b in up]
    return lax.ppermute(to_high, axis, up), lax.ppermute(to_low, axis, down)


def body(populations, cotangent, porosity, cell_type, rates, start_step):
    block = (27, NX, NY, LANES)
    wide = (27, PLANES, ROWS, LANES)
    tiles = (PLAN_X[FIRST, 1][1], NY, LANES), (PLAN_X[FIRST, -1][1], NY, LANES)
    rows = (PLAN_Y[FIRST, 1][1], LANES), (PLAN_Y[FIRST, -1][1], LANES)
    post, cell, speed_zero, to_low, to_high = call(
        first_kernel, (rates, start_step), (populations, cotangent, porosity, cell_type),
        (block, (2, NX, NY, LANES), (5, NX, NY, LANES)) + tiles,
    )
    x_halos = exchange("gx", to_low, to_high)
    to_low, to_high = call(second_kernel, (), (post, cotangent, cell) + x_halos, rows)
    y_halos = exchange("gy", to_low, to_high)
    wide_values = (5, PLANES, ROWS, LANES)
    tiles = (PLAN_X[SECOND, 1][1], NY, LANES), (PLAN_X[SECOND, -1][1], NY, LANES)
    rows = (PLAN_Y[SECOND, 1][1], LANES), (PLAN_Y[SECOND, -1][1], LANES)
    post, adjoint, wide_cell, speed_one, speed_two, gain, to_low, to_high = call(
        third_kernel, (rates, start_step), (post, cotangent, cell) + x_halos + y_halos,
        (block, block, (2, PLANES, ROWS, LANES), wide_values, wide_values, (NX, NY, LANES)) + tiles,
        (wide, wide, wide),
    )
    x_halos = exchange("gx", to_low, to_high)
    to_low, to_high = call(fourth_kernel, (), (post, adjoint, speed_two) + x_halos, rows)
    y_halos = exchange("gy", to_low, to_high)
    return call(
        fifth_kernel, (rates,),
        (post, adjoint, wide_cell, speed_zero, speed_one, speed_two, gain, porosity) + x_halos + y_halos,
        (block, block, (NX, NY, LANES)),
        (wide, wide, wide, wide_values, (2, PLANES, ROWS, LANES)),
    )


def solution(mesh):
    return jax.shard_map(
        body,
        mesh=mesh,
        in_specs=(
            P(None, "gx", "gy", None),
            P(None, "gx", "gy", None),
            P("gx", "gy", None),
            P("gx", "gy", None),
            P(),
            P(),
        ),
        out_specs=(P(None, "gx", "gy", None), P(None, "gx", "gy", None), P("gx", "gy", None)),
        check_vma=False,
    )
```

time: 253 us -> 103 us (0.41)
  the two profiles are of different devices: /device:TPU:199 before, /device:TPU:56 now
where the time goes in v1:
time: 103 us
  waiting for transfers between devices  47.6 us (46%)
  starting transfers between devices  36.8 us (36%)
  Pallas kernels  13.4 us (13%)
  local copies, waits for them, and re-layouts  3.46 us (3%)
  between operations  1.41 us (1%)
    ppermute x8, waiting for transfers between devices, exchange(): return (lax.ppermute(to_high, axis, up), lax.ppermute(to_low, axis, down))  47.6 us
    ppermute x8, starting transfers between devices, exchange(): return (lax.ppermute(to_high, axis, up), lax.ppermute(to_low, axis, down))  36.8 us
    pallas_call x5, Pallas kernels, call(): pl.pallas_call(kernel, out_shape=tuple((f32(*s) for s in outs)), in_specs...  13.4 us
    unnamed x12, local copies, waits for them, and re-layouts  3.46 us
  transfers between devices with their start and end apart: 8, of which 7 were waited for; matrix products, arithmetic and copies ran while one was open for 0% of the time, Pallas kernels for 0%

profile of v1, /device:TPU:56, one launch (start us, length us, event | category | flops | bytes accessed | tf_op | source)
XLA Modules:
  0.0 102.7 jit_solution(4878635725923581930)
XLA Ops:
  0.6 0.0 copy-start.5
  1.3 0.0 copy-done.5
  1.3 0.0 copy-start
  1.3 1.0 copy-done
  2.3 0.0 copy-start.2
  2.3 1.0 copy-done.2
  3.3 0.0 copy-start.3
  3.3 0.7 copy-done.3
  4.1 0.0 copy-start.4
  4.1 0.7 copy-done.4
  4.8 0.0 copy-start.1
  4.8 0.9 first_kernel.1
  5.7 10.1 %collective-permute-start = (f32[67,8,128]{2,1,0:T(8,128)S(1)}, f32[67,8,128]{2,1,0:T(8,128)S(1)}, u32[]{:S(2)}, u32[]{:S(2)}) collective-permute-start(f32[67,8,128]{2,1,0:T(8,128)S(1)} %get-tuple-element.22), channel_id=1, source_target_pairs={{0,32},{32,64},{64,96},{96,128},{128,160},{160,192},{192,224},{224... | collective-permute-start | bytes 823304 | tf_op jit(solution)/shard_map/ppermute | solution.py:409
  15.9 1.9 %collective-permute-start.1 = (f32[67,8,128]{2,1,0:T(8,128)S(1)}, f32[67,8,128]{2,1,0:T(8,128)S(1)}, u32[]{:S(2)}, u32[]{:S(2)}) collective-permute-start(f32[67,8,128]{2,1,0:T(8,128)S(1)} %get-tuple-element.23), channel_id=1, source_target_pairs={{32,0},{64,32},{96,64},{128,96},{160,128},{192,160},{224,192},{256... | collective-permute-start | bytes 823304 | tf_op jit(solution)/shard_map/ppermute | solution.py:409
  17.8 6.9 %collective-permute-done.from_low.low_x = f32[67,8,128]{2,1,0:T(8,128)S(1)} collective-permute-done((f32[67,8,128]{2,1,0:T(8,128)S(1)}, f32[67,8,128]{2,1,0:T(8,128)S(1)}, u32[]{:S(2)}, u32[]{:S(2)}) %collective-permute-start) | collective-permute-done | bytes 274464 | tf_op jit(solution)/shard_map/ppermute | solution.py:409
  24.7 14.2 %collective-permute-done.1.from_high.high_x = f32[67,8,128]{2,1,0:T(8,128)S(1)} collective-permute-done((f32[67,8,128]{2,1,0:T(8,128)S(1)}, f32[67,8,128]{2,1,0:T(8,128)S(1)}, u32[]{:S(2)}, u32[]{:S(2)}) %collective-permute-start.1) | collective-permute-done | bytes 274464 | tf_op jit(solution)/shard_map/ppermute | solution.py:409
  38.9 0.0 copy-done.1
  38.9 0.2 second_kernel.1
  39.1 1.9 %collective-permute-start.2 = (f32[512,128]{1,0:T(8,128)S(1)}, f32[512,128]{1,0:T(8,128)S(1)}, u32[]{:S(2)}, u32[]{:S(2)}) collective-permute-start(f32[512,128]{1,0:T(8,128)S(1)} %get-tuple-element.24), channel_id=1, source_target_pairs={{0,1},{1,2},{2,3},{3,4},{4,5},{5,6},{6,7},{7,8},{8,9},{9,10},{10,1... | collective-permute-start | bytes 786440 | tf_op jit(solution)/shard_map/ppermute | solution.py:409
  41.1 7.5 %collective-permute-start.3 = (f32[512,128]{1,0:T(8,128)S(1)}, f32[512,128]{1,0:T(8,128)S(1)}, u32[]{:S(2)}, u32[]{:S(2)}) collective-permute-start(f32[512,128]{1,0:T(8,128)S(1)} %get-tuple-element.25), channel_id=1, source_target_pairs={{1,0},{2,1},{3,2},{4,3},{5,4},{6,5},{7,6},{8,7},{9,8},{10,9},{11,1... | collective-permute-start | bytes 786440 | tf_op jit(solution)/shard_map/ppermute | solution.py:409
  48.6 3.4 %collective-permute-done.2.low_y = f32[512,128]{1,0:T(8,128)S(1)} collective-permute-done((f32[512,128]{1,0:T(8,128)S(1)}, f32[512,128]{1,0:T(8,128)S(1)}, u32[]{:S(2)}, u32[]{:S(2)}) %collective-permute-start.2) | collective-permute-done | bytes 262176 | tf_op jit(solution)/shard_map/ppermute | solution.py:409
  52.0 0.5 collective-permute-done.3.high_y
  52.5 5.8 %third_kernel.1 = (f32[27,4,8,128]{3,2,1,0:T(8,128)S(1)}, f32[27,4,8,128]{3,2,1,0:T(8,128)S(1)}, f32[2,10,24,128]{3,2,1,0:T(8,128)S(1)}, f32[5,10,24,128]{3,2,1,...) custom-call(f32[27]{0:T(128)S(1)} %copy-done.5, ...), custom_call_target="tpu_custom_call" | custom-call | tf_op jit(solution)/shard_map/third_kernel/pallas_call | solution.py:394
  58.3 1.9 %collective-permute-start.4 = (f32[71,8,128]{2,1,0:T(8,128)S(1)}, f32[71,8,128]{2,1,0:T(8,128)S(1)}, u32[]{:S(2)}, u32[]{:S(2)}) collective-permute-start(f32[71,8,128]{2,1,0:T(8,128)S(1)} %get-tuple-element.33), channel_id=1, source_target_pairs={{0,32},{32,64},{64,96},{96,128},{128,160},{160,192},{192,224},{224... | collective-permute-start | bytes 872456 | tf_op jit(solution)/shard_map/ppermute | solution.py:409
  60.2 3.9 %collective-permute-start.5 = (f32[71,8,128]{2,1,0:T(8,128)S(1)}, f32[71,8,128]{2,1,0:T(8,128)S(1)}, u32[]{:S(2)}, u32[]{:S(2)}) collective-permute-start(f32[71,8,128]{2,1,0:T(8,128)S(1)} %get-tuple-element.34), channel_id=1, source_target_pairs={{32,0},{64,32},{96,64},{128,96},{160,128},{192,160},{224,192},{256... | collective-permute-start | bytes 872456 | tf_op jit(solution)/shard_map/ppermute | solution.py:409
  64.2 3.1 %collective-permute-done.4.from_low.low_x = f32[71,8,128]{2,1,0:T(8,128)S(1)} collective-permute-done((f32[71,8,128]{2,1,0:T(8,128)S(1)}, f32[71,8,128]{2,1,0:T(8,128)S(1)}, u32[]{:S(2)}, u32[]{:S(2)}) %collective-permute-start.4) | collective-permute-done | bytes 290848 | tf_op jit(solution)/shard_map/ppermute | solution.py:409
  67.2 14.4 %collective-permute-done.5.from_high.high_x = f32[71,8,128]{2,1,0:T(8,128)S(1)} collective-permute-done((f32[71,8,128]{2,1,0:T(8,128)S(1)}, f32[71,8,128]{2,1,0:T(8,128)S(1)}, u32[]{:S(2)}, u32[]{:S(2)}) %collective-permute-start.5) | collective-permute-done | bytes 290848 | tf_op jit(solution)/shard_map/ppermute | solution.py:409
  81.7 0.2 fourth_kernel.1
  81.9 1.9 %collective-permute-start.6 = (f32[544,128]{1,0:T(8,128)S(1)}, f32[544,128]{1,0:T(8,128)S(1)}, u32[]{:S(2)}, u32[]{:S(2)}) collective-permute-start(f32[544,128]{1,0:T(8,128)S(1)} %get-tuple-element.35), channel_id=1, source_target_pairs={{0,1},{1,2},{2,3},{3,4},{4,5},{5,6},{6,7},{7,8},{8,9},{9,10},{10,1... | collective-permute-start | bytes 835592 | tf_op jit(solution)/shard_map/ppermute | solution.py:409
  83.8 7.5 %collective-permute-start.7 = (f32[544,128]{1,0:T(8,128)S(1)}, f32[544,128]{1,0:T(8,128)S(1)}, u32[]{:S(2)}, u32[]{:S(2)}) collective-permute-start(f32[544,128]{1,0:T(8,128)S(1)} %get-tuple-element.36), channel_id=1, source_target_pairs={{1,0},{2,1},{3,2},{4,3},{5,4},{6,5},{7,6},{8,7},{9,8},{10,9},{11,1... | collective-permute-start | bytes 835592 | tf_op jit(solution)/shard_map/ppermute | solution.py:409
  91.3 5.1 %collective-permute-done.6.low_y = f32[544,128]{1,0:T(8,128)S(1)} collective-permute-done((f32[544,128]{1,0:T(8,128)S(1)}, f32[544,128]{1,0:T(8,128)S(1)}, u32[]{:S(2)}, u32[]{:S(2)}) %collective-permute-start.6) | collective-permute-done | bytes 278560 | tf_op jit(solution)/shard_map/ppermute | solution.py:409
  96.5 0.0 collective-permute-done.7.high_y
  96.5 6.2 %fifth_kernel.1 = (f32[27,4,8,128]{3,2,1,0:T(8,128)}, f32[27,4,8,128]{3,2,1,0:T(8,128)}, f32[4,8,128]{2,1,0:T(8,128)}) custom-call(f32[27]{0:T(128)S(1)} %copy-done.5, f32[27,4,8,128]{3,2,1,0:T(8,128)S(1)} %get-tuple-element.26.post, f32[27,4,8,128]{3,2,1,0:T(8,128)S(1)} %get-tuple-element.27.adjoint, f32[2,10,24,128]{3,2,1,0:T(8,128)S(1)} %get-tuple-element.28.wide_cell, ...), custom_call_target="tpu_custom_call" | custom-call | tf_op jit(solution)/shard_map/fifth_kernel/pallas_call | solution.py:394
Async XLA Ops:
  0.6 0.7 copy-start.5
  1.3 1.0 copy-start
  2.3 1.0 copy-start.2
  3.3 0.7 copy-start.3
  4.1 0.7 copy-start.4
  4.8 34.2 %copy-start.1 = (f32[27,4,8,128]{3,2,1,0:T(8,128)S(1)}, f32[27,4,8,128]{3,2,1,0:T(8,128)}, u32[]{:S(2)}) copy-start(f32[27,4,8,128]{3,2,1,0:T(8,128)} %cotangent.5) | copy-start | bytes 1327108
  5.7 19.0 %collective-permute-start = (f32[67,8,128]{2,1,0:T(8,128)S(1)}, f32[67,8,128]{2,1,0:T(8,128)S(1)}, u32[]{:S(2)}, u32[]{:S(2)}) collective-permute-start(f32[67,8,128]{2,1,0:T(8,128)S(1)} %get-tuple-element.22), channel_id=1, source_target_pairs={{0,32},{32,64},{64,96},{96,128},{128,160},{160,192},{192,224},{224... | collective-permute-start | bytes 823304 | tf_op jit(solution)/shard_map/ppermute | solution.py:409
  15.9 23.1 %collective-permute-start.1 = (f32[67,8,128]{2,1,0:T(8,128)S(1)}, f32[67,8,128]{2,1,0:T(8,128)S(1)}, u32[]{:S(2)}, u32[]{:S(2)}) collective-permute-start(f32[67,8,128]{2,1,0:T(8,128)S(1)} %get-tuple-element.23), channel_id=1, source_target_pairs={{32,0},{64,32},{96,64},{128,96},{160,128},{192,160},{224,192},{256... | collective-permute-start | bytes 823304 | tf_op jit(solution)/shard_map/ppermute | solution.py:409
  39.1 12.9 %collective-permute-start.2 = (f32[512,128]{1,0:T(8,128)S(1)}, f32[512,128]{1,0:T(8,128)S(1)}, u32[]{:S(2)}, u32[]{:S(2)}) collective-permute-start(f32[512,128]{1,0:T(8,128)S(1)} %get-tuple-element.24), channel_id=1, source_target_pairs={{0,1},{1,2},{2,3},{3,4},{4,5},{5,6},{6,7},{7,8},{8,9},{9,10},{10,1... | collective-permute-start | bytes 786440 | tf_op jit(solution)/shard_map/ppermute | solution.py:409
  41.1 11.4 %collective-permute-start.3 = (f32[512,128]{1,0:T(8,128)S(1)}, f32[512,128]{1,0:T(8,128)S(1)}, u32[]{:S(2)}, u32[]{:S(2)}) collective-permute-start(f32[512,128]{1,0:T(8,128)S(1)} %get-tuple-element.25), channel_id=1, source_target_pairs={{1,0},{2,1},{3,2},{4,3},{5,4},{6,5},{7,6},{8,7},{9,8},{10,9},{11,1... | collective-permute-start | bytes 786440 | tf_op jit(solution)/shard_map/ppermute | solution.py:409
  58.3 8.9 %collective-permute-start.4 = (f32[71,8,128]{2,1,0:T(8,128)S(1)}, f32[71,8,128]{2,1,0:T(8,128)S(1)}, u32[]{:S(2)}, u32[]{:S(2)}) collective-permute-start(f32[71,8,128]{2,1,0:T(8,128)S(1)} %get-tuple-element.33), channel_id=1, source_target_pairs={{0,32},{32,64},{64,96},{96,128},{128,160},{160,192},{192,224},{224... | collective-permute-start | bytes 872456 | tf_op jit(solution)/shard_map/ppermute | solution.py:409
  60.2 21.4 %collective-permute-start.5 = (f32[71,8,128]{2,1,0:T(8,128)S(1)}, f32[71,8,128]{2,1,0:T(8,128)S(1)}, u32[]{:S(2)}, u32[]{:S(2)}) collective-permute-start(f32[71,8,128]{2,1,0:T(8,128)S(1)} %get-tuple-element.34), channel_id=1, source_target_pairs={{32,0},{64,32},{96,64},{128,96},{160,128},{192,160},{224,192},{256... | collective-permute-start | bytes 872456 | tf_op jit(solution)/shard_map/ppermute | solution.py:409
  81.9 14.6 %collective-permute-start.6 = (f32[544,128]{1,0:T(8,128)S(1)}, f32[544,128]{1,0:T(8,128)S(1)}, u32[]{:S(2)}, u32[]{:S(2)}) collective-permute-start(f32[544,128]{1,0:T(8,128)S(1)} %get-tuple-element.35), channel_id=1, source_target_pairs={{0,1},{1,2},{2,3},{3,4},{4,5},{5,6},{6,7},{7,8},{8,9},{9,10},{10,1... | collective-permute-start | bytes 835592 | tf_op jit(solution)/shard_map/ppermute | solution.py:409
  83.8 12.7 %collective-permute-start.7 = (f32[544,128]{1,0:T(8,128)S(1)}, f32[544,128]{1,0:T(8,128)S(1)}, u32[]{:S(2)}, u32[]{:S(2)}) collective-permute-start(f32[544,128]{1,0:T(8,128)S(1)} %get-tuple-element.36), channel_id=1, source_target_pairs={{1,0},{2,1},{3,2},{4,3},{5,4},{6,5},{7,6},{8,7},{9,8},{10,9},{11,1... | collective-permute-start | bytes 835592 | tf_op jit(solution)/shard_map/ppermute | solution.py:409

commit v2 on v1

--- a/solution.py
+++ b/solution.py
@@ -26,7 +26,7 @@
 
 
 def reach(component, side, width, direction):
-    if direction == 0:
+    if direction in (0, 2):
         return width
     inward = -side * direction
     return max(0, width - (0 if component == inward else 1 if component == 0 else 2))
@@ -34,13 +34,17 @@
 
 def member_reach(field, i, axis, side):
     _, _, width, direction = field
-    return reach(VEL[i][axis] if direction else 0, side, width, direction)
+    return reach(VEL[i][axis] if abs(direction) == 1 else 0, side, width, direction)
+
+
+def first_layer(field):
+    return field[2] if field[3] == 2 else 1
 
 
 def plan_x(fields, side):
     places = {}
     for field in fields:
-        for layer in range(1, field[2] + 1):
+        for layer in range(first_layer(field), field[2] + 1):
             for i in range(field[1]):
                 if member_reach(field, i, 0, side) >= layer:
                     places[field[0], i, layer] = len(places)
@@ -57,14 +61,15 @@
                 if plane >= NX and member_reach(field, i, 0, 1) < plane - NX + 1:
                     continue
                 rows = member_reach(field, i, 1, side)
-                if rows:
-                    entries.append((field[0], i, plane, start, rows))
-                    start += rows
+                skip = first_layer(field) - 1 if -field[2] < plane < NX + field[2] - 1 else 0
+                if rows > skip:
+                    entries.append((field[0], i, plane, start, skip, rows - skip))
+                    start += rows - skip
     return entries, -(-start // 8) * 8
 
 
 FIRST = (("post", 27, 3, 1), ("adjoint", 27, 1, -1), ("cell", 2, 2, 0))
-SECOND = (("adjoint", 27, 3, -1), ("post", 27, 1, 1), ("speed", 4, 2, 0))
+SECOND = (("adjoint", 27, 3, -1), ("post", 27, 1, 1), ("speed", 4, 2, 2))
 PLAN_X = {(f, s): plan_x(f, s) for f in (FIRST, SECOND) for s in (-1, 1)}
 PLAN_Y = {(f, s): plan_y(f, s) for f in (FIRST, SECOND) for s in (-1, 1)}
 
@@ -81,24 +86,64 @@
 
 
 def pack_y(fields, side, own, from_low, from_high, out):
-    for name, i, plane, start, rows in PLAN_Y[fields, side][0]:
-        first = 0 if side > 0 else NY - rows
-        if 0 <= plane < NX:
+    for name, i, plane, start, skip, rows in PLAN_Y[fields, side][0]:
+        first = skip if side > 0 else NY - skip - rows
+        if 0 <= plane < NX or (name == "speed" and -2 < plane < NX + 1):
             out[start : start + rows] = own(name, i, plane, first, rows)
         else:
             ref, place = halo_tile(fields, from_low, from_high, name, i, plane)
             out[start : start + rows] = ref[place, first : first + rows]
 
 
-def unpack(fields, wide, from_x, from_y):
+def by_parity(axis, run, from_even, from_odd):
+    parity = lax.axis_index(axis) % 2
+
+    @pl.when(parity == 0)
+    def _():
+        run(from_odd, from_even)
+
+    @pl.when(parity == 1)
+    def _():
+        run(from_even, from_odd)
+
+
+def unpack_x(fields, wide, *from_x):
     for side, ref in zip((-1, 1), from_x):
         for (name, i, layer), place in PLAN_X[fields, side][0].items():
             plane = NX - 1 + layer if side > 0 else -layer
             wide[name][i, plane + HALO, NY : 2 * NY] = ref[place]
+
+
+def unpack_y(fields, wide, *from_y):
     for side, ref in zip((-1, 1), from_y):
-        for name, i, plane, start, rows in PLAN_Y[fields, side][0]:
-            first = 2 * NY if side > 0 else NY - rows
+        for name, i, plane, start, skip, rows in PLAN_Y[fields, side][0]:
+            first = 2 * NY + skip if side > 0 else NY - skip - rows
             wide[name][i, plane + HALO, first : first + rows] = ref[start : start + rows]
+
+
+def unpack(fields, wide, even_x, odd_x, even_y, odd_y):
+    by_parity("gx", lambda low, high: unpack_x(fields, wide, low, high), even_x, odd_x)
+    partner = even_y.at[1 - lax.axis_index("gy") % 2]
+    by_parity("gy", lambda low, high: unpack_y(fields, wide, low, high), partner, odd_y)
+
+
+def send_x(fields, read, to_even, to_odd):
+    def run(to_low, to_high):
+        pack_x(fields, 1, read, to_low)
+        pack_x(fields, -1, read, to_high)
+
+    by_parity("gx", run, to_even, to_odd)
+
+
+def send_y(fields, own, even_x, odd_x, to_even, to_odd):
+    def with_halo(from_low, from_high):
+        def run(to_low, to_high):
+            pack_y(fields, 1, own, from_low, from_high, to_low)
+            pack_y(fields, -1, own, from_low, from_high, to_high)
+
+        by_parity("gy", run, to_even, to_odd)
+
+    by_parity("gx", with_halo, even_x, odd_x)
 
 
 def moments(f):
@@ -224,15 +269,29 @@
     return jnp.where(kind < 0.5, damping, jnp.where((kind > 2.5) & (kind < 3.5), 1.0, 0.0))
 
 
-def first_kernel(rates, start, populations, cotangent, porosity, cell_type, post, cell, speed, to_low, to_high):
+def first_kernel(
+    rates, start, populations, cotangent, porosity, cell_type, post, cell, speed, to_even, to_odd,
+    f, gamma, kinds, ends, sems,
+):
+    copies = [
+        pltpu.make_async_copy(porosity, gamma, sems.at[0]),
+        pltpu.make_async_copy(cell_type, kinds, sems.at[1]),
+        pltpu.make_async_copy(populations, f, sems.at[2]),
+        pltpu.make_async_copy(cotangent.at[18:27, 0], ends.at[0], sems.at[3]),
+        pltpu.make_async_copy(cotangent.at[0:9, NX - 1], ends.at[1], sems.at[4]),
+    ]
+    for copy in copies:
+        copy.start()
     inlet = inlet_speed(start, 0)
+    for copy in copies:
+        copy.wait()
 
     def plane_step(plane, carry):
-        kind = cell_type[plane].astype(jnp.float32)
-        kappa = kappa_of(porosity[plane], kind)
+        kind = kinds[plane].astype(jnp.float32)
+        kappa = kappa_of(gamma[plane], kind)
         cell[0, plane] = kappa
         cell[1, plane] = kind
-        out, values = collide([populations[i, plane] for i in range(27)], kappa, kind, rates, inlet)
+        out, values = collide([f[i, plane] for i in range(27)], kappa, kind, rates, inlet)
         for i in range(27):
             post[i, plane] = out[i]
         for i in range(5):
@@ -240,28 +299,27 @@
         return carry
 
     lax.fori_loop(0, NX, plane_step, 0)
-    sources = {"post": post, "adjoint": cotangent, "cell": cell}
 
     def read(name, i, plane):
-        return sources[name][i, plane]
-
-    pack_x(FIRST, 1, read, to_low)
-    pack_x(FIRST, -1, read, to_high)
-
-
-def second_kernel(post, cotangent, cell, from_low, from_high, to_low, to_high):
+        if name == "adjoint":
+            return ends[0, i - 18] if plane == 0 else ends[1, i]
+        return {"post": post, "cell": cell}[name][i, plane]
+
+    send_x(FIRST, read, to_even, to_odd)
+
+
+def second_kernel(post, cotangent, cell, even_x, odd_x, to_even, to_odd):
     sources = {"post": post, "adjoint": cotangent, "cell": cell}
 
     def own(name, i, plane, first, rows):
         return sources[name][i, plane, first : first + rows]
 
-    pack_y(FIRST, 1, own, from_low, from_high, to_low)
-    pack_y(FIRST, -1, own, from_low, from_high, to_high)
+    send_y(FIRST, own, even_x, odd_x, to_even, to_odd)
 
 
 def third_kernel(
-    rates, start, post, cotangent, cell, low_x, high_x, low_y, high_y,
-    last_post, adjoint, wide_cell, speed_one, speed_two, gain, to_low, to_high,
+    rates, start, post, cotangent, cell, even_x, odd_x, even_y, odd_y,
+    last_post, adjoint, wide_cell, speed_one, speed_two, gain, to_even, to_odd,
     wide_post, next_post, wide_adjoint,
 ):
     for i in range(27):
@@ -270,7 +328,7 @@
     for i in range(2):
         wide_cell[i, HALO : HALO + NX, NY : 2 * NY] = cell[i]
     wide = {"post": wide_post, "adjoint": wide_adjoint, "cell": wide_cell}
-    unpack(FIRST, wide, (low_x, high_x), (low_y, high_y))
+    unpack(FIRST, wide, even_x, odd_x, even_y, odd_y)
 
     def forward(step, source, target, speed, width):
         inlet = inlet_speed(start, step)
@@ -315,23 +373,21 @@
             return speed_two[i, plane + HALO, NY : 2 * NY]
         return {"post": last_post, "adjoint": adjoint}[name][i, plane]
 
-    pack_x(SECOND, 1, read, to_low)
-    pack_x(SECOND, -1, read, to_high)
-
-
-def fourth_kernel(post, adjoint, speed, from_low, from_high, to_low, to_high):
+    send_x(SECOND, read, to_even, to_odd)
+
+
+def fourth_kernel(post, adjoint, speed, even_x, odd_x, to_even, to_odd):
     def own(name, i, plane, first, rows):
         if name == "speed":
             return speed[i, plane + HALO, NY + first : NY + first + rows]
         return {"post": post, "adjoint": adjoint}[name][i, plane, first : first + rows]
 
-    pack_y(SECOND, 1, own, from_low, from_high, to_low)
-    pack_y(SECOND, -1, own, from_low, from_high, to_high)
+    send_y(SECOND, own, even_x, odd_x, to_even, to_odd)
 
 
 def fifth_kernel(
     rates, post, adjoint, wide_cell, speed_zero, speed_one, speed_two, gain, porosity,
-    low_x, high_x, low_y, high_y,
+    even_x, odd_x, even_y, odd_y,
     flow, first_adjoint, sensitivity,
     wide_post, wide_adjoint, next_adjoint, wide_speed, gains,
 ):
@@ -340,7 +396,7 @@
         wide_adjoint[i, HALO : HALO + NX, NY : 2 * NY] = adjoint[i]
     wide_speed[...] = speed_two[...]
     wide = {"post": wide_post, "adjoint": wide_adjoint, "speed": wide_speed}
-    unpack(SECOND, wide, (low_x, high_x), (low_y, high_y))
+    unpack(SECOND, wide, even_x, odd_x, even_y, odd_y)
 
     def back(source, target, speed, width, place):
         def body(n, carry):
@@ -388,25 +444,39 @@
     return jax.ShapeDtypeStruct(shape, jnp.float32)
 
 
-def call(kernel, scalars, arrays, outs, scratch=()):
+def call(kernel, scalars, arrays, outs, scratch=(), anywhere=False):
     smem = pl.BlockSpec(memory_space=pltpu.SMEM)
     vmem = pl.BlockSpec(memory_space=pltpu.VMEM)
+    held = pl.BlockSpec(memory_space=pl.ANY) if anywhere else vmem
     return pl.pallas_call(
         kernel,
         out_shape=tuple(f32(*s) for s in outs),
-        in_specs=[smem] * len(scalars) + [vmem] * len(arrays),
+        in_specs=[smem] * len(scalars) + [held] * len(arrays),
         out_specs=tuple(vmem for _ in outs),
-        scratch_shapes=[pltpu.VMEM(s, jnp.float32) for s in scratch],
+        scratch_shapes=[pltpu.VMEM(s, jnp.float32) if isinstance(s, tuple) else s for s in scratch],
         compiler_params=pltpu.CompilerParams(vmem_limit_bytes=VMEM_LIMIT),
         name=kernel.__name__,
     )(*scalars, *arrays)
 
 
-def exchange(axis, to_low, to_high):
+def partners(axis, first):
     count = lax.axis_size(axis)
-    up = [(i, (i + 1) % count) for i in range(count)]
-    down = [(b, a) for a, b in up]
-    return lax.ppermute(to_high, axis, up), lax.ppermute(to_low, axis, down)
+    return [[i % count, (i + 1) % count] for i in range(first, count + first, 2)]
+
+
+def swap(value, axis, first):
+    pairs = partners(axis, first)
+    return lax.ppermute(value, axis, [(a, b) for a, b in pairs] + [(b, a) for a, b in pairs])
+
+
+def exchange_x(to_even, to_odd):
+    from_odd = swap(to_odd, "gx", 1)
+    return swap(to_even, "gx", 0), from_odd
+
+
+def exchange_y(to_even, to_odd):
+    from_odd = swap(to_odd, "gy", 1)
+    return lax.all_gather(to_even, "gy", axis_index_groups=partners("gy", 0)), from_odd
 
 
 def body(populations, cotangent, porosity, cell_type, rates, start_step):
@@ -414,24 +484,29 @@
     wide = (27, PLANES, ROWS, LANES)
     tiles = (PLAN_X[FIRST, 1][1], NY, LANES), (PLAN_X[FIRST, -1][1], NY, LANES)
     rows = (PLAN_Y[FIRST, 1][1], LANES), (PLAN_Y[FIRST, -1][1], LANES)
-    post, cell, speed_zero, to_low, to_high = call(
+    post, cell, speed_zero, to_even, to_odd = call(
         first_kernel, (rates, start_step), (populations, cotangent, porosity, cell_type),
         (block, (2, NX, NY, LANES), (5, NX, NY, LANES)) + tiles,
+        (
+            block, (NX, NY, LANES), pltpu.VMEM((NX, NY, LANES), jnp.int32), (2, 9, NY, LANES),
+            pltpu.SemaphoreType.DMA((5,)),
+        ),
+        anywhere=True,
     )
-    x_halos = exchange("gx", to_low, to_high)
-    to_low, to_high = call(second_kernel, (), (post, cotangent, cell) + x_halos, rows)
-    y_halos = exchange("gy", to_low, to_high)
+    x_halos = exchange_x(to_even, to_odd)
+    to_even, to_odd = call(second_kernel, (), (post, cotangent, cell) + x_halos, rows)
+    y_halos = exchange_y(to_even, to_odd)
     wide_values = (5, PLANES, ROWS, LANES)
     tiles = (PLAN_X[SECOND, 1][1], NY, LANES), (PLAN_X[SECOND, -1][1], NY, LANES)
     rows = (PLAN_Y[SECOND, 1][1], LANES), (PLAN_Y[SECOND, -1][1], LANES)
-    post, adjoint, wide_cell, speed_one, speed_two, gain, to_low, to_high = call(
+    post, adjoint, wide_cell, speed_one, speed_two, gain, to_even, to_odd = call(
         third_kernel, (rates, start_step), (post, cotangent, cell) + x_halos + y_halos,
         (block, block, (2, PLANES, ROWS, LANES), wide_values, wide_values, (NX, NY, LANES)) + tiles,
         (wide, wide, wide),
     )
-    x_halos = exchange("gx", to_low, to_high)
-    to_low, to_high = call(fourth_kernel, (), (post, adjoint, speed_two) + x_halos, rows)
-    y_halos = exchange("gy", to_low, to_high)
+    x_halos = exchange_x(to_even, to_odd)
+    to_even, to_odd = call(fourth_kernel, (), (post, adjoint, speed_two) + x_halos, rows)
+    y_halos = exchange_y(to_even, to_odd)
     return call(
         fifth_kernel, (rates,),
         (post, adjoint, wide_cell, speed_zero, speed_one, speed_two, gain, porosity) + x_halos + y_halos,

time: 103 us -> 95.7 us (0.929)
  the two profiles are of different devices: /device:TPU:56 before, /device:TPU:6 now
where the time goes in v2:
time: 95.7 us; the launch traced here: 95.2 us
  starting transfers between devices  36.2 us (38%)
  waiting for transfers between devices  35.9 us (38%)
  Pallas kernels  13.8 us (14%)
  blocking collectives  4.37 us (5%)
  local copies, waits for them, and re-layouts  3.47 us (4%)
  between operations  1.43 us (1%)
    ppermute x6, starting transfers between devices, swap(): lax.ppermute(value, axis, [(a, b) for a, b in pairs] + [(b, a) for a, b i...  36.2 us
    ppermute x6, waiting for transfers between devices, swap(): lax.ppermute(value, axis, [(a, b) for a, b in pairs] + [(b, a) for a, b i...  35.9 us
    pallas_call x5, Pallas kernels, call(): pl.pallas_call(kernel, out_shape=tuple((f32(*s) for s in outs)), in_specs...  13.8 us
    all_gather x2, blocking collectives, exchange_y(): lax.all_gather(to_even, 'gy', axis_index_groups=partners('gy', 0))  4.37 us
    unnamed x14, local copies, waits for them, and re-layouts  3.47 us
  transfers between devices with their start and end apart: 6, of which 4 were waited for; matrix products, arithmetic and copies ran while one was open for 0% of the time, Pallas kernels for 0%

profile of v2, /device:TPU:6, one launch (start us, length us, event | category | flops | bytes accessed | tf_op | source)
XLA Modules:
  0.0 95.2 jit_solution(6610821660323209116)
XLA Ops:
  0.6 0.0 copy-start.6
  1.3 0.0 copy-done.6
  1.3 0.0 copy-start
  1.3 1.0 %copy-done = f32[27,4,8,128]{3,2,1,0:T(8,128)S(1)} copy-done((f32[27,4,8,128]{3,2,1,0:T(8,128)S(1)}, f32[27,4,8,128]{3,2,1,0:T(8,128)}, u32[]{:S(2)}) %copy-start) | copy-done | bytes 442392
  2.3 0.0 copy-start.2
  2.3 1.0 %copy-done.2 = f32[27,4,8,128]{3,2,1,0:T(8,128)S(1)} copy-done((f32[27,4,8,128]{3,2,1,0:T(8,128)S(1)}, f32[27,4,8,128]{3,2,1,0:T(8,128)}, u32[]{:S(2)}) %copy-start.2) | copy-done | bytes 442392
  3.3 0.0 copy-start.3
  3.3 0.7 copy-done.3
  4.1 0.0 copy-start.5
  4.1 0.7 copy-done.5
  4.8 0.0 copy-start.1
  4.8 1.3 %first_kernel.1 = (f32[27,4,8,128]{3,2,1,0:T(8,128)S(1)}, f32[2,4,8,128]{3,2,1,0:T(8,128)S(1)}, f32[5,4,8,128]{3,2,1,0:T(8,128)S(1)}, f32[67,8,128]{2,1,0:T(8,128)S(1)}, f32[67,8,128]{2,1,0:T(8,128)S(1)}) custom-call(f32[27]{0:T(128)S(1)} %copy-done.6, s32[1]{0:T(128)S(6)} %copy.9.start, f32[27,4,8,128]{3,2,1,0:T(8,128)S(1)} %copy-done.2, ...), custom_call_target="tpu_custom_call" | custom-call | tf_op jit(solution)/shard_map/first_kernel/pallas_call | solution.py:451
  6.1 3.5 %collective-permute-start = (f32[67,8,128]{2,1,0:T(8,128)S(1)}, f32[67,8,128]{2,1,0:T(8,128)S(1)}, u32[]{:S(2)}, u32[]{:S(2)}) collective-permute-start(f32[67,8,128]{2,1,0:T(8,128)S(1)} %get-tuple-element.22), channel_id=1, source_target_pairs={{0,32},{64,96},{128,160},{192,224},{256,288},{320,352},{384,416},{... | collective-permute-start | bytes 823304 | tf_op jit(solution)/shard_map/ppermute | solution.py:469
  9.6 13.6 %collective-permute-start.1 = (f32[67,8,128]{2,1,0:T(8,128)S(1)}, f32[67,8,128]{2,1,0:T(8,128)S(1)}, u32[]{:S(2)}, u32[]{:S(2)}) collective-permute-start(f32[67,8,128]{2,1,0:T(8,128)S(1)} %get-tuple-element.23), channel_id=1, source_target_pairs={{32,64},{96,128},{160,192},{224,256},{288,320},{352,384},{416,448}... | collective-permute-start | bytes 823304 | tf_op jit(solution)/shard_map/ppermute | solution.py:469
  23.2 0.0 collective-permute-done.even_x
  23.2 12.1 %collective-permute-done.1.odd_x = f32[67,8,128]{2,1,0:T(8,128)S(1)} collective-permute-done((f32[67,8,128]{2,1,0:T(8,128)S(1)}, f32[67,8,128]{2,1,0:T(8,128)S(1)}, u32[]{:S(2)}, u32[]{:S(2)}) %collective-permute-start.1) | collective-permute-done | bytes 274464 | tf_op jit(solution)/shard_map/ppermute | solution.py:469
  35.3 0.0 copy-done.1
  35.3 0.2 second_kernel.1
  35.5 2.2 %collective-permute-start.2 = (f32[512,128]{1,0:T(8,128)S(1)}, f32[512,128]{1,0:T(8,128)S(1)}, u32[]{:S(2)}, u32[]{:S(2)}) collective-permute-start(f32[512,128]{1,0:T(8,128)S(1)} %get-tuple-element.25), channel_id=1, source_target_pairs={{1,2},{3,4},{5,6},{7,8},{9,10},{11,12},{13,14},{15,16},{17,18},{19... | collective-permute-start | bytes 786440 | tf_op jit(solution)/shard_map/ppermute | solution.py:469
  37.7 2.2 %all-gather = f32[1024,128]{1,0:T(8,128)S(1)} all-gather(f32[512,128]{1,0:T(8,128)S(1)} %get-tuple-element.24), channel_id=2, replica_groups={{0,1},{2,3},{4,5},{6,7},{8,9},{10,11},{12,13},{14,15},{16,17},{18,19},{..., dimensions={0}, use_global_device_ids=true | all-gather | bytes 786432 | tf_op jit(solution)/shard_map/all_gather | solution.py:479
  39.9 8.7 %collective-permute-done.2.odd_y = f32[512,128]{1,0:T(8,128)S(1)} collective-permute-done((f32[512,128]{1,0:T(8,128)S(1)}, f32[512,128]{1,0:T(8,128)S(1)}, u32[]{:S(2)}, u32[]{:S(2)}) %collective-permute-start.2) | collective-permute-done | bytes 262176 | tf_op jit(solution)/shard_map/ppermute | solution.py:469
  48.6 5.8 %third_kernel.1 = (f32[27,4,8,128]{3,2,1,0:T(8,128)S(1)}, f32[27,4,8,128]{3,2,1,0:T(8,128)S(1)}, f32[2,10,24,128]{3,2,1,0:T(8,128)S(1)}, f32[5,10,24,128]{3,2,1,...) custom-call(f32[27]{0:T(128)S(1)} %copy-done.6, ...), custom_call_target="tpu_custom_call" | custom-call | tf_op jit(solution)/shard_map/third_kernel/pallas_call | solution.py:451
  54.5 1.9 %collective-permute-start.3 = (f32[67,8,128]{2,1,0:T(8,128)S(1)}, f32[67,8,128]{2,1,0:T(8,128)S(1)}, u32[]{:S(2)}, u32[]{:S(2)}) collective-permute-start(f32[67,8,128]{2,1,0:T(8,128)S(1)} %get-tuple-element.33), channel_id=1, source_target_pairs={{0,32},{64,96},{128,160},{192,224},{256,288},{320,352},{384,416},{... | collective-permute-start | bytes 823304 | tf_op jit(solution)/shard_map/ppermute | solution.py:469
  56.4 9.7 %collective-permute-start.4 = (f32[67,8,128]{2,1,0:T(8,128)S(1)}, f32[67,8,128]{2,1,0:T(8,128)S(1)}, u32[]{:S(2)}, u32[]{:S(2)}) collective-permute-start(f32[67,8,128]{2,1,0:T(8,128)S(1)} %get-tuple-element.34), channel_id=1, source_target_pairs={{32,64},{96,128},{160,192},{224,256},{288,320},{352,384},{416,448}... | collective-permute-start | bytes 823304 | tf_op jit(solution)/shard_map/ppermute | solution.py:469
  66.1 0.0 collective-permute-done.3.even_x
  66.1 9.5 %collective-permute-done.4.odd_x = f32[67,8,128]{2,1,0:T(8,128)S(1)} collective-permute-done((f32[67,8,128]{2,1,0:T(8,128)S(1)}, f32[67,8,128]{2,1,0:T(8,128)S(1)}, u32[]{:S(2)}, u32[]{:S(2)}) %collective-permute-start.4) | collective-permute-done | bytes 274464 | tf_op jit(solution)/shard_map/ppermute | solution.py:469
  75.6 0.2 fourth_kernel.1
  75.8 5.3 %collective-permute-start.5 = (f32[520,128]{1,0:T(8,128)S(1)}, f32[520,128]{1,0:T(8,128)S(1)}, u32[]{:S(2)}, u32[]{:S(2)}) collective-permute-start(f32[520,128]{1,0:T(8,128)S(1)} %get-tuple-element.36), channel_id=1, source_target_pairs={{1,2},{3,4},{5,6},{7,8},{9,10},{11,12},{13,14},{15,16},{17,18},{19... | collective-permute-start | bytes 798728 | tf_op jit(solution)/shard_map/ppermute | solution.py:469
  81.1 0.0 copy-start.4
  81.1 2.2 %all-gather.1 = f32[1040,128]{1,0:T(8,128)S(1)} all-gather(f32[520,128]{1,0:T(8,128)S(1)} %get-tuple-element.35), channel_id=3, replica_groups={{0,1},{2,3},{4,5},{6,7},{8,9},{10,11},{12,13},{14,15},{16,17},{18,19},{..., dimensions={0}, use_global_device_ids=true | all-gather | bytes 798720 | tf_op jit(solution)/shard_map/all_gather | solution.py:479
  83.3 5.6 %collective-permute-done.5.odd_y = f32[520,128]{1,0:T(8,128)S(1)} collective-permute-done((f32[520,128]{1,0:T(8,128)S(1)}, f32[520,128]{1,0:T(8,128)S(1)}, u32[]{:S(2)}, u32[]{:S(2)}) %collective-permute-start.5) | collective-permute-done | bytes 266272 | tf_op jit(solution)/shard_map/ppermute | solution.py:469
  88.9 0.0 copy-done.4
  88.9 6.2 %fifth_kernel.1 = (f32[27,4,8,128]{3,2,1,0:T(8,128)}, f32[27,4,8,128]{3,2,1,0:T(8,128)}, f32[4,8,128]{2,1,0:T(8,128)}) custom-call(f32[27]{0:T(128)S(1)} %copy-done.6, f32[27,4,8,128]{3,2,1,0:T(8,128)S(1)} %get-tuple-element.26.post, f32[27,4,8,128]{3,2,1,0:T(8,128)S(1)} %get-tuple-element.27.adjoint, f32[2,10,24,128]{3,2,1,0:T(8,128)S(1)} %get-tuple-element.28.wide_cell, ...), custom_call_target="tpu_custom_call" | custom-call | tf_op jit(solution)/shard_map/fifth_kernel/pallas_call | solution.py:451
Async XLA Ops:
  0.6 0.7 copy-start.6
  1.3 1.0 %copy-start = (f32[27,4,8,128]{3,2,1,0:T(8,128)S(1)}, f32[27,4,8,128]{3,2,1,0:T(8,128)}, u32[]{:S(2)}) copy-start(f32[27,4,8,128]{3,2,1,0:T(8,128)} %cotangent.5) | copy-start | bytes 1327108
  2.3 1.0 %copy-start.2 = (f32[27,4,8,128]{3,2,1,0:T(8,128)S(1)}, f32[27,4,8,128]{3,2,1,0:T(8,128)}, u32[]{:S(2)}) copy-start(f32[27,4,8,128]{3,2,1,0:T(8,128)} %populations.1) | copy-start | bytes 1327108
  3.3 0.7 copy-start.3
  4.1 0.7 copy-start.5
  4.8 30.5 %copy-start.1 = (f32[27,4,8,128]{3,2,1,0:T(8,128)S(1)}, f32[27,4,8,128]{3,2,1,0:T(8,128)}, u32[]{:S(2)}) copy-start(f32[27,4,8,128]{3,2,1,0:T(8,128)} %cotangent.5) | copy-start | bytes 1327108
  6.1 17.1 %collective-permute-start = (f32[67,8,128]{2,1,0:T(8,128)S(1)}, f32[67,8,128]{2,1,0:T(8,128)S(1)}, u32[]{:S(2)}, u32[]{:S(2)}) collective-permute-start(f32[67,8,128]{2,1,0:T(8,128)S(1)} %get-tuple-element.22), channel_id=1, source_target_pairs={{0,32},{64,96},{128,160},{192,224},{256,288},{320,352},{384,416},{... | collective-permute-start | bytes 823304 | tf_op jit(solution)/shard_map/ppermute | solution.py:469
  9.6 25.7 %collective-permute-start.1 = (f32[67,8,128]{2,1,0:T(8,128)S(1)}, f32[67,8,128]{2,1,0:T(8,128)S(1)}, u32[]{:S(2)}, u32[]{:S(2)}) collective-permute-start(f32[67,8,128]{2,1,0:T(8,128)S(1)} %get-tuple-element.23), channel_id=1, source_target_pairs={{32,64},{96,128},{160,192},{224,256},{288,320},{352,384},{416,448}... | collective-permute-start | bytes 823304 | tf_op jit(solution)/shard_map/ppermute | solution.py:469
  35.5 13.1 %collective-permute-start.2 = (f32[512,128]{1,0:T(8,128)S(1)}, f32[512,128]{1,0:T(8,128)S(1)}, u32[]{:S(2)}, u32[]{:S(2)}) collective-permute-start(f32[512,128]{1,0:T(8,128)S(1)} %get-tuple-element.25), channel_id=1, source_target_pairs={{1,2},{3,4},{5,6},{7,8},{9,10},{11,12},{13,14},{15,16},{17,18},{19... | collective-permute-start | bytes 786440 | tf_op jit(solution)/shard_map/ppermute | solution.py:469
  54.5 11.6 %collective-permute-start.3 = (f32[67,8,128]{2,1,0:T(8,128)S(1)}, f32[67,8,128]{2,1,0:T(8,128)S(1)}, u32[]{:S(2)}, u32[]{:S(2)}) collective-permute-start(f32[67,8,128]{2,1,0:T(8,128)S(1)} %get-tuple-element.33), channel_id=1, source_target_pairs={{0,32},{64,96},{128,160},{192,224},{256,288},{320,352},{384,416},{... | collective-permute-start | bytes 823304 | tf_op jit(solution)/shard_map/ppermute | solution.py:469
  56.4 19.2 %collective-permute-start.4 = (f32[67,8,128]{2,1,0:T(8,128)S(1)}, f32[67,8,128]{2,1,0:T(8,128)S(1)}, u32[]{:S(2)}, u32[]{:S(2)}) collective-permute-start(f32[67,8,128]{2,1,0:T(8,128)S(1)} %get-tuple-element.34), channel_id=1, source_target_pairs={{32,64},{96,128},{160,192},{224,256},{288,320},{352,384},{416,448}... | collective-permute-start | bytes 823304 | tf_op jit(solution)/shard_map/ppermute | solution.py:469
  75.8 13.1 %collective-permute-start.5 = (f32[520,128]{1,0:T(8,128)S(1)}, f32[520,128]{1,0:T(8,128)S(1)}, u32[]{:S(2)}, u32[]{:S(2)}) collective-permute-start(f32[520,128]{1,0:T(8,128)S(1)} %get-tuple-element.36), channel_id=1, source_target_pairs={{1,2},{3,4},{5,6},{7,8},{9,10},{11,12},{13,14},{15,16},{17,18},{19... | collective-permute-start | bytes 798728 | tf_op jit(solution)/shard_map/ppermute | solution.py:469
  81.1 7.8 %copy-start.4 = (f32[4,8,128]{2,1,0:T(8,128)S(1)}, f32[4,8,128]{2,1,0:T(8,128)}, u32[]{:S(2)}) copy-start(f32[4,8,128]{2,1,0:T(8,128)} %porosity.3) | copy-start | bytes 49156

commit v3 on v2

--- a/solution.py
+++ b/solution.py
@@ -95,7 +95,7 @@
             out[start : start + rows] = ref[place, first : first + rows]
 
 
-def by_parity(axis, run, from_even, from_odd):
+def by_parity(axis, run, from_odd, from_even):
     parity = lax.axis_index(axis) % 2
 
     @pl.when(parity == 0)
@@ -121,29 +121,29 @@
             wide[name][i, plane + HALO, first : first + rows] = ref[start : start + rows]
 
 
-def unpack(fields, wide, even_x, odd_x, even_y, odd_y):
-    by_parity("gx", lambda low, high: unpack_x(fields, wide, low, high), even_x, odd_x)
+def unpack(fields, wide, odd_x, even_x, odd_y, even_y):
+    by_parity("gx", lambda low, high: unpack_x(fields, wide, low, high), odd_x, even_x)
     partner = even_y.at[1 - lax.axis_index("gy") % 2]
-    by_parity("gy", lambda low, high: unpack_y(fields, wide, low, high), partner, odd_y)
-
-
-def send_x(fields, read, to_even, to_odd):
+    by_parity("gy", lambda low, high: unpack_y(fields, wide, low, high), odd_y, partner)
+
+
+def send_x(fields, read, to_odd, to_even):
     def run(to_low, to_high):
         pack_x(fields, 1, read, to_low)
         pack_x(fields, -1, read, to_high)
 
-    by_parity("gx", run, to_even, to_odd)
-
-
-def send_y(fields, own, even_x, odd_x, to_even, to_odd):
+    by_parity("gx", run, to_odd, to_even)
+
+
+def send_y(fields, own, odd_x, even_x, to_odd, to_even):
     def with_halo(from_low, from_high):
         def run(to_low, to_high):
             pack_y(fields, 1, own, from_low, from_high, to_low)
             pack_y(fields, -1, own, from_low, from_high, to_high)
 
-        by_parity("gy", run, to_even, to_odd)
-
-    by_parity("gx", with_halo, even_x, odd_x)
+        by_parity("gy", run, to_odd, to_even)
+
+    by_parity("gx", with_halo, odd_x, even_x)
 
 
 def moments(f):
@@ -270,21 +270,24 @@
 
 
 def first_kernel(
-    rates, start, populations, cotangent, porosity, cell_type, post, cell, speed, to_even, to_odd,
-    f, gamma, kinds, ends, sems,
+    rates_hbm, start_hbm, populations, cotangent, porosity, cell_type,
+    post, held, gamma, cell, speed, to_odd, to_even,
+    rates, start, f, kinds, sems,
 ):
     copies = [
-        pltpu.make_async_copy(porosity, gamma, sems.at[0]),
-        pltpu.make_async_copy(cell_type, kinds, sems.at[1]),
-        pltpu.make_async_copy(populations, f, sems.at[2]),
-        pltpu.make_async_copy(cotangent.at[18:27, 0], ends.at[0], sems.at[3]),
-        pltpu.make_async_copy(cotangent.at[0:9, NX - 1], ends.at[1], sems.at[4]),
+        pltpu.make_async_copy(source, target, sems.at[n])
+        for n, (source, target) in enumerate(
+            (
+                (rates_hbm, rates), (start_hbm, start), (porosity, gamma), (cell_type, kinds),
+                (populations, f), (cotangent, held),
+            )
+        )
     ]
     for copy in copies:
         copy.start()
+    for copy in copies[:5]:
+        copy.wait()
     inlet = inlet_speed(start, 0)
-    for copy in copies:
-        copy.wait()
 
     def plane_step(plane, carry):
         kind = kinds[plane].astype(jnp.float32)
@@ -299,36 +302,43 @@
         return carry
 
     lax.fori_loop(0, NX, plane_step, 0)
+    copies[5].wait()
 
     def read(name, i, plane):
-        if name == "adjoint":
-            return ends[0, i - 18] if plane == 0 else ends[1, i]
-        return {"post": post, "cell": cell}[name][i, plane]
-
-    send_x(FIRST, read, to_even, to_odd)
-
-
-def second_kernel(post, cotangent, cell, even_x, odd_x, to_even, to_odd):
+        return {"post": post, "adjoint": held, "cell": cell}[name][i, plane]
+
+    send_x(FIRST, read, to_odd, to_even)
+
+
+def second_kernel(post, cotangent, cell, odd_x, even_x, to_odd, to_even):
     sources = {"post": post, "adjoint": cotangent, "cell": cell}
 
     def own(name, i, plane, first, rows):
         return sources[name][i, plane, first : first + rows]
 
-    send_y(FIRST, own, even_x, odd_x, to_even, to_odd)
+    send_y(FIRST, own, odd_x, even_x, to_odd, to_even)
 
 
 def third_kernel(
-    rates, start, post, cotangent, cell, even_x, odd_x, even_y, odd_y,
-    last_post, adjoint, wide_cell, speed_one, speed_two, gain, to_even, to_odd,
-    wide_post, next_post, wide_adjoint,
+    rates_hbm, start_hbm, post, cotangent, cell, odd_x, even_x, odd_y, even_y,
+    last_post, adjoint, wide_cell, speed_one, speed_two, gain, to_odd, to_even,
+    wide_post, next_post, wide_adjoint, rates, start, sems,
 ):
+    copies = [
+        pltpu.make_async_copy(rates_hbm, rates, sems.at[0]),
+        pltpu.make_async_copy(start_hbm, start, sems.at[1]),
+    ]
+    for copy in copies:
+        copy.start()
     for i in range(27):
         wide_post[i, HALO : HALO + NX, NY : 2 * NY] = post[i]
         wide_adjoint[i, HALO : HALO + NX, NY : 2 * NY] = cotangent[i]
     for i in range(2):
         wide_cell[i, HALO : HALO + NX, NY : 2 * NY] = cell[i]
     wide = {"post": wide_post, "adjoint": wide_adjoint, "cell": wide_cell}
-    unpack(FIRST, wide, even_x, odd_x, even_y, odd_y)
+    unpack(FIRST, wide, odd_x, even_x, odd_y, even_y)
+    for copy in copies:
+        copy.wait()
 
     def forward(step, source, target, speed, width):
         inlet = inlet_speed(start, step)
@@ -373,30 +383,33 @@
             return speed_two[i, plane + HALO, NY : 2 * NY]
         return {"post": last_post, "adjoint": adjoint}[name][i, plane]
 
-    send_x(SECOND, read, to_even, to_odd)
-
-
-def fourth_kernel(post, adjoint, speed, even_x, odd_x, to_even, to_odd):
+    send_x(SECOND, read, to_odd, to_even)
+
+
+def fourth_kernel(post, adjoint, speed, odd_x, even_x, to_odd, to_even):
     def own(name, i, plane, first, rows):
         if name == "speed":
             return speed[i, plane + HALO, NY + first : NY + first + rows]
         return {"post": post, "adjoint": adjoint}[name][i, plane, first : first + rows]
 
-    send_y(SECOND, own, even_x, odd_x, to_even, to_odd)
+    send_y(SECOND, own, odd_x, even_x, to_odd, to_even)
 
 
 def fifth_kernel(
-    rates, post, adjoint, wide_cell, speed_zero, speed_one, speed_two, gain, porosity,
-    even_x, odd_x, even_y, odd_y,
+    rates_hbm, post, adjoint, wide_cell, speed_zero, speed_one, speed_two, gain, porosity,
+    odd_x, even_x, odd_y, even_y,
     flow, first_adjoint, sensitivity,
-    wide_post, wide_adjoint, next_adjoint, wide_speed, gains,
+    wide_post, wide_adjoint, next_adjoint, wide_speed, gains, rates, sem,
 ):
+    copy = pltpu.make_async_copy(rates_hbm, rates, sem)
+    copy.start()
     for i in range(27):
         wide_post[i, HALO : HALO + NX, NY : 2 * NY] = post[i]
         wide_adjoint[i, HALO : HALO + NX, NY : 2 * NY] = adjoint[i]
     wide_speed[...] = speed_two[...]
     wide = {"post": wide_post, "adjoint": wide_adjoint, "speed": wide_speed}
-    unpack(SECOND, wide, even_x, odd_x, even_y, odd_y)
+    unpack(SECOND, wide, odd_x, even_x, odd_y, even_y)
+    copy.wait()
 
     def back(source, target, speed, width, place):
         def body(n, carry):
@@ -444,19 +457,18 @@
     return jax.ShapeDtypeStruct(shape, jnp.float32)
 
 
-def call(kernel, scalars, arrays, outs, scratch=(), anywhere=False):
-    smem = pl.BlockSpec(memory_space=pltpu.SMEM)
+def call(kernel, far, arrays, outs, scratch=()):
+    hbm = pl.BlockSpec(memory_space=pltpu.HBM)
     vmem = pl.BlockSpec(memory_space=pltpu.VMEM)
-    held = pl.BlockSpec(memory_space=pl.ANY) if anywhere else vmem
     return pl.pallas_call(
         kernel,
         out_shape=tuple(f32(*s) for s in outs),
-        in_specs=[smem] * len(scalars) + [held] * len(arrays),
+        in_specs=[hbm] * len(far) + [vmem] * len(arrays),
         out_specs=tuple(vmem for _ in outs),
         scratch_shapes=[pltpu.VMEM(s, jnp.float32) if isinstance(s, tuple) else s for s in scratch],
         compiler_params=pltpu.CompilerParams(vmem_limit_bytes=VMEM_LIMIT),
         name=kernel.__name__,
-    )(*scalars, *arrays)
+    )(*far, *arrays)
 
 
 def partners(axis, first):
@@ -469,14 +481,13 @@
     return lax.ppermute(value, axis, [(a, b) for a, b in pairs] + [(b, a) for a, b in pairs])
 
 
-def exchange_x(to_even, to_odd):
-    from_odd = swap(to_odd, "gx", 1)
-    return swap(to_even, "gx", 0), from_odd
-
-
-def exchange_y(to_even, to_odd):
+def exchange_x(to_odd, to_even):
+    return swap(to_odd, "gx", 1), swap(to_even, "gx", 0)
+
+
+def exchange_y(to_odd, to_even):
     from_odd = swap(to_odd, "gy", 1)
-    return lax.all_gather(to_even, "gy", axis_index_groups=partners("gy", 0)), from_odd
+    return from_odd, lax.all_gather(to_even, "gy", axis_index_groups=partners("gy", 0))
 
 
 def body(populations, cotangent, porosity, cell_type, rates, start_step):
@@ -484,34 +495,34 @@
     wide = (27, PLANES, ROWS, LANES)
     tiles = (PLAN_X[FIRST, 1][1], NY, LANES), (PLAN_X[FIRST, -1][1], NY, LANES)
     rows = (PLAN_Y[FIRST, 1][1], LANES), (PLAN_Y[FIRST, -1][1], LANES)
-    post, cell, speed_zero, to_even, to_odd = call(
-        first_kernel, (rates, start_step), (populations, cotangent, porosity, cell_type),
-        (block, (2, NX, NY, LANES), (5, NX, NY, LANES)) + tiles,
+    rates_here, start_here = pltpu.SMEM((27,), jnp.float32), pltpu.SMEM((1,), jnp.int32)
+    post, held, gamma, cell, speed_zero, to_odd, to_even = call(
+        first_kernel, (rates, start_step, populations, cotangent, porosity, cell_type), (),
+        (block, block, (NX, NY, LANES), (2, NX, NY, LANES), (5, NX, NY, LANES)) + tiles,
         (
-            block, (NX, NY, LANES), pltpu.VMEM((NX, NY, LANES), jnp.int32), (2, 9, NY, LANES),
-            pltpu.SemaphoreType.DMA((5,)),
+            rates_here, start_here, block, pltpu.VMEM((NX, NY, LANES), jnp.int32),
+            pltpu.SemaphoreType.DMA((6,)),
         ),
-        anywhere=True,
     )
-    x_halos = exchange_x(to_even, to_odd)
-    to_even, to_odd = call(second_kernel, (), (post, cotangent, cell) + x_halos, rows)
-    y_halos = exchange_y(to_even, to_odd)
+    x_halos = exchange_x(to_odd, to_even)
+    to_odd, to_even = call(second_kernel, (), (post, held, cell) + x_halos, rows)
+    y_halos = exchange_y(to_odd, to_even)
     wide_values = (5, PLANES, ROWS, LANES)
     tiles = (PLAN_X[SECOND, 1][1], NY, LANES), (PLAN_X[SECOND, -1][1], NY, LANES)
     rows = (PLAN_Y[SECOND, 1][1], LANES), (PLAN_Y[SECOND, -1][1], LANES)
-    post, adjoint, wide_cell, speed_one, speed_two, gain, to_even, to_odd = call(
-        third_kernel, (rates, start_step), (post, cotangent, cell) + x_halos + y_halos,
+    post, adjoint, wide_cell, speed_one, speed_two, gain, to_odd, to_even = call(
+        third_kernel, (rates, start_step), (post, held, cell) + x_halos + y_halos,
         (block, block, (2, PLANES, ROWS, LANES), wide_values, wide_values, (NX, NY, LANES)) + tiles,
-        (wide, wide, wide),
+        (wide, wide, wide, rates_here, start_here, pltpu.SemaphoreType.DMA((2,))),
     )
-    x_halos = exchange_x(to_even, to_odd)
-    to_even, to_odd = call(fourth_kernel, (), (post, adjoint, speed_two) + x_halos, rows)
-    y_halos = exchange_y(to_even, to_odd)
+    x_halos = exchange_x(to_odd, to_even)
+    to_odd, to_even = call(fourth_kernel, (), (post, adjoint, speed_two) + x_halos, rows)
+    y_halos = exchange_y(to_odd, to_even)
     return call(
         fifth_kernel, (rates,),
-        (post, adjoint, wide_cell, speed_zero, speed_one, speed_two, gain, porosity) + x_halos + y_halos,
+        (post, adjoint, wide_cell, speed_zero, speed_one, speed_two, gain, gamma) + x_halos + y_halos,
         (block, block, (NX, NY, LANES)),
-        (wide, wide, wide, wide_values, (2, PLANES, ROWS, LANES)),
+        (wide, wide, wide, wide_values, (2, PLANES, ROWS, LANES), rates_here, pltpu.SemaphoreType.DMA(())),
     )
 
 

time: 95.7 us -> 89.9 us (0.939)
  waiting for transfers between devices: 35.9 us -> 31.4 us
    ppermute x6, waiting for transfers between devices: 35.9 us -> 31.4 us  [swap(): lax.ppermute(value, axis, [(a, b) for a, b in pairs] + [(b, a) for a, b i...]
    unnamed x14 -> x10, local copies, waits for them, and re-layouts: 3.47 us -> 3.46 us
where the time goes in v3:
time: 89.9 us; the launch traced here: 89.4 us
  starting transfers between devices  35.8 us (40%)
  waiting for transfers between devices  31.4 us (35%)
  Pallas kernels  12.9 us (14%)
  blocking collectives  4.37 us (5%)
  local copies, waits for them, and re-layouts  3.46 us (4%)
  between operations  1.4 us (2%)
    ppermute x6, starting transfers between devices, swap(): lax.ppermute(value, axis, [(a, b) for a, b in pairs] + [(b, a) for a, b i...  35.8 us
    ppermute x6, waiting for transfers between devices, swap(): lax.ppermute(value, axis, [(a, b) for a, b in pairs] + [(b, a) for a, b i...  31.4 us
    pallas_call x5, Pallas kernels, call(): pl.pallas_call(kernel, out_shape=tuple((f32(*s) for s in outs)), in_specs...  12.9 us
    all_gather x2, blocking collectives, exchange_y(): lax.all_gather(to_even, 'gy', axis_index_groups=partners('gy', 0))  4.37 us
    unnamed x10, local copies, waits for them, and re-layouts  3.46 us
  transfers between devices with their start and end apart: 6, of which 4 were waited for; matrix products, arithmetic and copies ran while one was open for 0% of the time, Pallas kernels for 0%

profile of v3, /device:TPU:6, one launch (start us, length us, event | category | flops | bytes accessed | tf_op | source)
XLA Modules:
  0.0 89.4 jit_solution(16369928439113797224)
XLA Ops:
  0.6 0.0 copy-start.4
  1.3 0.0 copy-done.4
  1.3 0.0 copy-start
  1.3 1.0 %copy-done = f32[27,4,8,128]{3,2,1,0:T(8,128)S(1)} copy-done((f32[27,4,8,128]{3,2,1,0:T(8,128)S(1)}, f32[27,4,8,128]{3,2,1,0:T(8,128)}, u32[]{:S(2)}) %copy-start) | copy-done | bytes 442392
  2.3 0.0 copy-start.1
  2.3 1.0 %copy-done.1 = f32[27,4,8,128]{3,2,1,0:T(8,128)S(1)} copy-done((f32[27,4,8,128]{3,2,1,0:T(8,128)S(1)}, f32[27,4,8,128]{3,2,1,0:T(8,128)}, u32[]{:S(2)}) %copy-start.1) | copy-done | bytes 442392
  3.3 0.0 copy-start.2
  3.3 0.7 copy-done.2
  4.1 0.0 copy-start.3
  4.1 0.7 copy-done.3
  4.8 1.0 %first_kernel.1 = (f32[27,4,8,128]{3,2,1,0:T(8,128)S(1)}, f32[27,4,8,128]{3,2,1,0:T(8,128)S(1)}, f32[4,8,128]{2,1,0:T(8,128)S(1)}, f32[2,4,8,128]{3,2,1,0:T(8,12...) custom-call(f32[27]{0:T(128)S(1)} %copy-done.4, s32[1]{0:T(128)S(6)} %copy.9.start_hbm, ...), custom_call_target="tpu_custom_call" | custom-call | tf_op jit(solution)/shard_map/first_kernel/pallas_call | solution.py:463
  5.8 13.8 %collective-permute-start = (f32[67,8,128]{2,1,0:T(8,128)S(1)}, f32[67,8,128]{2,1,0:T(8,128)S(1)}, u32[]{:S(2)}, u32[]{:S(2)}) collective-permute-start(f32[67,8,128]{2,1,0:T(8,128)S(1)} %get-tuple-element.25), channel_id=1, source_target_pairs={{32,64},{96,128},{160,192},{224,256},{288,320},{352,384},{416,448}... | collective-permute-start | bytes 823304 | tf_op jit(solution)/shard_map/ppermute | solution.py:481
  19.6 1.9 %collective-permute-start.1 = (f32[67,8,128]{2,1,0:T(8,128)S(1)}, f32[67,8,128]{2,1,0:T(8,128)S(1)}, u32[]{:S(2)}, u32[]{:S(2)}) collective-permute-start(f32[67,8,128]{2,1,0:T(8,128)S(1)} %get-tuple-element.26), channel_id=1, source_target_pairs={{0,32},{64,96},{128,160},{192,224},{256,288},{320,352},{384,416},{... | collective-permute-start | bytes 823304 | tf_op jit(solution)/shard_map/ppermute | solution.py:481
  21.6 10.4 %collective-permute-done.odd_x = f32[67,8,128]{2,1,0:T(8,128)S(1)} collective-permute-done((f32[67,8,128]{2,1,0:T(8,128)S(1)}, f32[67,8,128]{2,1,0:T(8,128)S(1)}, u32[]{:S(2)}, u32[]{:S(2)}) %collective-permute-start) | collective-permute-done | bytes 274464 | tf_op jit(solution)/shard_map/ppermute | solution.py:481
  32.0 0.0 collective-permute-done.1.even_x
  32.0 0.2 second_kernel.1
  32.2 3.2 %collective-permute-start.2 = (f32[512,128]{1,0:T(8,128)S(1)}, f32[512,128]{1,0:T(8,128)S(1)}, u32[]{:S(2)}, u32[]{:S(2)}) collective-permute-start(f32[512,128]{1,0:T(8,128)S(1)} %get-tuple-element.27), channel_id=1, source_target_pairs={{1,2},{3,4},{5,6},{7,8},{9,10},{11,12},{13,14},{15,16},{17,18},{19... | collective-permute-start | bytes 786440 | tf_op jit(solution)/shard_map/ppermute | solution.py:481
  35.4 2.2 %all-gather = f32[1024,128]{1,0:T(8,128)S(1)} all-gather(f32[512,128]{1,0:T(8,128)S(1)} %get-tuple-element.28), channel_id=2, replica_groups={{0,1},{2,3},{4,5},{6,7},{8,9},{10,11},{12,13},{14,15},{16,17},{18,19},{..., dimensions={0}, use_global_device_ids=true | all-gather | bytes 786432 | tf_op jit(solution)/shard_map/all_gather | solution.py:490
  37.6 7.7 %collective-permute-done.2.odd_y = f32[512,128]{1,0:T(8,128)S(1)} collective-permute-done((f32[512,128]{1,0:T(8,128)S(1)}, f32[512,128]{1,0:T(8,128)S(1)}, u32[]{:S(2)}, u32[]{:S(2)}) %collective-permute-start.2) | collective-permute-done | bytes 262176 | tf_op jit(solution)/shard_map/ppermute | solution.py:481
  45.3 5.6 %third_kernel.1 = (f32[27,4,8,128]{3,2,1,0:T(8,128)S(1)}, f32[27,4,8,128]{3,2,1,0:T(8,128)S(1)}, f32[2,10,24,128]{3,2,1,0:T(8,128)S(1)}, f32[5,10,24,128]{3,2,1,...) custom-call(f32[27]{0:T(128)S(1)} %copy-done.4, ...), custom_call_target="tpu_custom_call" | custom-call | tf_op jit(solution)/shard_map/third_kernel/pallas_call | solution.py:463
  50.9 9.8 %collective-permute-start.3 = (f32[67,8,128]{2,1,0:T(8,128)S(1)}, f32[67,8,128]{2,1,0:T(8,128)S(1)}, u32[]{:S(2)}, u32[]{:S(2)}) collective-permute-start(f32[67,8,128]{2,1,0:T(8,128)S(1)} %get-tuple-element.37), channel_id=1, source_target_pairs={{32,64},{96,128},{160,192},{224,256},{288,320},{352,384},{416,448}... | collective-permute-start | bytes 823304 | tf_op jit(solution)/shard_map/ppermute | solution.py:481
  60.6 1.9 %collective-permute-start.4 = (f32[67,8,128]{2,1,0:T(8,128)S(1)}, f32[67,8,128]{2,1,0:T(8,128)S(1)}, u32[]{:S(2)}, u32[]{:S(2)}) collective-permute-start(f32[67,8,128]{2,1,0:T(8,128)S(1)} %get-tuple-element.38), channel_id=1, source_target_pairs={{0,32},{64,96},{128,160},{192,224},{256,288},{320,352},{384,416},{... | collective-permute-start | bytes 823304 | tf_op jit(solution)/shard_map/ppermute | solution.py:481
  62.6 7.5 %collective-permute-done.3.odd_x = f32[67,8,128]{2,1,0:T(8,128)S(1)} collective-permute-done((f32[67,8,128]{2,1,0:T(8,128)S(1)}, f32[67,8,128]{2,1,0:T(8,128)S(1)}, u32[]{:S(2)}, u32[]{:S(2)}) %collective-permute-start.3) | collective-permute-done | bytes 274464 | tf_op jit(solution)/shard_map/ppermute | solution.py:481
  70.1 0.0 collective-permute-done.4.even_x
  70.1 0.2 fourth_kernel.1
  70.3 5.2 %collective-permute-start.5 = (f32[520,128]{1,0:T(8,128)S(1)}, f32[520,128]{1,0:T(8,128)S(1)}, u32[]{:S(2)}, u32[]{:S(2)}) collective-permute-start(f32[520,128]{1,0:T(8,128)S(1)} %get-tuple-element.39), channel_id=1, source_target_pairs={{1,2},{3,4},{5,6},{7,8},{9,10},{11,12},{13,14},{15,16},{17,18},{19... | collective-permute-start | bytes 798728 | tf_op jit(solution)/shard_map/ppermute | solution.py:481
  75.5 2.2 %all-gather.1 = f32[1040,128]{1,0:T(8,128)S(1)} all-gather(f32[520,128]{1,0:T(8,128)S(1)} %get-tuple-element.40), channel_id=3, replica_groups={{0,1},{2,3},{4,5},{6,7},{8,9},{10,11},{12,13},{14,15},{16,17},{18,19},{..., dimensions={0}, use_global_device_ids=true | all-gather | bytes 798720 | tf_op jit(solution)/shard_map/all_gather | solution.py:490
  77.7 5.8 %collective-permute-done.5.odd_y = f32[520,128]{1,0:T(8,128)S(1)} collective-permute-done((f32[520,128]{1,0:T(8,128)S(1)}, f32[520,128]{1,0:T(8,128)S(1)}, u32[]{:S(2)}, u32[]{:S(2)}) %collective-permute-start.5) | collective-permute-done | bytes 266272 | tf_op jit(solution)/shard_map/ppermute | solution.py:481
  83.5 5.9 %fifth_kernel.1 = (f32[27,4,8,128]{3,2,1,0:T(8,128)}, f32[27,4,8,128]{3,2,1,0:T(8,128)}, f32[4,8,128]{2,1,0:T(8,128)}) custom-call(f32[27]{0:T(128)S(1)} %copy-done.4, f32[27,4,8,128]{3,2,1,0:T(8,128)S(1)} %get-tuple-element.29.post, f32[27,4,8,128]{3,2,1,0:T(8,128)S(1)} %get-tuple-element.30.adjoint, f32[2,10,24,128]{3,2,1,0:T(8,128)S(1)} %get-tuple-element.31.wide_cell, ...), custom_call_target="tpu_custom_call" | custom-call | tf_op jit(solution)/shard_map/fifth_kernel/pallas_call | solution.py:463
Async XLA Ops:
  0.6 0.7 copy-start.4
  1.3 1.0 %copy-start = (f32[27,4,8,128]{3,2,1,0:T(8,128)S(1)}, f32[27,4,8,128]{3,2,1,0:T(8,128)}, u32[]{:S(2)}) copy-start(f32[27,4,8,128]{3,2,1,0:T(8,128)} %populations.1) | copy-start | bytes 1327108
  2.3 1.0 %copy-start.1 = (f32[27,4,8,128]{3,2,1,0:T(8,128)S(1)}, f32[27,4,8,128]{3,2,1,0:T(8,128)}, u32[]{:S(2)}) copy-start(f32[27,4,8,128]{3,2,1,0:T(8,128)} %cotangent.1) | copy-start | bytes 1327108
  3.3 0.7 copy-start.2
  4.1 0.7 copy-start.3
  5.8 26.2 %collective-permute-start = (f32[67,8,128]{2,1,0:T(8,128)S(1)}, f32[67,8,128]{2,1,0:T(8,128)S(1)}, u32[]{:S(2)}, u32[]{:S(2)}) collective-permute-start(f32[67,8,128]{2,1,0:T(8,128)S(1)} %get-tuple-element.25), channel_id=1, source_target_pairs={{32,64},{96,128},{160,192},{224,256},{288,320},{352,384},{416,448}... | collective-permute-start | bytes 823304 | tf_op jit(solution)/shard_map/ppermute | solution.py:481
  19.6 12.4 %collective-permute-start.1 = (f32[67,8,128]{2,1,0:T(8,128)S(1)}, f32[67,8,128]{2,1,0:T(8,128)S(1)}, u32[]{:S(2)}, u32[]{:S(2)}) collective-permute-start(f32[67,8,128]{2,1,0:T(8,128)S(1)} %get-tuple-element.26), channel_id=1, source_target_pairs={{0,32},{64,96},{128,160},{192,224},{256,288},{320,352},{384,416},{... | collective-permute-start | bytes 823304 | tf_op jit(solution)/shard_map/ppermute | solution.py:481
  32.2 13.0 %collective-permute-start.2 = (f32[512,128]{1,0:T(8,128)S(1)}, f32[512,128]{1,0:T(8,128)S(1)}, u32[]{:S(2)}, u32[]{:S(2)}) collective-permute-start(f32[512,128]{1,0:T(8,128)S(1)} %get-tuple-element.27), channel_id=1, source_target_pairs={{1,2},{3,4},{5,6},{7,8},{9,10},{11,12},{13,14},{15,16},{17,18},{19... | collective-permute-start | bytes 786440 | tf_op jit(solution)/shard_map/ppermute | solution.py:481
  50.9 19.2 %collective-permute-start.3 = (f32[67,8,128]{2,1,0:T(8,128)S(1)}, f32[67,8,128]{2,1,0:T(8,128)S(1)}, u32[]{:S(2)}, u32[]{:S(2)}) collective-permute-start(f32[67,8,128]{2,1,0:T(8,128)S(1)} %get-tuple-element.37), channel_id=1, source_target_pairs={{32,64},{96,128},{160,192},{224,256},{288,320},{352,384},{416,448}... | collective-permute-start | bytes 823304 | tf_op jit(solution)/shard_map/ppermute | solution.py:481
  60.6 9.4 %collective-permute-start.4 = (f32[67,8,128]{2,1,0:T(8,128)S(1)}, f32[67,8,128]{2,1,0:T(8,128)S(1)}, u32[]{:S(2)}, u32[]{:S(2)}) collective-permute-start(f32[67,8,128]{2,1,0:T(8,128)S(1)} %get-tuple-element.38), channel_id=1, source_target_pairs={{0,32},{64,96},{128,160},{192,224},{256,288},{320,352},{384,416},{... | collective-permute-start | bytes 823304 | tf_op jit(solution)/shard_map/ppermute | solution.py:481
  70.3 13.3 %collective-permute-start.5 = (f32[520,128]{1,0:T(8,128)S(1)}, f32[520,128]{1,0:T(8,128)S(1)}, u32[]{:S(2)}, u32[]{:S(2)}) collective-permute-start(f32[520,128]{1,0:T(8,128)S(1)} %get-tuple-element.39), channel_id=1, source_target_pairs={{1,2},{3,4},{5,6},{7,8},{9,10},{11,12},{13,14},{15,16},{17,18},{19... | collective-permute-start | bytes 798728 | tf_op jit(solution)/shard_map/ppermute | solution.py:481

commit v4 on v3

--- a/solution.py
+++ b/solution.py
@@ -16,6 +16,7 @@
 PLANES = NX + 2 * HALO
 ROWS = 3 * NY
 VMEM_LIMIT = 48 * 1024 * 1024
+FIRST_LIMIT = 64 * 1024 * 1024
 
 SCALE = [
     float(s)
@@ -271,15 +272,15 @@
 
 def first_kernel(
     rates_hbm, start_hbm, populations, cotangent, porosity, cell_type,
-    post, held, gamma, cell, speed, to_odd, to_even,
-    rates, start, f, kinds, sems,
+    post, cell, speed, to_odd, to_even,
+    rates, start, f, gamma, kinds, ends, sems,
 ):
     copies = [
         pltpu.make_async_copy(source, target, sems.at[n])
         for n, (source, target) in enumerate(
             (
                 (rates_hbm, rates), (start_hbm, start), (porosity, gamma), (cell_type, kinds),
-                (populations, f), (cotangent, held),
+                (populations, f), (cotangent.at[18:27, 0], ends.at[0]), (cotangent.at[0:9, NX - 1], ends.at[1]),
             )
         )
     ]
@@ -302,12 +303,23 @@
         return carry
 
     lax.fori_loop(0, NX, plane_step, 0)
-    copies[5].wait()
+    for copy in copies[5:]:
+        copy.wait()
 
     def read(name, i, plane):
-        return {"post": post, "adjoint": held, "cell": cell}[name][i, plane]
+        if name == "adjoint":
+            return ends[0, i - 18] if plane == 0 else ends[1, i]
+        return {"post": post, "cell": cell}[name][i, plane]
 
     send_x(FIRST, read, to_odd, to_even)
+
+
+def holding_kernel(*refs):
+    half = len(refs) // 2
+    for n in range(half):
+        pltpu.make_async_copy(refs[n], refs[half + n], refs[-1].at[n]).start()
+    for n in range(half):
+        pltpu.make_async_copy(refs[n], refs[half + n], refs[-1].at[n]).wait()
 
 
 def second_kernel(post, cotangent, cell, odd_x, even_x, to_odd, to_even):
@@ -457,7 +469,7 @@
     return jax.ShapeDtypeStruct(shape, jnp.float32)
 
 
-def call(kernel, far, arrays, outs, scratch=()):
+def call(kernel, far, arrays, outs, scratch=(), limit=VMEM_LIMIT):
     hbm = pl.BlockSpec(memory_space=pltpu.HBM)
     vmem = pl.BlockSpec(memory_space=pltpu.VMEM)
     return pl.pallas_call(
@@ -466,7 +478,7 @@
         in_specs=[hbm] * len(far) + [vmem] * len(arrays),
         out_specs=tuple(vmem for _ in outs),
         scratch_shapes=[pltpu.VMEM(s, jnp.float32) if isinstance(s, tuple) else s for s in scratch],
-        compiler_params=pltpu.CompilerParams(vmem_limit_bytes=VMEM_LIMIT),
+        compiler_params=pltpu.CompilerParams(vmem_limit_bytes=limit),
         name=kernel.__name__,
     )(*far, *arrays)
 
@@ -496,13 +508,18 @@
     tiles = (PLAN_X[FIRST, 1][1], NY, LANES), (PLAN_X[FIRST, -1][1], NY, LANES)
     rows = (PLAN_Y[FIRST, 1][1], LANES), (PLAN_Y[FIRST, -1][1], LANES)
     rates_here, start_here = pltpu.SMEM((27,), jnp.float32), pltpu.SMEM((1,), jnp.int32)
-    post, held, gamma, cell, speed_zero, to_odd, to_even = call(
+    post, cell, speed_zero, to_odd, to_even = call(
         first_kernel, (rates, start_step, populations, cotangent, porosity, cell_type), (),
-        (block, block, (NX, NY, LANES), (2, NX, NY, LANES), (5, NX, NY, LANES)) + tiles,
+        (block, (2, NX, NY, LANES), (5, NX, NY, LANES)) + tiles,
         (
-            rates_here, start_here, block, pltpu.VMEM((NX, NY, LANES), jnp.int32),
-            pltpu.SemaphoreType.DMA((6,)),
+            rates_here, start_here, block, (NX, NY, LANES), pltpu.VMEM((NX, NY, LANES), jnp.int32),
+            (2, 9, NY, LANES), pltpu.SemaphoreType.DMA((7,)),
         ),
+        FIRST_LIMIT,
+    )
+    kept = (post, cotangent, cell)
+    post, held, cell = call(
+        holding_kernel, kept, (), tuple(a.shape for a in kept), (pltpu.SemaphoreType.DMA((len(kept),)),)
     )
     x_halos = exchange_x(to_odd, to_even)
     to_odd, to_even = call(second_kernel, (), (post, held, cell) + x_halos, rows)
@@ -520,7 +537,7 @@
     y_halos = exchange_y(to_odd, to_even)
     return call(
         fifth_kernel, (rates,),
-        (post, adjoint, wide_cell, speed_zero, speed_one, speed_two, gain, gamma) + x_halos + y_halos,
+        (post, adjoint, wide_cell, speed_zero, speed_one, speed_two, gain, porosity) + x_halos + y_halos,
         (block, block, (NX, NY, LANES)),
         (wide, wide, wide, wide_values, (2, PLANES, ROWS, LANES), rates_here, pltpu.SemaphoreType.DMA(())),
     )

time: 89.9 us -> 88.1 us (0.980)
  waiting for transfers between devices: 31.4 us -> 28.1 us
  Pallas kernels: 12.9 us -> 15 us
    ppermute x6, waiting for transfers between devices: 31.4 us -> 28.1 us  [swap(): lax.ppermute(value, axis, [(a, b) for a, b in pairs] + [(b, a) for a, b i...]
    pallas_call x5 -> x6, Pallas kernels: 12.9 us -> 15 us  [call(): pl.pallas_call(kernel, out_shape=tuple((f32(*s) for s in outs)), in_specs...]
    unnamed x10 -> x12, local copies, waits for them, and re-layouts: 3.46 us -> 2.79 us
  transfers between devices with their start and end apart: 6 -> 6, of which waited for: 4 -> 4; matrix products, arithmetic and copies ran while one was open for 0% -> 0% of each run, Pallas kernels for 0% -> 1%
where the time goes in v4:
time: 88.1 us; the launch traced here: 87.6 us
  starting transfers between devices  35.9 us (41%)
  waiting for transfers between devices  28.1 us (32%)
  Pallas kernels  15 us (17%)
  blocking collectives  4.5 us (5%)
  local copies, waits for them, and re-layouts  2.79 us (3%)
  between operations  1.4 us (2%)
    ppermute x6, starting transfers between devices, swap(): lax.ppermute(value, axis, [(a, b) for a, b in pairs] + [(b, a) for a, b i...  35.9 us
    ppermute x6, waiting for transfers between devices, swap(): lax.ppermute(value, axis, [(a, b) for a, b in pairs] + [(b, a) for a, b i...  28.1 us
    pallas_call x6, Pallas kernels, call(): pl.pallas_call(kernel, out_shape=tuple((f32(*s) for s in outs)), in_specs...  15 us
    all_gather x2, blocking collectives, exchange_y(): lax.all_gather(to_even, 'gy', axis_index_groups=partners('gy', 0))  4.5 us
    unnamed x12, local copies, waits for them, and re-layouts  2.79 us
  transfers between devices with their start and end apart: 6, of which 4 were waited for; matrix products, arithmetic and copies ran while one was open for 0% of the time, Pallas kernels for 1%

profile of v4, /device:TPU:6, one launch (start us, length us, event | category | flops | bytes accessed | tf_op | source)
XLA Modules:
  0.0 87.6 jit_solution(7770886857835922440)
XLA Ops:
  1.3 2.5 %first_kernel.1 = (f32[27,4,8,128]{3,2,1,0:T(8,128)}, f32[2,4,8,128]{3,2,1,0:T(8,128)}, f32[5,4,8,128]{3,2,1,0:T(8,128)}, f32[67,8,128]{2,1,0:T(8,128)}, f32[67,8,128]{2,1,0:T(8,128)}) custom-call(f32[27]{0:T(128)} %rates_hbm.5, s32[1]{0:T(128)S(6)} %copy.9.start_hbm, f32[27,4,8,128]{3,2,1,0:T(8,128)} %populations.1, f32[27,4,8,128]{3,2,1,0:T(8,128)} %refs_1_.1, ...), custom_call_target="tpu_custom_call" | custom-call | tf_op jit(solution)/shard_map/first_kernel/pallas_call | solution.py:475
  3.8 13.8 %collective-permute-start = (f32[67,8,128]{2,1,0:T(8,128)}, f32[67,8,128]{2,1,0:T(8,128)S(1)}, u32[]{:S(2)}, u32[]{:S(2)}) collective-permute-start(f32[67,8,128]{2,1,0:T(8,128)} %get-tuple-element.28), channel_id=1, source_target_pairs={{32,64},{96,128},{160,192},{224,256},{288,320},{352,384},{416,448}... | collective-permute-start | bytes 823304 | tf_op jit(solution)/shard_map/ppermute | solution.py:493
  17.6 1.9 %collective-permute-start.1 = (f32[67,8,128]{2,1,0:T(8,128)}, f32[67,8,128]{2,1,0:T(8,128)S(1)}, u32[]{:S(2)}, u32[]{:S(2)}) collective-permute-start(f32[67,8,128]{2,1,0:T(8,128)} %get-tuple-element.29), channel_id=1, source_target_pairs={{0,32},{64,96},{128,160},{192,224},{256,288},{320,352},{384,416},{... | collective-permute-start | bytes 823304 | tf_op jit(solution)/shard_map/ppermute | solution.py:493
  19.5 0.0 copy-start
  19.6 1.0 %copy-done = f32[27,4,8,128]{3,2,1,0:T(8,128)S(1)} copy-done((f32[27,4,8,128]{3,2,1,0:T(8,128)S(1)}, f32[27,4,8,128]{3,2,1,0:T(8,128)}, u32[]{:S(2)}) %copy-start) | copy-done | bytes 442392
  20.6 0.0 copy-start.1
  20.6 1.0 %copy-done.1 = f32[27,4,8,128]{3,2,1,0:T(8,128)S(1)} copy-done((f32[27,4,8,128]{3,2,1,0:T(8,128)S(1)}, f32[27,4,8,128]{3,2,1,0:T(8,128)}, u32[]{:S(2)}) %copy-start.1) | copy-done | bytes 442392
  21.6 0.0 copy-start.4
  21.6 0.8 copy-done.4
  22.3 0.6 holding_kernel.1
  22.9 7.3 %collective-permute-done.odd_x = f32[67,8,128]{2,1,0:T(8,128)S(1)} collective-permute-done((f32[67,8,128]{2,1,0:T(8,128)}, f32[67,8,128]{2,1,0:T(8,128)S(1)}, u32[]{:S(2)}, u32[]{:S(2)}) %collective-permute-start) | collective-permute-done | bytes 274464 | tf_op jit(solution)/shard_map/ppermute | solution.py:493
  30.2 0.0 collective-permute-done.1.even_x
  30.2 0.2 second_kernel.1
  30.4 3.2 %collective-permute-start.2 = (f32[512,128]{1,0:T(8,128)S(1)}, f32[512,128]{1,0:T(8,128)S(1)}, u32[]{:S(2)}, u32[]{:S(2)}) collective-permute-start(f32[512,128]{1,0:T(8,128)S(1)} %get-tuple-element.30), channel_id=1, source_target_pairs={{1,2},{3,4},{5,6},{7,8},{9,10},{11,12},{13,14},{15,16},{17,18},{19... | collective-permute-start | bytes 786440 | tf_op jit(solution)/shard_map/ppermute | solution.py:493
  33.6 2.2 %all-gather = f32[1024,128]{1,0:T(8,128)S(1)} all-gather(f32[512,128]{1,0:T(8,128)S(1)} %get-tuple-element.31), channel_id=2, replica_groups={{0,1},{2,3},{4,5},{6,7},{8,9},{10,11},{12,13},{14,15},{16,17},{18,19},{..., dimensions={0}, use_global_device_ids=true | all-gather | bytes 786432 | tf_op jit(solution)/shard_map/all_gather | solution.py:502
  35.8 0.0 copy-start.5
  35.8 7.7 %collective-permute-done.2.odd_y = f32[512,128]{1,0:T(8,128)S(1)} collective-permute-done((f32[512,128]{1,0:T(8,128)S(1)}, f32[512,128]{1,0:T(8,128)S(1)}, u32[]{:S(2)}, u32[]{:S(2)}) %collective-permute-start.2) | collective-permute-done | bytes 262176 | tf_op jit(solution)/shard_map/ppermute | solution.py:493
  43.4 0.0 copy-done.5
  43.5 5.6 %third_kernel.1 = (f32[27,4,8,128]{3,2,1,0:T(8,128)S(1)}, f32[27,4,8,128]{3,2,1,0:T(8,128)S(1)}, f32[2,10,24,128]{3,2,1,0:T(8,128)S(1)}, f32[5,10,24,128]{3,2,1,...) custom-call(f32[27]{0:T(128)S(1)} %copy-done.5, ...), custom_call_target="tpu_custom_call" | custom-call | tf_op jit(solution)/shard_map/third_kernel/pallas_call | solution.py:475
  49.0 9.8 %collective-permute-start.3 = (f32[67,8,128]{2,1,0:T(8,128)S(1)}, f32[67,8,128]{2,1,0:T(8,128)S(1)}, u32[]{:S(2)}, u32[]{:S(2)}) collective-permute-start(f32[67,8,128]{2,1,0:T(8,128)S(1)} %get-tuple-element.39), channel_id=1, source_target_pairs={{32,64},{96,128},{160,192},{224,256},{288,320},{352,384},{416,448}... | collective-permute-start | bytes 823304 | tf_op jit(solution)/shard_map/ppermute | solution.py:493
  58.8 1.9 %collective-permute-start.4 = (f32[67,8,128]{2,1,0:T(8,128)S(1)}, f32[67,8,128]{2,1,0:T(8,128)S(1)}, u32[]{:S(2)}, u32[]{:S(2)}) collective-permute-start(f32[67,8,128]{2,1,0:T(8,128)S(1)} %get-tuple-element.40), channel_id=1, source_target_pairs={{0,32},{64,96},{128,160},{192,224},{256,288},{320,352},{384,416},{... | collective-permute-start | bytes 823304 | tf_op jit(solution)/shard_map/ppermute | solution.py:493
  60.8 7.5 %collective-permute-done.3.odd_x = f32[67,8,128]{2,1,0:T(8,128)S(1)} collective-permute-done((f32[67,8,128]{2,1,0:T(8,128)S(1)}, f32[67,8,128]{2,1,0:T(8,128)S(1)}, u32[]{:S(2)}, u32[]{:S(2)}) %collective-permute-start.3) | collective-permute-done | bytes 274464 | tf_op jit(solution)/shard_map/ppermute | solution.py:493
  68.3 0.0 collective-permute-done.4.even_x
  68.3 0.2 fourth_kernel.1
  68.5 5.2 %collective-permute-start.5 = (f32[520,128]{1,0:T(8,128)S(1)}, f32[520,128]{1,0:T(8,128)S(1)}, u32[]{:S(2)}, u32[]{:S(2)}) collective-permute-start(f32[520,128]{1,0:T(8,128)S(1)} %get-tuple-element.41), channel_id=1, source_target_pairs={{1,2},{3,4},{5,6},{7,8},{9,10},{11,12},{13,14},{15,16},{17,18},{19... | collective-permute-start | bytes 798728 | tf_op jit(solution)/shard_map/ppermute | solution.py:493
  73.7 0.0 copy-start.2
  73.7 0.0 copy-start.3
  73.8 2.3 %all-gather.1 = f32[1040,128]{1,0:T(8,128)S(1)} all-gather(f32[520,128]{1,0:T(8,128)S(1)} %get-tuple-element.42), channel_id=3, replica_groups={{0,1},{2,3},{4,5},{6,7},{8,9},{10,11},{12,13},{14,15},{16,17},{18,19},{..., dimensions={0}, use_global_device_ids=true | all-gather | bytes 798720 | tf_op jit(solution)/shard_map/all_gather | solution.py:502
  76.1 5.6 %collective-permute-done.5.odd_y = f32[520,128]{1,0:T(8,128)S(1)} collective-permute-done((f32[520,128]{1,0:T(8,128)S(1)}, f32[520,128]{1,0:T(8,128)S(1)}, u32[]{:S(2)}, u32[]{:S(2)}) %collective-permute-start.5) | collective-permute-done | bytes 266272 | tf_op jit(solution)/shard_map/ppermute | solution.py:493
  81.7 0.0 copy-done.2
  81.7 0.0 copy-done.3
  81.7 5.9 %fifth_kernel.1 = (f32[27,4,8,128]{3,2,1,0:T(8,128)}, f32[27,4,8,128]{3,2,1,0:T(8,128)}, f32[4,8,128]{2,1,0:T(8,128)}) custom-call(f32[27]{0:T(128)S(1)} %copy-done.5, f32[27,4,8,128]{3,2,1,0:T(8,128)S(1)} %get-tuple-element.32.post, f32[27,4,8,128]{3,2,1,0:T(8,128)S(1)} %get-tuple-element.33.adjoint, f32[2,10,24,128]{3,2,1,0:T(8,128)S(1)} %get-tuple-element.34.wide_cell, ...), custom_call_target="tpu_custom_call" | custom-call | tf_op jit(solution)/shard_map/fifth_kernel/pallas_call | solution.py:475
Async XLA Ops:
  3.8 26.4 %collective-permute-start = (f32[67,8,128]{2,1,0:T(8,128)}, f32[67,8,128]{2,1,0:T(8,128)S(1)}, u32[]{:S(2)}, u32[]{:S(2)}) collective-permute-start(f32[67,8,128]{2,1,0:T(8,128)} %get-tuple-element.28), channel_id=1, source_target_pairs={{32,64},{96,128},{160,192},{224,256},{288,320},{352,384},{416,448}... | collective-permute-start | bytes 823304 | tf_op jit(solution)/shard_map/ppermute | solution.py:493
  17.6 12.6 %collective-permute-start.1 = (f32[67,8,128]{2,1,0:T(8,128)}, f32[67,8,128]{2,1,0:T(8,128)S(1)}, u32[]{:S(2)}, u32[]{:S(2)}) collective-permute-start(f32[67,8,128]{2,1,0:T(8,128)} %get-tuple-element.29), channel_id=1, source_target_pairs={{0,32},{64,96},{128,160},{192,224},{256,288},{320,352},{384,416},{... | collective-permute-start | bytes 823304 | tf_op jit(solution)/shard_map/ppermute | solution.py:493
  19.5 1.0 %copy-start = (f32[27,4,8,128]{3,2,1,0:T(8,128)S(1)}, f32[27,4,8,128]{3,2,1,0:T(8,128)}, u32[]{:S(2)}) copy-start(f32[27,4,8,128]{3,2,1,0:T(8,128)} %refs_1_.1) | copy-start | bytes 1327108
  20.6 1.0 %copy-start.1 = (f32[27,4,8,128]{3,2,1,0:T(8,128)S(1)}, f32[27,4,8,128]{3,2,1,0:T(8,128)}, u32[]{:S(2)}) copy-start(f32[27,4,8,128]{3,2,1,0:T(8,128)} %get-tuple-element.23.refs_0_) | copy-start | bytes 1327108
  21.6 0.8 copy-start.4
  30.4 13.0 %collective-permute-start.2 = (f32[512,128]{1,0:T(8,128)S(1)}, f32[512,128]{1,0:T(8,128)S(1)}, u32[]{:S(2)}, u32[]{:S(2)}) collective-permute-start(f32[512,128]{1,0:T(8,128)S(1)} %get-tuple-element.30), channel_id=1, source_target_pairs={{1,2},{3,4},{5,6},{7,8},{9,10},{11,12},{13,14},{15,16},{17,18},{19... | collective-permute-start | bytes 786440 | tf_op jit(solution)/shard_map/ppermute | solution.py:493
  35.8 7.7 %copy-start.5 = (f32[27]{0:T(128)S(1)}, f32[27]{0:T(128)}, u32[]{:S(2)}) copy-start(f32[27]{0:T(128)} %rates_hbm.5) | copy-start | bytes 328
  49.0 19.2 %collective-permute-start.3 = (f32[67,8,128]{2,1,0:T(8,128)S(1)}, f32[67,8,128]{2,1,0:T(8,128)S(1)}, u32[]{:S(2)}, u32[]{:S(2)}) collective-permute-start(f32[67,8,128]{2,1,0:T(8,128)S(1)} %get-tuple-element.39), channel_id=1, source_target_pairs={{32,64},{96,128},{160,192},{224,256},{288,320},{352,384},{416,448}... | collective-permute-start | bytes 823304 | tf_op jit(solution)/shard_map/ppermute | solution.py:493
  58.8 9.4 %collective-permute-start.4 = (f32[67,8,128]{2,1,0:T(8,128)S(1)}, f32[67,8,128]{2,1,0:T(8,128)S(1)}, u32[]{:S(2)}, u32[]{:S(2)}) collective-permute-start(f32[67,8,128]{2,1,0:T(8,128)S(1)} %get-tuple-element.40), channel_id=1, source_target_pairs={{0,32},{64,96},{128,160},{192,224},{256,288},{320,352},{384,416},{... | collective-permute-start | bytes 823304 | tf_op jit(solution)/shard_map/ppermute | solution.py:493
  68.5 13.2 %collective-permute-start.5 = (f32[520,128]{1,0:T(8,128)S(1)}, f32[520,128]{1,0:T(8,128)S(1)}, u32[]{:S(2)}, u32[]{:S(2)}) collective-permute-start(f32[520,128]{1,0:T(8,128)S(1)} %get-tuple-element.41), channel_id=1, source_target_pairs={{1,2},{3,4},{5,6},{7,8},{9,10},{11,12},{13,14},{15,16},{17,18},{19... | collective-permute-start | bytes 798728 | tf_op jit(solution)/shard_map/ppermute | solution.py:493
  73.7 8.0 %copy-start.2 = (f32[5,4,8,128]{3,2,1,0:T(8,128)S(1)}, f32[5,4,8,128]{3,2,1,0:T(8,128)}, u32[]{:S(2)}) copy-start(f32[5,4,8,128]{3,2,1,0:T(8,128)} %get-tuple-element.35.speed_zero) | copy-start | bytes 245764
  73.7 8.0 %copy-start.3 = (f32[4,8,128]{2,1,0:T(8,128)S(1)}, f32[4,8,128]{2,1,0:T(8,128)}, u32[]{:S(2)}) copy-start(f32[4,8,128]{2,1,0:T(8,128)} %porosity.3) | copy-start | bytes 49156

commit v5 on v4

--- a/solution.py
+++ b/solution.py
@@ -15,7 +15,7 @@
 HALO = 3
 PLANES = NX + 2 * HALO
 ROWS = 3 * NY
-VMEM_LIMIT = 48 * 1024 * 1024
+VMEM_LIMIT = 16 * 1024 * 1024
 FIRST_LIMIT = 64 * 1024 * 1024
 
 SCALE = [
@@ -122,8 +122,11 @@
             wide[name][i, plane + HALO, first : first + rows] = ref[start : start + rows]
 
 
-def unpack(fields, wide, odd_x, even_x, odd_y, even_y):
+def receive_x(fields, wide, odd_x, even_x):
     by_parity("gx", lambda low, high: unpack_x(fields, wide, low, high), odd_x, even_x)
+
+
+def receive_y(fields, wide, odd_y, even_y):
     partner = even_y.at[1 - lax.axis_index("gy") % 2]
     by_parity("gy", lambda low, high: unpack_y(fields, wide, low, high), odd_y, partner)
 
@@ -250,12 +253,75 @@
     return value if shift == 0 else pltpu.roll(value, shift % LANES, axis=1)
 
 
-def pulled(wide, plane, row, direction):
+def own_rows(ref, place):
+    return ref[place + (slice(NY, 2 * NY),)]
+
+
+def edge_rows(ref, place):
+    low, high = ref[place + (slice(NY - 2, 2 * NY - 2),)], ref[place + (slice(NY + 2, 2 * NY + 2),)]
+    return jnp.where(lax.broadcasted_iota(jnp.int32, (NY, LANES), 0) < NY // 2, low, high)
+
+
+def put_edge_rows(ref, place, value):
+    ref[place + (slice(NY - 2, NY + 2),)] = value[: NY // 2]
+    ref[place + (slice(2 * NY - 2, 2 * NY + 2),)] = value[NY // 2 :]
+
+
+def put_own_rows(ref, place, value):
+    ref[place + (slice(NY, 2 * NY),)] = value
+
+
+OWN = (own_rows, put_own_rows)
+EDGE = (edge_rows, put_edge_rows)
+
+
+def shifted(wide, shift):
+    class View:
+        def __getitem__(self, place):
+            return wide[place[:-1] + (slice(place[-1].start + shift, place[-1].stop + shift),)]
+
+    return View()
+
+
+def pulled(wide, plane, rows, direction):
     tiles = []
     for i, (cx, cy, cz) in enumerate(VEL):
-        tile = wide[i, plane - direction * cx, pl.ds(row - direction * cy, NY)]
+        tile = rows(shifted(wide, -direction * cy), (i, plane - direction * cx))
         tiles.append(turned(tile, direction * cz))
     return tiles
+
+
+def forward(where, source, target, cell, speed, rates, inlet, width):
+    get, put = where
+
+    def body(plane, carry):
+        out, values = collide(
+            pulled(source, plane, get, 1), get(cell, (0, plane)), get(cell, (1, plane)), rates, inlet
+        )
+        for i in range(27):
+            put(target, (i, plane), out[i])
+        for i in range(5):
+            put(speed, (i, plane), values[i])
+        return carry
+
+    lax.fori_loop(HALO - width, HALO + NX + width, body, 0)
+
+
+def backward(where, source, target, cell, speed, gain, rates, width):
+    get, put = where
+
+    def body(plane, carry):
+        values = [get(speed, (i, plane)) for i in range(5)]
+        out, grad = collide_back(
+            pulled(source, plane, get, -1), get(cell, (0, plane)), get(cell, (1, plane)), rates,
+            values[:4], values[4],
+        )
+        for i in range(27):
+            put(target, (i, plane), out[i])
+        put(gain, (plane,), grad)
+        return carry
+
+    lax.fori_loop(HALO - width, HALO + NX + width, body, 0)
 
 
 def inlet_speed(start, step):
@@ -331,57 +397,55 @@
     send_y(FIRST, own, odd_x, even_x, to_odd, to_even)
 
 
-def third_kernel(
-    rates_hbm, start_hbm, post, cotangent, cell, odd_x, even_x, odd_y, even_y,
-    last_post, adjoint, wide_cell, speed_one, speed_two, gain, to_odd, to_even,
-    wide_post, next_post, wide_adjoint, rates, start, sems,
-):
-    copies = [
-        pltpu.make_async_copy(rates_hbm, rates, sems.at[0]),
-        pltpu.make_async_copy(start_hbm, start, sems.at[1]),
-    ]
+def fetch(sems, *pairs):
+    copies = [pltpu.make_async_copy(a, b, sems.at[n]) for n, (a, b) in enumerate(pairs)]
     for copy in copies:
         copy.start()
-    for i in range(27):
-        wide_post[i, HALO : HALO + NX, NY : 2 * NY] = post[i]
-        wide_adjoint[i, HALO : HALO + NX, NY : 2 * NY] = cotangent[i]
-    for i in range(2):
-        wide_cell[i, HALO : HALO + NX, NY : 2 * NY] = cell[i]
-    wide = {"post": wide_post, "adjoint": wide_adjoint, "cell": wide_cell}
-    unpack(FIRST, wide, odd_x, even_x, odd_y, even_y)
     for copy in copies:
         copy.wait()
 
-    def forward(step, source, target, speed, width):
-        inlet = inlet_speed(start, step)
-
-        def body(n, carry):
-            plane = n // 2 + (HALO - width)
-            row = (n % 2) * NY + NY // 2
-            here = pl.ds(row, NY)
-            f = pulled(source, plane, row, 1)
-            out, values = collide(f, wide_cell[0, plane, here], wide_cell[1, plane, here], rates, inlet)
-            for i in range(27):
-                target[i, plane, here] = out[i]
-            for i in range(5):
-                speed[i, plane, here] = values[i]
-            return carry
-
-        lax.fori_loop(0, 2 * (NX + 2 * width), body, 0)
-
-    forward(1, wide_post, next_post, speed_one, 2)
-    forward(2, next_post, wide_post, speed_two, 1)
+
+def put_block(wide, block, members):
+    for i in range(members):
+        wide[i, HALO : HALO + NX, NY : 2 * NY] = block[i]
+
+
+def third_early_kernel(
+    rates_hbm, start_hbm, post, cotangent, cell, odd_x, even_x,
+    post_zero, post_one, post_two, wide_adjoint, wide_cell, speed_one, speed_two,
+    rates, start, sems,
+):
+    fetch(sems, (rates_hbm, rates), (start_hbm, start))
+    put_block(post_zero, post, 27)
+    put_block(wide_adjoint, cotangent, 27)
+    put_block(wide_cell, cell, 2)
+    wide = {"post": post_zero, "adjoint": wide_adjoint, "cell": wide_cell}
+    receive_x(FIRST, wide, odd_x, even_x)
+    forward(OWN, post_zero, post_one, wide_cell, speed_one, rates, inlet_speed(start, 1), 2)
+    forward(OWN, post_one, post_two, wide_cell, speed_two, rates, inlet_speed(start, 2), 1)
+
+
+def third_late_kernel(
+    rates_hbm, start_hbm, _0, _1, _2, _3, _4, _5, _6, odd_y, even_y,
+    post_zero, post_one, post_two, wide_adjoint, wide_cell, speed_one, speed_two,
+    last_post, adjoint, gain, to_odd, to_even,
+    rates, start, sems,
+):
+    fetch(sems, (rates_hbm, rates), (start_hbm, start))
+    wide = {"post": post_zero, "adjoint": wide_adjoint, "cell": wide_cell}
+    receive_y(FIRST, wide, odd_y, even_y)
+    forward(EDGE, post_zero, post_one, wide_cell, speed_one, rates, inlet_speed(start, 1), 2)
+    forward(EDGE, post_one, post_two, wide_cell, speed_two, rates, inlet_speed(start, 2), 1)
     inlet = inlet_speed(start, 3)
 
     def last(n, carry):
         plane = n + HALO
-        here = pl.ds(NY, NY)
-        kappa, kind = wide_cell[0, plane, here], wide_cell[1, plane, here]
-        out, values = collide(pulled(wide_post, plane, NY, 1), kappa, kind, rates, inlet)
+        kappa, kind = own_rows(wide_cell, (0, plane)), own_rows(wide_cell, (1, plane))
+        out, values = collide(pulled(post_two, plane, own_rows, 1), kappa, kind, rates, inlet)
         for i in range(27):
             last_post[i, n] = out[i]
         back, grad = collide_back(
-            pulled(wide_adjoint, plane, NY, -1), kappa, kind, rates, values[:4], values[4]
+            pulled(wide_adjoint, plane, own_rows, -1), kappa, kind, rates, values[:4], values[4]
         )
         for i in range(27):
             adjoint[i, n] = back[i]
@@ -407,57 +471,46 @@
     send_y(SECOND, own, odd_x, even_x, to_odd, to_even)
 
 
-def fifth_kernel(
-    rates_hbm, post, adjoint, wide_cell, speed_zero, speed_one, speed_two, gain, porosity,
-    odd_x, even_x, odd_y, even_y,
+def fifth_early_kernel(
+    rates_hbm, post, adjoint, wide_cell, speed_one, _0, odd_x, even_x,
+    speed_two, adjoint_three, adjoint_two, adjoint_one, wide_post, gain_two, gain_one,
+    rates, sems,
+):
+    fetch(sems, (rates_hbm, rates))
+    put_block(wide_post, post, 27)
+    put_block(adjoint_three, adjoint, 27)
+    wide = {"post": wide_post, "adjoint": adjoint_three, "speed": speed_two}
+    receive_x(SECOND, wide, odd_x, even_x)
+    backward(OWN, adjoint_three, adjoint_two, wide_cell, speed_two, gain_two, rates, 2)
+    backward(OWN, adjoint_two, adjoint_one, wide_cell, speed_one, gain_one, rates, 1)
+
+
+def fifth_late_kernel(
+    rates_hbm, wide_cell, speed_zero, speed_one, gain, porosity, odd_y, even_y, _0, _1, _2, _3, _4, _5, _6,
     flow, first_adjoint, sensitivity,
-    wide_post, wide_adjoint, next_adjoint, wide_speed, gains, rates, sem,
+    speed_two, adjoint_three, adjoint_two, adjoint_one, wide_post, gain_two, gain_one,
+    rates, sems,
 ):
-    copy = pltpu.make_async_copy(rates_hbm, rates, sem)
-    copy.start()
-    for i in range(27):
-        wide_post[i, HALO : HALO + NX, NY : 2 * NY] = post[i]
-        wide_adjoint[i, HALO : HALO + NX, NY : 2 * NY] = adjoint[i]
-    wide_speed[...] = speed_two[...]
-    wide = {"post": wide_post, "adjoint": wide_adjoint, "speed": wide_speed}
-    unpack(SECOND, wide, odd_x, even_x, odd_y, even_y)
-    copy.wait()
-
-    def back(source, target, speed, width, place):
-        def body(n, carry):
-            plane = n // 2 + (HALO - width)
-            row = (n % 2) * NY + NY // 2
-            here = pl.ds(row, NY)
-            h = pulled(source, plane, row, -1)
-            values = [speed[i, plane, here] for i in range(5)]
-            out, grad = collide_back(
-                h, wide_cell[0, plane, here], wide_cell[1, plane, here], rates, values[:4], values[4]
-            )
-            for i in range(27):
-                target[i, plane, here] = out[i]
-            gains[place, plane, here] = grad
-            return carry
-
-        lax.fori_loop(0, 2 * (NX + 2 * width), body, 0)
-
-    back(wide_adjoint, next_adjoint, wide_speed, 2, 0)
-    back(next_adjoint, wide_adjoint, speed_one, 1, 1)
+    fetch(sems, (rates_hbm, rates))
+    wide = {"post": wide_post, "adjoint": adjoint_three, "speed": speed_two}
+    receive_y(SECOND, wide, odd_y, even_y)
+    backward(EDGE, adjoint_three, adjoint_two, wide_cell, speed_two, gain_two, rates, 2)
+    backward(EDGE, adjoint_two, adjoint_one, wide_cell, speed_one, gain_one, rates, 1)
 
     def last(n, carry):
         plane = n + HALO
-        here = pl.ds(NY, NY)
-        kappa, kind = wide_cell[0, plane, here], wide_cell[1, plane, here]
+        kappa, kind = own_rows(wide_cell, (0, plane)), own_rows(wide_cell, (1, plane))
         values = [speed_zero[i, n] for i in range(5)]
         out, grad = collide_back(
-            pulled(wide_adjoint, plane, NY, -1), kappa, kind, rates, values[:4], values[4]
+            pulled(adjoint_one, plane, own_rows, -1), kappa, kind, rates, values[:4], values[4]
         )
         for i in range(27):
             first_adjoint[i, n] = out[i]
-        total = ((gain[n] + gains[0, plane, here]) + gains[1, plane, here]) + grad
+        total = ((gain[n] + own_rows(gain_two, (plane,))) + own_rows(gain_one, (plane,))) + grad
         ramp = RAMP_Q * (1.0 + DRAG_MAX) + (1.0 - DRAG_MAX * RAMP_Q) * porosity[n]
         slope = (DRAG_MAX * RAMP_Q * (1.0 + RAMP_Q)) / (ramp * ramp)
         sensitivity[n] = jnp.where(kind < 0.5, slope * total, 0.0)
-        tiles = pulled(wide_post, plane, NY, 1)
+        tiles = pulled(wide_post, plane, own_rows, 1)
         for i in range(27):
             flow[i, n] = tiles[i]
         return carry
@@ -469,7 +522,7 @@
     return jax.ShapeDtypeStruct(shape, jnp.float32)
 
 
-def call(kernel, far, arrays, outs, scratch=(), limit=VMEM_LIMIT):
+def call(kernel, far, arrays, outs, scratch=(), limit=VMEM_LIMIT, aliases=None):
     hbm = pl.BlockSpec(memory_space=pltpu.HBM)
     vmem = pl.BlockSpec(memory_space=pltpu.VMEM)
     return pl.pallas_call(
@@ -479,6 +532,7 @@
         out_specs=tuple(vmem for _ in outs),
         scratch_shapes=[pltpu.VMEM(s, jnp.float32) if isinstance(s, tuple) else s for s in scratch],
         compiler_params=pltpu.CompilerParams(vmem_limit_bytes=limit),
+        input_output_aliases=aliases or {},
         name=kernel.__name__,
     )(*far, *arrays)
 
@@ -525,22 +579,34 @@
     to_odd, to_even = call(second_kernel, (), (post, held, cell) + x_halos, rows)
     y_halos = exchange_y(to_odd, to_even)
     wide_values = (5, PLANES, ROWS, LANES)
+    wides = (wide, wide, wide, wide, (2, PLANES, ROWS, LANES), wide_values, wide_values)
+    scalars = (rates_here, start_here, pltpu.SemaphoreType.DMA((2,)))
+    wides = call(
+        third_early_kernel, (rates, start_step), (post, held, cell) + x_halos, wides, scalars
+    )
     tiles = (PLAN_X[SECOND, 1][1], NY, LANES), (PLAN_X[SECOND, -1][1], NY, LANES)
     rows = (PLAN_Y[SECOND, 1][1], LANES), (PLAN_Y[SECOND, -1][1], LANES)
-    post, adjoint, wide_cell, speed_one, speed_two, gain, to_odd, to_even = call(
-        third_kernel, (rates, start_step), (post, held, cell) + x_halos + y_halos,
-        (block, block, (2, PLANES, ROWS, LANES), wide_values, wide_values, (NX, NY, LANES)) + tiles,
-        (wide, wide, wide, rates_here, start_here, pltpu.SemaphoreType.DMA((2,))),
+    *wides, post, adjoint, gain, to_odd, to_even = call(
+        third_late_kernel, (rates, start_step), tuple(wides) + y_halos,
+        tuple(a.shape for a in wides) + (block, block, (NX, NY, LANES)) + tiles,
+        scalars, aliases={2 + n: n for n in range(len(wides))},
     )
+    wide_cell, speed_one, speed_two = wides[4:]
     x_halos = exchange_x(to_odd, to_even)
     to_odd, to_even = call(fourth_kernel, (), (post, adjoint, speed_two) + x_halos, rows)
     y_halos = exchange_y(to_odd, to_even)
+    scalars = (rates_here, pltpu.SemaphoreType.DMA((1,)))
+    wide_gain = (PLANES, ROWS, LANES)
+    wides = call(
+        fifth_early_kernel, (rates,), (post, adjoint, wide_cell, speed_one, speed_two) + x_halos,
+        (wide_values, wide, wide, wide, wide, wide_gain, wide_gain), scalars, aliases={5: 0},
+    )
     return call(
-        fifth_kernel, (rates,),
-        (post, adjoint, wide_cell, speed_zero, speed_one, speed_two, gain, porosity) + x_halos + y_halos,
-        (block, block, (NX, NY, LANES)),
-        (wide, wide, wide, wide_values, (2, PLANES, ROWS, LANES), rates_here, pltpu.SemaphoreType.DMA(())),
-    )
+        fifth_late_kernel, (rates,),
+        (wide_cell, speed_zero, speed_one, gain, porosity) + y_halos + tuple(wides),
+        (block, block, (NX, NY, LANES)) + tuple(a.shape for a in wides), scalars,
+        aliases={8 + n: 3 + n for n in range(len(wides))},
+    )[:3]
 
 
 def solution(mesh):

time: 88.1 us -> 84.4 us (0.958)
  waiting for transfers between devices: 28.1 us -> 21.5 us
  Pallas kernels: 15 us -> 16.8 us
    ppermute x6, waiting for transfers between devices: 28.1 us -> 21.5 us  [swap(): lax.ppermute(value, axis, [(a, b) for a, b in pairs] + [(b, a) for a, b i...]
    pallas_call x6 -> x8, Pallas kernels: 15 us -> 16.8 us  [call(): pl.pallas_call(kernel, out_shape=tuple((f32(*s) for s in outs)), in_specs...]
  transfers between devices with their start and end apart: 6 -> 6, of which waited for: 4 -> 4; matrix products, arithmetic and copies ran while one was open for 0% -> 0% of each run, Pallas kernels for 1% -> 7%
where the time goes in v5:
time: 84.4 us; the launch traced here: 83.9 us
  starting transfers between devices  36.4 us (43%)
  waiting for transfers between devices  21.5 us (25%)
  Pallas kernels  16.8 us (20%)
  blocking collectives  4.37 us (5%)
  local copies, waits for them, and re-layouts  3.44 us (4%)
  between operations  1.42 us (2%)
    ppermute x6, starting transfers between devices, swap(): lax.ppermute(value, axis, [(a, b) for a, b in pairs] + [(b, a) for a, b i...  36.4 us
    ppermute x6, waiting for transfers between devices, swap(): lax.ppermute(value, axis, [(a, b) for a, b in pairs] + [(b, a) for a, b i...  21.5 us
    pallas_call x8, Pallas kernels, call(): pl.pallas_call(kernel, out_shape=tuple((f32(*s) for s in outs)), in_specs...  16.8 us
    all_gather x2, blocking collectives, exchange_y(): lax.all_gather(to_even, 'gy', axis_index_groups=partners('gy', 0))  4.37 us
    unnamed x12, local copies, waits for them, and re-layouts  3.44 us
  transfers between devices with their start and end apart: 6, of which 4 were waited for; matrix products, arithmetic and copies ran while one was open for 0% of the time, Pallas kernels for 7%

profile of v5, /device:TPU:6, one launch (start us, length us, event | category | flops | bytes accessed | tf_op | source)
XLA Modules:
  0.0 83.9 jit_solution(4097054685791928856)
XLA Ops:
  1.3 2.5 %first_kernel.1 = (f32[27,4,8,128]{3,2,1,0:T(8,128)}, f32[2,4,8,128]{3,2,1,0:T(8,128)}, f32[5,4,8,128]{3,2,1,0:T(8,128)}, f32[67,8,128]{2,1,0:T(8,128)}, f32[67,8,128]{2,1,0:T(8,128)}) custom-call(f32[27]{0:T(128)} %rates_hbm.9, s32[1]{0:T(128)S(6)} %copy.39.start_hbm, f32[27,4,8,128]{3,2,1,0:T(8,128)} %populations.1, f32[27,4,8,128]{3,2,1,0:T(8,128)} %refs_1_.1, ...), custom_call_target="tpu_custom_call" | custom-call | tf_op jit(solution)/shard_map/first_kernel/pallas_call | solution.py:528
  3.8 13.8 %collective-permute-start = (f32[67,8,128]{2,1,0:T(8,128)}, f32[67,8,128]{2,1,0:T(8,128)S(1)}, u32[]{:S(2)}, u32[]{:S(2)}) collective-permute-start(f32[67,8,128]{2,1,0:T(8,128)} %get-tuple-element.45), channel_id=1, source_target_pairs={{32,64},{96,128},{160,192},{224,256},{288,320},{352,384},{416,448}... | collective-permute-start | bytes 823304 | tf_op jit(solution)/shard_map/ppermute | solution.py:547
  17.6 1.9 %collective-permute-start.1 = (f32[67,8,128]{2,1,0:T(8,128)}, f32[67,8,128]{2,1,0:T(8,128)S(1)}, u32[]{:S(2)}, u32[]{:S(2)}) collective-permute-start(f32[67,8,128]{2,1,0:T(8,128)} %get-tuple-element.46), channel_id=1, source_target_pairs={{0,32},{64,96},{128,160},{192,224},{256,288},{320,352},{384,416},{... | collective-permute-start | bytes 823304 | tf_op jit(solution)/shard_map/ppermute | solution.py:547
  19.6 0.0 copy-start
  19.6 1.0 %copy-done = f32[27,4,8,128]{3,2,1,0:T(8,128)S(1)} copy-done((f32[27,4,8,128]{3,2,1,0:T(8,128)S(1)}, f32[27,4,8,128]{3,2,1,0:T(8,128)}, u32[]{:S(2)}) %copy-start) | copy-done | bytes 442392
  20.6 0.0 copy-start.1
  20.6 1.0 %copy-done.1 = f32[27,4,8,128]{3,2,1,0:T(8,128)S(1)} copy-done((f32[27,4,8,128]{3,2,1,0:T(8,128)S(1)}, f32[27,4,8,128]{3,2,1,0:T(8,128)}, u32[]{:S(2)}) %copy-start.1) | copy-done | bytes 442392
  21.6 0.0 copy-start.4
  21.6 0.8 copy-done.4
  22.3 0.6 holding_kernel.1
  22.9 7.3 %collective-permute-done.odd_x = f32[67,8,128]{2,1,0:T(8,128)S(1)} collective-permute-done((f32[67,8,128]{2,1,0:T(8,128)}, f32[67,8,128]{2,1,0:T(8,128)S(1)}, u32[]{:S(2)}, u32[]{:S(2)}) %collective-permute-start) | collective-permute-done | bytes 274464 | tf_op jit(solution)/shard_map/ppermute | solution.py:547
  30.2 0.0 collective-permute-done.1.even_x
  30.2 0.2 second_kernel.1
  30.4 3.2 %collective-permute-start.2 = (f32[512,128]{1,0:T(8,128)S(1)}, f32[512,128]{1,0:T(8,128)S(1)}, u32[]{:S(2)}, u32[]{:S(2)}) collective-permute-start(f32[512,128]{1,0:T(8,128)S(1)} %get-tuple-element.54), channel_id=1, source_target_pairs={{1,2},{3,4},{5,6},{7,8},{9,10},{11,12},{13,14},{15,16},{17,18},{19... | collective-permute-start | bytes 786440 | tf_op jit(solution)/shard_map/ppermute | solution.py:547
  33.6 0.0 copy-start.5
  33.6 0.6 copy-done.5
  34.3 2.7 %third_early_kernel.1 = (f32[27,10,24,128]{3,2,1,0:T(8,128)S(1)}, f32[27,10,24,128]{3,2,1,0:T(8,128)S(1)}, f32[27,10,24,128]{3,2,1,0:T(8,128)S(1)}, f32[27,10,24...) custom-call(f32[27]{0:T(128)S(1)} %copy-done.5, ...), custom_call_target="tpu_custom_call" | custom-call | tf_op jit(solution)/shard_map/third_early_kernel/pallas_call | solution.py:528
  37.0 2.2 %all-gather = f32[1024,128]{1,0:T(8,128)S(1)} all-gather(f32[512,128]{1,0:T(8,128)S(1)} %get-tuple-element.55), channel_id=2, replica_groups={{0,1},{2,3},{4,5},{6,7},{8,9},{10,11},{12,13},{14,15},{16,17},{18,19},{..., dimensions={0}, use_global_device_ids=true | all-gather | bytes 786432 | tf_op jit(solution)/shard_map/all_gather | solution.py:556
  39.2 4.3 %collective-permute-done.2.odd_y = f32[512,128]{1,0:T(8,128)S(1)} collective-permute-done((f32[512,128]{1,0:T(8,128)S(1)}, f32[512,128]{1,0:T(8,128)S(1)}, u32[]{:S(2)}, u32[]{:S(2)}) %collective-permute-start.2) | collective-permute-done | bytes 262176 | tf_op jit(solution)/shard_map/ppermute | solution.py:547
  43.5 3.8 %third_late_kernel.1 = (f32[27,10,24,128]{3,2,1,0:T(8,128)S(1)}, f32[27,10,24,128]{3,2,1,0:T(8,128)S(1)}, f32[27,10,24,128]{3,2,1,0:T(8,128)S(1)}, f32[27,10,24,...) custom-call(f32[27]{0:T(128)S(1)} %copy-done.5, ...), custom_call_target="tpu_custom_call", output_to_operand_aliasing={{0}: (2, {}), {1}: (3, {}), {2}: (4, {}), {3}: (5, {}), {4}... | custom-call | tf_op jit(solution)/shard_map/third_late_kernel/pallas_call | solution.py:528
  47.3 0.0 copy-start.2
  47.3 0.0 copy-start.3
  47.3 9.9 %collective-permute-start.3 = (f32[67,8,128]{2,1,0:T(8,128)S(1)}, f32[67,8,128]{2,1,0:T(8,128)S(1)}, u32[]{:S(2)}, u32[]{:S(2)}) collective-permute-start(f32[67,8,128]{2,1,0:T(8,128)S(1)} %get-tuple-element.63), channel_id=1, source_target_pairs={{32,64},{96,128},{160,192},{224,256},{288,320},{352,384},{416,448}... | collective-permute-start | bytes 823304 | tf_op jit(solution)/shard_map/ppermute | solution.py:547
  57.2 1.9 %collective-permute-start.4 = (f32[67,8,128]{2,1,0:T(8,128)S(1)}, f32[67,8,128]{2,1,0:T(8,128)S(1)}, u32[]{:S(2)}, u32[]{:S(2)}) collective-permute-start(f32[67,8,128]{2,1,0:T(8,128)S(1)} %get-tuple-element.64), channel_id=1, source_target_pairs={{0,32},{64,96},{128,160},{192,224},{256,288},{320,352},{384,416},{... | collective-permute-start | bytes 823304 | tf_op jit(solution)/shard_map/ppermute | solution.py:547
  59.2 7.5 %collective-permute-done.3.odd_x = f32[67,8,128]{2,1,0:T(8,128)S(1)} collective-permute-done((f32[67,8,128]{2,1,0:T(8,128)S(1)}, f32[67,8,128]{2,1,0:T(8,128)S(1)}, u32[]{:S(2)}, u32[]{:S(2)}) %collective-permute-start.3) | collective-permute-done | bytes 274464 | tf_op jit(solution)/shard_map/ppermute | solution.py:547
  66.7 0.0 collective-permute-done.4.even_x
  66.7 0.2 fourth_kernel.1
  66.9 5.7 %collective-permute-start.5 = (f32[520,128]{1,0:T(8,128)S(1)}, f32[520,128]{1,0:T(8,128)S(1)}, u32[]{:S(2)}, u32[]{:S(2)}) collective-permute-start(f32[520,128]{1,0:T(8,128)S(1)} %get-tuple-element.65), channel_id=1, source_target_pairs={{1,2},{3,4},{5,6},{7,8},{9,10},{11,12},{13,14},{15,16},{17,18},{19... | collective-permute-start | bytes 798728 | tf_op jit(solution)/shard_map/ppermute | solution.py:547
  72.6 2.5 %fifth_early_kernel.1 = (f32[5,10,24,128]{3,2,1,0:T(8,128)S(1)}, f32[27,10,24,128]{3,2,1,0:T(8,128)S(1)}, f32[27,10,24,128]{3,2,1,0:T(8,128)S(1)}, f32[27,10,24,...) custom-call(f32[27]{0:T(128)S(1)} %copy-done.5, ...), custom_call_target="tpu_custom_call", output_to_operand_aliasing={{0}: (5, {})} | custom-call | tf_op jit(solution)/shard_map/fifth_early_kernel/pallas_call | solution.py:528
  75.2 2.2 %all-gather.1 = f32[1040,128]{1,0:T(8,128)S(1)} all-gather(f32[520,128]{1,0:T(8,128)S(1)} %get-tuple-element.66), channel_id=3, replica_groups={{0,1},{2,3},{4,5},{6,7},{8,9},{10,11},{12,13},{14,15},{16,17},{18,19},{..., dimensions={0}, use_global_device_ids=true | all-gather | bytes 798720 | tf_op jit(solution)/shard_map/all_gather | solution.py:556
  77.3 2.4 %collective-permute-done.5.odd_y = f32[520,128]{1,0:T(8,128)S(1)} collective-permute-done((f32[520,128]{1,0:T(8,128)S(1)}, f32[520,128]{1,0:T(8,128)S(1)}, u32[]{:S(2)}, u32[]{:S(2)}) %collective-permute-start.5) | collective-permute-done | bytes 266272 | tf_op jit(solution)/shard_map/ppermute | solution.py:547
  79.7 0.0 copy-done.2
  79.7 0.0 copy-done.3
  79.7 4.2 %fifth_late_kernel.1 = (f32[27,4,8,128]{3,2,1,0:T(8,128)}, f32[27,4,8,128]{3,2,1,0:T(8,128)}, f32[4,8,128]{2,1,0:T(8,128)}, f32[5,10,24,128]{3,2,1,0:T(8,128)S(1...) custom-call(f32[27]{0:T(128)S(1)} %copy-done.5, ...), custom_call_target="tpu_custom_call", output_to_operand_aliasing={{3}: (8, {}), {4}: (9, {}), {5}: (10, {}), {6}: (11, {}), {... | custom-call | tf_op jit(solution)/shard_map/fifth_late_kernel/pallas_call | solution.py:528
Async XLA Ops:
  3.8 26.4 %collective-permute-start = (f32[67,8,128]{2,1,0:T(8,128)}, f32[67,8,128]{2,1,0:T(8,128)S(1)}, u32[]{:S(2)}, u32[]{:S(2)}) collective-permute-start(f32[67,8,128]{2,1,0:T(8,128)} %get-tuple-element.45), channel_id=1, source_target_pairs={{32,64},{96,128},{160,192},{224,256},{288,320},{352,384},{416,448}... | collective-permute-start | bytes 823304 | tf_op jit(solution)/shard_map/ppermute | solution.py:547
  17.6 12.6 %collective-permute-start.1 = (f32[67,8,128]{2,1,0:T(8,128)}, f32[67,8,128]{2,1,0:T(8,128)S(1)}, u32[]{:S(2)}, u32[]{:S(2)}) collective-permute-start(f32[67,8,128]{2,1,0:T(8,128)} %get-tuple-element.46), channel_id=1, source_target_pairs={{0,32},{64,96},{128,160},{192,224},{256,288},{320,352},{384,416},{... | collective-permute-start | bytes 823304 | tf_op jit(solution)/shard_map/ppermute | solution.py:547
  19.6 1.0 %copy-start = (f32[27,4,8,128]{3,2,1,0:T(8,128)S(1)}, f32[27,4,8,128]{3,2,1,0:T(8,128)}, u32[]{:S(2)}) copy-start(f32[27,4,8,128]{3,2,1,0:T(8,128)} %refs_1_.1) | copy-start | bytes 1327108
  20.6 1.0 %copy-start.1 = (f32[27,4,8,128]{3,2,1,0:T(8,128)S(1)}, f32[27,4,8,128]{3,2,1,0:T(8,128)}, u32[]{:S(2)}) copy-start(f32[27,4,8,128]{3,2,1,0:T(8,128)} %get-tuple-element.40.refs_0_) | copy-start | bytes 1327108
  21.6 0.8 copy-start.4
  30.4 13.0 %collective-permute-start.2 = (f32[512,128]{1,0:T(8,128)S(1)}, f32[512,128]{1,0:T(8,128)S(1)}, u32[]{:S(2)}, u32[]{:S(2)}) collective-permute-start(f32[512,128]{1,0:T(8,128)S(1)} %get-tuple-element.54), channel_id=1, source_target_pairs={{1,2},{3,4},{5,6},{7,8},{9,10},{11,12},{13,14},{15,16},{17,18},{19... | collective-permute-start | bytes 786440 | tf_op jit(solution)/shard_map/ppermute | solution.py:547
  33.6 0.7 copy-start.5
  47.3 32.4 %copy-start.2 = (f32[5,4,8,128]{3,2,1,0:T(8,128)S(1)}, f32[5,4,8,128]{3,2,1,0:T(8,128)}, u32[]{:S(2)}) copy-start(f32[5,4,8,128]{3,2,1,0:T(8,128)} %get-tuple-element.57.speed_zero) | copy-start | bytes 245764
  47.3 32.4 %copy-start.3 = (f32[4,8,128]{2,1,0:T(8,128)S(1)}, f32[4,8,128]{2,1,0:T(8,128)}, u32[]{:S(2)}) copy-start(f32[4,8,128]{2,1,0:T(8,128)} %porosity.3) | copy-start | bytes 49156
  47.3 19.3 %collective-permute-start.3 = (f32[67,8,128]{2,1,0:T(8,128)S(1)}, f32[67,8,128]{2,1,0:T(8,128)S(1)}, u32[]{:S(2)}, u32[]{:S(2)}) collective-permute-start(f32[67,8,128]{2,1,0:T(8,128)S(1)} %get-tuple-element.63), channel_id=1, source_target_pairs={{32,64},{96,128},{160,192},{224,256},{288,320},{352,384},{416,448}... | collective-permute-start | bytes 823304 | tf_op jit(solution)/shard_map/ppermute | solution.py:547
  57.2 9.4 %collective-permute-start.4 = (f32[67,8,128]{2,1,0:T(8,128)S(1)}, f32[67,8,128]{2,1,0:T(8,128)S(1)}, u32[]{:S(2)}, u32[]{:S(2)}) collective-permute-start(f32[67,8,128]{2,1,0:T(8,128)S(1)} %get-tuple-element.64), channel_id=1, source_target_pairs={{0,32},{64,96},{128,160},{192,224},{256,288},{320,352},{384,416},{... | collective-permute-start | bytes 823304 | tf_op jit(solution)/shard_map/ppermute | solution.py:547
  66.9 12.8 %collective-permute-start.5 = (f32[520,128]{1,0:T(8,128)S(1)}, f32[520,128]{1,0:T(8,128)S(1)}, u32[]{:S(2)}, u32[]{:S(2)}) collective-permute-start(f32[520,128]{1,0:T(8,128)S(1)} %get-tuple-element.65), channel_id=1, source_target_pairs={{1,2},{3,4},{5,6},{7,8},{9,10},{11,12},{13,14},{15,16},{17,18},{19... | collective-permute-start | bytes 798728 | tf_op jit(solution)/shard_map/ppermute | solution.py:547

commit v6 on v5

--- a/solution.py
+++ b/solution.py
@@ -13,6 +13,7 @@
 
 NX, NY, LANES = 4, 8, 128
 HALO = 3
+TOGETHER = {8: 4, 6: 3, 4: 4}
 PLANES = NX + 2 * HALO
 ROWS = 3 * NY
 VMEM_LIMIT = 16 * 1024 * 1024
@@ -291,37 +292,56 @@
     return tiles
 
 
+def planes_loop(first, last, load, work, store):
+    together = TOGETHER[last - first]
+
+    def body(n, carry):
+        planes = [first + together * n + k for k in range(together)]
+        loaded = [load(plane) for plane in planes]
+        results = [work(*values) for values in loaded]
+        for plane, result in zip(planes, results):
+            store(plane, result)
+        return carry
+
+    lax.fori_loop(0, (last - first) // together, body, 0)
+
+
 def forward(where, source, target, cell, speed, rates, inlet, width):
     get, put = where
 
-    def body(plane, carry):
-        out, values = collide(
-            pulled(source, plane, get, 1), get(cell, (0, plane)), get(cell, (1, plane)), rates, inlet
-        )
+    def load(plane):
+        return pulled(source, plane, get, 1), get(cell, (0, plane)), get(cell, (1, plane))
+
+    def work(f, kappa, kind):
+        return collide(f, kappa, kind, rates, inlet)
+
+    def store(plane, result):
+        out, values = result
         for i in range(27):
             put(target, (i, plane), out[i])
         for i in range(5):
             put(speed, (i, plane), values[i])
-        return carry
-
-    lax.fori_loop(HALO - width, HALO + NX + width, body, 0)
+
+    planes_loop(HALO - width, HALO + NX + width, load, work, store)
 
 
 def backward(where, source, target, cell, speed, gain, rates, width):
     get, put = where
 
-    def body(plane, carry):
+    def load(plane):
         values = [get(speed, (i, plane)) for i in range(5)]
-        out, grad = collide_back(
-            pulled(source, plane, get, -1), get(cell, (0, plane)), get(cell, (1, plane)), rates,
-            values[:4], values[4],
-        )
+        return pulled(source, plane, get, -1), get(cell, (0, plane)), get(cell, (1, plane)), values
+
+    def work(h, kappa, kind, values):
+        return collide_back(h, kappa, kind, rates, values[:4], values[4])
+
+    def store(plane, result):
+        out, grad = result
         for i in range(27):
             put(target, (i, plane), out[i])
         put(gain, (plane,), grad)
-        return carry
-
-    lax.fori_loop(HALO - width, HALO + NX + width, body, 0)
+
+    planes_loop(HALO - width, HALO + NX + width, load, work, store)
 
 
 def inlet_speed(start, step):
@@ -338,39 +358,41 @@
 
 def first_kernel(
     rates_hbm, start_hbm, populations, cotangent, porosity, cell_type,
-    post, cell, speed, to_odd, to_even,
-    rates, start, f, gamma, kinds, ends, sems,
+    post_hbm, cell_hbm, speed_hbm, to_odd_hbm, to_even_hbm,
+    rates, start, f, gamma, kinds, ends, post, cell, speed, to_odd, to_even, sems,
 ):
-    copies = [
-        pltpu.make_async_copy(source, target, sems.at[n])
-        for n, (source, target) in enumerate(
-            (
-                (rates_hbm, rates), (start_hbm, start), (porosity, gamma), (cell_type, kinds),
-                (populations, f), (cotangent.at[18:27, 0], ends.at[0]), (cotangent.at[0:9, NX - 1], ends.at[1]),
-            )
-        )
+    small = start_copies(
+        sems, (rates_hbm, rates), (start_hbm, start), (porosity, gamma), (cell_type, kinds)
+    )
+    halves = [
+        start_copies(sems.at[4 + n : 5 + n], (populations.at[:, 2 * n : 2 * n + 2], f.at[:, 2 * n : 2 * n + 2]))
+        for n in range(NX // 2)
     ]
-    for copy in copies:
-        copy.start()
-    for copy in copies[:5]:
-        copy.wait()
+    tail = start_copies(
+        sems.at[6:8], (cotangent.at[18:27, 0], ends.at[0]), (cotangent.at[0:9, NX - 1], ends.at[1])
+    )
+    small()
     inlet = inlet_speed(start, 0)
-
-    def plane_step(plane, carry):
-        kind = kinds[plane].astype(jnp.float32)
-        kappa = kappa_of(gamma[plane], kind)
-        cell[0, plane] = kappa
-        cell[1, plane] = kind
-        out, values = collide([f[i, plane] for i in range(27)], kappa, kind, rates, inlet)
-        for i in range(27):
-            post[i, plane] = out[i]
-        for i in range(5):
-            speed[i, plane] = values[i]
-        return carry
-
-    lax.fori_loop(0, NX, plane_step, 0)
-    for copy in copies[5:]:
-        copy.wait()
+    done = []
+    for n, arrived in enumerate(halves):
+        arrived()
+        planes = range(2 * n, 2 * n + 2)
+        results = []
+        for plane in planes:
+            kind = kinds[plane].astype(jnp.float32)
+            kappa = kappa_of(gamma[plane], kind)
+            cell[0, plane] = kappa
+            cell[1, plane] = kind
+            results.append(collide([f[i, plane] for i in range(27)], kappa, kind, rates, inlet))
+        for plane, (out, values) in zip(planes, results):
+            for i in range(27):
+                post[i, plane] = out[i]
+            for i in range(5):
+                speed[i, plane] = values[i]
+        part = slice(2 * n, 2 * n + 2)
+        done.append(start_copies(sems.at[4 + n : 5 + n], (post.at[:, part], post_hbm.at[:, part])))
+    done.append(start_copies(sems, (cell, cell_hbm), (speed, speed_hbm)))
+    tail()
 
     def read(name, i, plane):
         if name == "adjoint":
@@ -378,6 +400,9 @@
         return {"post": post, "cell": cell}[name][i, plane]
 
     send_x(FIRST, read, to_odd, to_even)
+    done.append(start_copies(sems.at[6:8], (to_odd, to_odd_hbm), (to_even, to_even_hbm)))
+    for wait in done:
+        wait()
 
 
 def holding_kernel(*refs):
@@ -397,12 +422,16 @@
     send_y(FIRST, own, odd_x, even_x, to_odd, to_even)
 
 
-def fetch(sems, *pairs):
+def start_copies(sems, *pairs):
     copies = [pltpu.make_async_copy(a, b, sems.at[n]) for n, (a, b) in enumerate(pairs)]
     for copy in copies:
         copy.start()
-    for copy in copies:
-        copy.wait()
+
+    def wait():
+        for copy in copies:
+            copy.wait()
+
+    return wait
 
 
 def put_block(wide, block, members):
@@ -415,12 +444,13 @@
     post_zero, post_one, post_two, wide_adjoint, wide_cell, speed_one, speed_two,
     rates, start, sems,
 ):
-    fetch(sems, (rates_hbm, rates), (start_hbm, start))
+    wait = start_copies(sems, (rates_hbm, rates), (start_hbm, start))
     put_block(post_zero, post, 27)
     put_block(wide_adjoint, cotangent, 27)
     put_block(wide_cell, cell, 2)
     wide = {"post": post_zero, "adjoint": wide_adjoint, "cell": wide_cell}
     receive_x(FIRST, wide, odd_x, even_x)
+    wait()
     forward(OWN, post_zero, post_one, wide_cell, speed_one, rates, inlet_speed(start, 1), 2)
     forward(OWN, post_one, post_two, wide_cell, speed_two, rates, inlet_speed(start, 2), 1)
 
@@ -431,28 +461,33 @@
     last_post, adjoint, gain, to_odd, to_even,
     rates, start, sems,
 ):
-    fetch(sems, (rates_hbm, rates), (start_hbm, start))
+    wait = start_copies(sems, (rates_hbm, rates), (start_hbm, start))
     wide = {"post": post_zero, "adjoint": wide_adjoint, "cell": wide_cell}
     receive_y(FIRST, wide, odd_y, even_y)
+    wait()
     forward(EDGE, post_zero, post_one, wide_cell, speed_one, rates, inlet_speed(start, 1), 2)
     forward(EDGE, post_one, post_two, wide_cell, speed_two, rates, inlet_speed(start, 2), 1)
     inlet = inlet_speed(start, 3)
 
-    def last(n, carry):
+    def load(n):
         plane = n + HALO
-        kappa, kind = own_rows(wide_cell, (0, plane)), own_rows(wide_cell, (1, plane))
-        out, values = collide(pulled(post_two, plane, own_rows, 1), kappa, kind, rates, inlet)
+        return (
+            pulled(post_two, plane, own_rows, 1), pulled(wide_adjoint, plane, own_rows, -1),
+            own_rows(wide_cell, (0, plane)), own_rows(wide_cell, (1, plane)),
+        )
+
+    def work(f, h, kappa, kind):
+        out, values = collide(f, kappa, kind, rates, inlet)
+        return out, collide_back(h, kappa, kind, rates, values[:4], values[4])
+
+    def store(n, result):
+        out, (back, grad) = result
         for i in range(27):
             last_post[i, n] = out[i]
-        back, grad = collide_back(
-            pulled(wide_adjoint, plane, own_rows, -1), kappa, kind, rates, values[:4], values[4]
-        )
-        for i in range(27):
             adjoint[i, n] = back[i]
         gain[n] = grad
-        return carry
-
-    lax.fori_loop(0, NX, last, 0)
+
+    planes_loop(0, NX, load, work, store)
 
     def read(name, i, plane):
         if name == "speed":
@@ -476,11 +511,12 @@
     speed_two, adjoint_three, adjoint_two, adjoint_one, wide_post, gain_two, gain_one,
     rates, sems,
 ):
-    fetch(sems, (rates_hbm, rates))
+    wait = start_copies(sems, (rates_hbm, rates))
     put_block(wide_post, post, 27)
     put_block(adjoint_three, adjoint, 27)
     wide = {"post": wide_post, "adjoint": adjoint_three, "speed": speed_two}
     receive_x(SECOND, wide, odd_x, even_x)
+    wait()
     backward(OWN, adjoint_three, adjoint_two, wide_cell, speed_two, gain_two, rates, 2)
     backward(OWN, adjoint_two, adjoint_one, wide_cell, speed_one, gain_one, rates, 1)
 
@@ -489,47 +525,61 @@
     rates_hbm, wide_cell, speed_zero, speed_one, gain, porosity, odd_y, even_y, _0, _1, _2, _3, _4, _5, _6,
     flow, first_adjoint, sensitivity,
     speed_two, adjoint_three, adjoint_two, adjoint_one, wide_post, gain_two, gain_one,
-    rates, sems,
+    rates, flow_here, adjoint_here, sensitivity_here, sems,
 ):
-    fetch(sems, (rates_hbm, rates))
+    wait = start_copies(sems, (rates_hbm, rates))
     wide = {"post": wide_post, "adjoint": adjoint_three, "speed": speed_two}
     receive_y(SECOND, wide, odd_y, even_y)
+
+    def run(n, carry):
+        tiles = pulled(wide_post, n + HALO, own_rows, 1)
+        for i in range(27):
+            flow_here[i, n] = tiles[i]
+        return carry
+
+    lax.fori_loop(0, NX, run, 0)
+    wait()
+    wait = start_copies(sems, (flow_here, flow))
     backward(EDGE, adjoint_three, adjoint_two, wide_cell, speed_two, gain_two, rates, 2)
     backward(EDGE, adjoint_two, adjoint_one, wide_cell, speed_one, gain_one, rates, 1)
 
-    def last(n, carry):
+    def load(n):
         plane = n + HALO
+        total = (gain[n] + own_rows(gain_two, (plane,))) + own_rows(gain_one, (plane,))
+        ramp = RAMP_Q * (1.0 + DRAG_MAX) + (1.0 - DRAG_MAX * RAMP_Q) * porosity[n]
+        slope = (DRAG_MAX * RAMP_Q * (1.0 + RAMP_Q)) / (ramp * ramp)
         kappa, kind = own_rows(wide_cell, (0, plane)), own_rows(wide_cell, (1, plane))
         values = [speed_zero[i, n] for i in range(5)]
-        out, grad = collide_back(
-            pulled(adjoint_one, plane, own_rows, -1), kappa, kind, rates, values[:4], values[4]
-        )
+        return pulled(adjoint_one, plane, own_rows, -1), kappa, kind, values, total, slope
+
+    def work(h, kappa, kind, values, total, slope):
+        out, grad = collide_back(h, kappa, kind, rates, values[:4], values[4])
+        return out, jnp.where(kind < 0.5, slope * (total + grad), 0.0)
+
+    def store(n, result):
+        out, gradient = result
         for i in range(27):
-            first_adjoint[i, n] = out[i]
-        total = ((gain[n] + own_rows(gain_two, (plane,))) + own_rows(gain_one, (plane,))) + grad
-        ramp = RAMP_Q * (1.0 + DRAG_MAX) + (1.0 - DRAG_MAX * RAMP_Q) * porosity[n]
-        slope = (DRAG_MAX * RAMP_Q * (1.0 + RAMP_Q)) / (ramp * ramp)
-        sensitivity[n] = jnp.where(kind < 0.5, slope * total, 0.0)
-        tiles = pulled(wide_post, plane, own_rows, 1)
-        for i in range(27):
-            flow[i, n] = tiles[i]
-        return carry
-
-    lax.fori_loop(0, NX, last, 0)
+            adjoint_here[i, n] = out[i]
+        sensitivity_here[n] = gradient
+
+    planes_loop(0, NX, load, work, store)
+    last = start_copies(sems.at[1:3], (adjoint_here, first_adjoint), (sensitivity_here, sensitivity))
+    wait()
+    last()
 
 
 def f32(*shape):
     return jax.ShapeDtypeStruct(shape, jnp.float32)
 
 
-def call(kernel, far, arrays, outs, scratch=(), limit=VMEM_LIMIT, aliases=None):
+def call(kernel, far, arrays, outs, scratch=(), limit=VMEM_LIMIT, aliases=None, far_outs=0):
     hbm = pl.BlockSpec(memory_space=pltpu.HBM)
     vmem = pl.BlockSpec(memory_space=pltpu.VMEM)
     return pl.pallas_call(
         kernel,
         out_shape=tuple(f32(*s) for s in outs),
         in_specs=[hbm] * len(far) + [vmem] * len(arrays),
-        out_specs=tuple(vmem for _ in outs),
+        out_specs=(hbm,) * far_outs + (vmem,) * (len(outs) - far_outs),
         scratch_shapes=[pltpu.VMEM(s, jnp.float32) if isinstance(s, tuple) else s for s in scratch],
         compiler_params=pltpu.CompilerParams(vmem_limit_bytes=limit),
         input_output_aliases=aliases or {},
@@ -567,9 +617,11 @@
         (block, (2, NX, NY, LANES), (5, NX, NY, LANES)) + tiles,
         (
             rates_here, start_here, block, (NX, NY, LANES), pltpu.VMEM((NX, NY, LANES), jnp.int32),
-            (2, 9, NY, LANES), pltpu.SemaphoreType.DMA((7,)),
+            (2, 9, NY, LANES), block, (2, NX, NY, LANES), (5, NX, NY, LANES), *tiles,
+            pltpu.SemaphoreType.DMA((8,)),
         ),
         FIRST_LIMIT,
+        far_outs=5,
     )
     kept = (post, cotangent, cell)
     post, held, cell = call(
@@ -604,8 +656,9 @@
     return call(
         fifth_late_kernel, (rates,),
         (wide_cell, speed_zero, speed_one, gain, porosity) + y_halos + tuple(wides),
-        (block, block, (NX, NY, LANES)) + tuple(a.shape for a in wides), scalars,
-        aliases={8 + n: 3 + n for n in range(len(wides))},
+        (block, block, (NX, NY, LANES)) + tuple(a.shape for a in wides),
+        (rates_here, block, block, (NX, NY, LANES), pltpu.SemaphoreType.DMA((3,))),
+        aliases={8 + n: 3 + n for n in range(len(wides))}, far_outs=3,
     )[:3]
 
 

time: 84.4 us -> 82 us (0.972)
  Pallas kernels: 16.8 us -> 12.4 us
  waiting for transfers between devices: 21.5 us -> 23.9 us
    pallas_call x8, Pallas kernels: 16.8 us -> 12.4 us  [call(): pl.pallas_call(kernel, out_shape=tuple((f32(*s) for s in outs)), in_specs...]
    ppermute x6, waiting for transfers between devices: 21.5 us -> 23.9 us  [swap(): lax.ppermute(value, axis, [(a, b) for a, b in pairs] + [(b, a) for a, b i...]
  transfers between devices with their start and end apart: 6 -> 6, of which waited for: 4 -> 4; matrix products, arithmetic and copies ran while one was open for 0% -> 0% of each run, Pallas kernels for 7% -> 5%
where the time goes in v6:
time: 82 us; the launch traced here: 81.5 us
  starting transfers between devices  36 us (44%)
  waiting for transfers between devices  23.9 us (29%)
  Pallas kernels  12.4 us (15%)
  blocking collectives  4.37 us (5%)
  local copies, waits for them, and re-layouts  3.44 us (4%)
  between operations  1.42 us (2%)
    ppermute x6, starting transfers between devices, swap(): lax.ppermute(value, axis, [(a, b) for a, b in pairs] + [(b, a) for a, b i...  36 us
    ppermute x6, waiting for transfers between devices, swap(): lax.ppermute(value, axis, [(a, b) for a, b in pairs] + [(b, a) for a, b i...  23.9 us
    pallas_call x8, Pallas kernels, call(): pl.pallas_call(kernel, out_shape=tuple((f32(*s) for s in outs)), in_specs...  12.4 us
    all_gather x2, blocking collectives, exchange_y(): lax.all_gather(to_even, 'gy', axis_index_groups=partners('gy', 0))  4.37 us
    unnamed x12, local copies, waits for them, and re-layouts  3.44 us
  transfers between devices with their start and end apart: 6, of which 4 were waited for; matrix products, arithmetic and copies ran while one was open for 0% of the time, Pallas kernels for 5%

profile of v6, /device:TPU:6, one launch (start us, length us, event | category | flops | bytes accessed | tf_op | source)
XLA Modules:
  0.0 81.5 jit_solution(14512518616095053112)
XLA Ops:
  1.3 2.3 %first_kernel.1 = (f32[27,4,8,128]{3,2,1,0:T(8,128)}, f32[2,4,8,128]{3,2,1,0:T(8,128)}, f32[5,4,8,128]{3,2,1,0:T(8,128)}, f32[67,8,128]{2,1,0:T(8,128)}, f32[67,8,128]{2,1,0:T(8,128)}) custom-call(f32[27]{0:T(128)} %rates_hbm.9, s32[1]{0:T(128)S(6)} %copy.39.start_hbm, f32[27,4,8,128]{3,2,1,0:T(8,128)} %populations.1, f32[27,4,8,128]{3,2,1,0:T(8,128)} %refs_1_.1, ...), custom_call_target="tpu_custom_call" | custom-call | tf_op jit(solution)/shard_map/first_kernel/pallas_call | solution.py:578
  3.5 13.8 %collective-permute-start = (f32[67,8,128]{2,1,0:T(8,128)}, f32[67,8,128]{2,1,0:T(8,128)S(1)}, u32[]{:S(2)}, u32[]{:S(2)}) collective-permute-start(f32[67,8,128]{2,1,0:T(8,128)} %get-tuple-element.45), channel_id=1, source_target_pairs={{32,64},{96,128},{160,192},{224,256},{288,320},{352,384},{416,448}... | collective-permute-start | bytes 823304 | tf_op jit(solution)/shard_map/ppermute | solution.py:597
  17.4 1.9 %collective-permute-start.1 = (f32[67,8,128]{2,1,0:T(8,128)}, f32[67,8,128]{2,1,0:T(8,128)S(1)}, u32[]{:S(2)}, u32[]{:S(2)}) collective-permute-start(f32[67,8,128]{2,1,0:T(8,128)} %get-tuple-element.46), channel_id=1, source_target_pairs={{0,32},{64,96},{128,160},{192,224},{256,288},{320,352},{384,416},{... | collective-permute-start | bytes 823304 | tf_op jit(solution)/shard_map/ppermute | solution.py:597
  19.3 0.0 copy-start
  19.3 1.0 %copy-done = f32[27,4,8,128]{3,2,1,0:T(8,128)S(1)} copy-done((f32[27,4,8,128]{3,2,1,0:T(8,128)S(1)}, f32[27,4,8,128]{3,2,1,0:T(8,128)}, u32[]{:S(2)}) %copy-start) | copy-done | bytes 442392
  20.3 0.0 copy-start.1
  20.3 1.0 %copy-done.1 = f32[27,4,8,128]{3,2,1,0:T(8,128)S(1)} copy-done((f32[27,4,8,128]{3,2,1,0:T(8,128)S(1)}, f32[27,4,8,128]{3,2,1,0:T(8,128)}, u32[]{:S(2)}) %copy-start.1) | copy-done | bytes 442392
  21.3 0.0 copy-start.4
  21.3 0.8 copy-done.4
  22.1 0.6 holding_kernel.1
  22.7 7.3 %collective-permute-done.odd_x = f32[67,8,128]{2,1,0:T(8,128)S(1)} collective-permute-done((f32[67,8,128]{2,1,0:T(8,128)}, f32[67,8,128]{2,1,0:T(8,128)S(1)}, u32[]{:S(2)}, u32[]{:S(2)}) %collective-permute-start) | collective-permute-done | bytes 274464 | tf_op jit(solution)/shard_map/ppermute | solution.py:597
  29.9 0.0 collective-permute-done.1.even_x
  30.0 0.2 second_kernel.1
  30.2 3.2 %collective-permute-start.2 = (f32[512,128]{1,0:T(8,128)S(1)}, f32[512,128]{1,0:T(8,128)S(1)}, u32[]{:S(2)}, u32[]{:S(2)}) collective-permute-start(f32[512,128]{1,0:T(8,128)S(1)} %get-tuple-element.54), channel_id=1, source_target_pairs={{1,2},{3,4},{5,6},{7,8},{9,10},{11,12},{13,14},{15,16},{17,18},{19... | collective-permute-start | bytes 786440 | tf_op jit(solution)/shard_map/ppermute | solution.py:597
  33.3 0.0 copy-start.5
  33.4 0.6 copy-done.5
  34.0 1.9 %third_early_kernel.1 = (f32[27,10,24,128]{3,2,1,0:T(8,128)S(1)}, f32[27,10,24,128]{3,2,1,0:T(8,128)S(1)}, f32[27,10,24,128]{3,2,1,0:T(8,128)S(1)}, f32[27,10,24...) custom-call(f32[27]{0:T(128)S(1)} %copy-done.5, ...), custom_call_target="tpu_custom_call" | custom-call | tf_op jit(solution)/shard_map/third_early_kernel/pallas_call | solution.py:578
  35.9 2.2 %all-gather = f32[1024,128]{1,0:T(8,128)S(1)} all-gather(f32[512,128]{1,0:T(8,128)S(1)} %get-tuple-element.55), channel_id=2, replica_groups={{0,1},{2,3},{4,5},{6,7},{8,9},{10,11},{12,13},{14,15},{16,17},{18,19},{..., dimensions={0}, use_global_device_ids=true | all-gather | bytes 786432 | tf_op jit(solution)/shard_map/all_gather | solution.py:606
  38.1 5.1 %collective-permute-done.2.odd_y = f32[512,128]{1,0:T(8,128)S(1)} collective-permute-done((f32[512,128]{1,0:T(8,128)S(1)}, f32[512,128]{1,0:T(8,128)S(1)}, u32[]{:S(2)}, u32[]{:S(2)}) %collective-permute-start.2) | collective-permute-done | bytes 262176 | tf_op jit(solution)/shard_map/ppermute | solution.py:597
  43.2 2.6 %third_late_kernel.1 = (f32[27,10,24,128]{3,2,1,0:T(8,128)S(1)}, f32[27,10,24,128]{3,2,1,0:T(8,128)S(1)}, f32[27,10,24,128]{3,2,1,0:T(8,128)S(1)}, f32[27,10,24,...) custom-call(f32[27]{0:T(128)S(1)} %copy-done.5, ...), custom_call_target="tpu_custom_call", output_to_operand_aliasing={{0}: (2, {}), {1}: (3, {}), {2}: (4, {}), {3}: (5, {}), {4}... | custom-call | tf_op jit(solution)/shard_map/third_late_kernel/pallas_call | solution.py:578
  45.8 0.0 copy-start.2
  45.8 0.0 copy-start.3
  45.8 9.9 %collective-permute-start.3 = (f32[67,8,128]{2,1,0:T(8,128)S(1)}, f32[67,8,128]{2,1,0:T(8,128)S(1)}, u32[]{:S(2)}, u32[]{:S(2)}) collective-permute-start(f32[67,8,128]{2,1,0:T(8,128)S(1)} %get-tuple-element.63), channel_id=1, source_target_pairs={{32,64},{96,128},{160,192},{224,256},{288,320},{352,384},{416,448}... | collective-permute-start | bytes 823304 | tf_op jit(solution)/shard_map/ppermute | solution.py:597
  55.7 1.9 %collective-permute-start.4 = (f32[67,8,128]{2,1,0:T(8,128)S(1)}, f32[67,8,128]{2,1,0:T(8,128)S(1)}, u32[]{:S(2)}, u32[]{:S(2)}) collective-permute-start(f32[67,8,128]{2,1,0:T(8,128)S(1)} %get-tuple-element.64), channel_id=1, source_target_pairs={{0,32},{64,96},{128,160},{192,224},{256,288},{320,352},{384,416},{... | collective-permute-start | bytes 823304 | tf_op jit(solution)/shard_map/ppermute | solution.py:597
  57.6 7.5 %collective-permute-done.3.odd_x = f32[67,8,128]{2,1,0:T(8,128)S(1)} collective-permute-done((f32[67,8,128]{2,1,0:T(8,128)S(1)}, f32[67,8,128]{2,1,0:T(8,128)S(1)}, u32[]{:S(2)}, u32[]{:S(2)}) %collective-permute-start.3) | collective-permute-done | bytes 274464 | tf_op jit(solution)/shard_map/ppermute | solution.py:597
  65.1 0.0 collective-permute-done.4.even_x
  65.1 0.2 fourth_kernel.1
  65.3 5.3 %collective-permute-start.5 = (f32[520,128]{1,0:T(8,128)S(1)}, f32[520,128]{1,0:T(8,128)S(1)}, u32[]{:S(2)}, u32[]{:S(2)}) collective-permute-start(f32[520,128]{1,0:T(8,128)S(1)} %get-tuple-element.65), channel_id=1, source_target_pairs={{1,2},{3,4},{5,6},{7,8},{9,10},{11,12},{13,14},{15,16},{17,18},{19... | collective-permute-start | bytes 798728 | tf_op jit(solution)/shard_map/ppermute | solution.py:597
  70.6 1.8 %fifth_early_kernel.1 = (f32[5,10,24,128]{3,2,1,0:T(8,128)S(1)}, f32[27,10,24,128]{3,2,1,0:T(8,128)S(1)}, f32[27,10,24,128]{3,2,1,0:T(8,128)S(1)}, f32[27,10,24,...) custom-call(f32[27]{0:T(128)S(1)} %copy-done.5, ...), custom_call_target="tpu_custom_call", output_to_operand_aliasing={{0}: (5, {})} | custom-call | tf_op jit(solution)/shard_map/fifth_early_kernel/pallas_call | solution.py:578
  72.4 2.2 %all-gather.1 = f32[1040,128]{1,0:T(8,128)S(1)} all-gather(f32[520,128]{1,0:T(8,128)S(1)} %get-tuple-element.66), channel_id=3, replica_groups={{0,1},{2,3},{4,5},{6,7},{8,9},{10,11},{12,13},{14,15},{16,17},{18,19},{..., dimensions={0}, use_global_device_ids=true | all-gather | bytes 798720 | tf_op jit(solution)/shard_map/all_gather | solution.py:606
  74.6 4.0 %collective-permute-done.5.odd_y = f32[520,128]{1,0:T(8,128)S(1)} collective-permute-done((f32[520,128]{1,0:T(8,128)S(1)}, f32[520,128]{1,0:T(8,128)S(1)}, u32[]{:S(2)}, u32[]{:S(2)}) %collective-permute-start.5) | collective-permute-done | bytes 266272 | tf_op jit(solution)/shard_map/ppermute | solution.py:597
  78.6 0.0 copy-done.2
  78.6 0.0 copy-done.3
  78.6 2.9 %fifth_late_kernel.1 = (f32[27,4,8,128]{3,2,1,0:T(8,128)}, f32[27,4,8,128]{3,2,1,0:T(8,128)}, f32[4,8,128]{2,1,0:T(8,128)}, f32[5,10,24,128]{3,2,1,0:T(8,128)S(1...) custom-call(f32[27]{0:T(128)S(1)} %copy-done.5, ...), custom_call_target="tpu_custom_call", output_to_operand_aliasing={{3}: (8, {}), {4}: (9, {}), {5}: (10, {}), {6}: (11, {}), {... | custom-call | tf_op jit(solution)/shard_map/fifth_late_kernel/pallas_call | solution.py:578
Async XLA Ops:
  3.5 26.4 %collective-permute-start = (f32[67,8,128]{2,1,0:T(8,128)}, f32[67,8,128]{2,1,0:T(8,128)S(1)}, u32[]{:S(2)}, u32[]{:S(2)}) collective-permute-start(f32[67,8,128]{2,1,0:T(8,128)} %get-tuple-element.45), channel_id=1, source_target_pairs={{32,64},{96,128},{160,192},{224,256},{288,320},{352,384},{416,448}... | collective-permute-start | bytes 823304 | tf_op jit(solution)/shard_map/ppermute | solution.py:597
  17.4 12.6 %collective-permute-start.1 = (f32[67,8,128]{2,1,0:T(8,128)}, f32[67,8,128]{2,1,0:T(8,128)S(1)}, u32[]{:S(2)}, u32[]{:S(2)}) collective-permute-start(f32[67,8,128]{2,1,0:T(8,128)} %get-tuple-element.46), channel_id=1, source_target_pairs={{0,32},{64,96},{128,160},{192,224},{256,288},{320,352},{384,416},{... | collective-permute-start | bytes 823304 | tf_op jit(solution)/shard_map/ppermute | solution.py:597
  19.3 1.0 %copy-start = (f32[27,4,8,128]{3,2,1,0:T(8,128)S(1)}, f32[27,4,8,128]{3,2,1,0:T(8,128)}, u32[]{:S(2)}) copy-start(f32[27,4,8,128]{3,2,1,0:T(8,128)} %refs_1_.1) | copy-start | bytes 1327108
  20.3 1.0 %copy-start.1 = (f32[27,4,8,128]{3,2,1,0:T(8,128)S(1)}, f32[27,4,8,128]{3,2,1,0:T(8,128)}, u32[]{:S(2)}) copy-start(f32[27,4,8,128]{3,2,1,0:T(8,128)} %get-tuple-element.40.refs_0_) | copy-start | bytes 1327108
  21.3 0.8 copy-start.4
  30.2 13.0 %collective-permute-start.2 = (f32[512,128]{1,0:T(8,128)S(1)}, f32[512,128]{1,0:T(8,128)S(1)}, u32[]{:S(2)}, u32[]{:S(2)}) collective-permute-start(f32[512,128]{1,0:T(8,128)S(1)} %get-tuple-element.54), channel_id=1, source_target_pairs={{1,2},{3,4},{5,6},{7,8},{9,10},{11,12},{13,14},{15,16},{17,18},{19... | collective-permute-start | bytes 786440 | tf_op jit(solution)/shard_map/ppermute | solution.py:597
  33.3 0.7 copy-start.5
  45.8 32.8 %copy-start.2 = (f32[5,4,8,128]{3,2,1,0:T(8,128)S(1)}, f32[5,4,8,128]{3,2,1,0:T(8,128)}, u32[]{:S(2)}) copy-start(f32[5,4,8,128]{3,2,1,0:T(8,128)} %get-tuple-element.57.speed_zero) | copy-start | bytes 245764
  45.8 32.8 %copy-start.3 = (f32[4,8,128]{2,1,0:T(8,128)S(1)}, f32[4,8,128]{2,1,0:T(8,128)}, u32[]{:S(2)}) copy-start(f32[4,8,128]{2,1,0:T(8,128)} %porosity.3) | copy-start | bytes 49156
  45.8 19.3 %collective-permute-start.3 = (f32[67,8,128]{2,1,0:T(8,128)S(1)}, f32[67,8,128]{2,1,0:T(8,128)S(1)}, u32[]{:S(2)}, u32[]{:S(2)}) collective-permute-start(f32[67,8,128]{2,1,0:T(8,128)S(1)} %get-tuple-element.63), channel_id=1, source_target_pairs={{32,64},{96,128},{160,192},{224,256},{288,320},{352,384},{416,448}... | collective-permute-start | bytes 823304 | tf_op jit(solution)/shard_map/ppermute | solution.py:597
  55.7 9.4 %collective-permute-start.4 = (f32[67,8,128]{2,1,0:T(8,128)S(1)}, f32[67,8,128]{2,1,0:T(8,128)S(1)}, u32[]{:S(2)}, u32[]{:S(2)}) collective-permute-start(f32[67,8,128]{2,1,0:T(8,128)S(1)} %get-tuple-element.64), channel_id=1, source_target_pairs={{0,32},{64,96},{128,160},{192,224},{256,288},{320,352},{384,416},{... | collective-permute-start | bytes 823304 | tf_op jit(solution)/shard_map/ppermute | solution.py:597
  65.3 13.2 %collective-permute-start.5 = (f32[520,128]{1,0:T(8,128)S(1)}, f32[520,128]{1,0:T(8,128)S(1)}, u32[]{:S(2)}, u32[]{:S(2)}) collective-permute-start(f32[520,128]{1,0:T(8,128)S(1)} %get-tuple-element.65), channel_id=1, source_target_pairs={{1,2},{3,4},{5,6},{7,8},{9,10},{11,12},{13,14},{15,16},{17,18},{19... | collective-permute-start | bytes 798728 | tf_op jit(solution)/shard_map/ppermute | solution.py:597

commit v7 on v6

--- a/solution.py
+++ b/solution.py
@@ -13,7 +13,7 @@
 
 NX, NY, LANES = 4, 8, 128
 HALO = 3
-TOGETHER = {8: 4, 6: 3, 4: 4}
+TOGETHER = {6: 3, 4: 4, 2: 2}
 PLANES = NX + 2 * HALO
 ROWS = 3 * NY
 VMEM_LIMIT = 16 * 1024 * 1024
@@ -28,73 +28,109 @@
 
 
 def reach(component, side, width, direction):
-    if direction in (0, 2):
-        return width
     inward = -side * direction
     return max(0, width - (0 if component == inward else 1 if component == 0 else 2))
 
 
-def member_reach(field, i, axis, side):
-    _, _, width, direction = field
-    return reach(VEL[i][axis] if abs(direction) == 1 else 0, side, width, direction)
-
-
-def first_layer(field):
-    return field[2] if field[3] == 2 else 1
+def layers_x(field, i, side):
+    _, _, kind, width, _, direction = field
+    if kind == "stream":
+        return 1, reach(VEL[i][0], side, width, direction)
+    if kind == "strip":
+        return (reach(VEL[i][0], side, width, direction),) * 2
+    if kind == "next":
+        return width, width if VEL[i][0] == -side * direction else 0
+    return (width if kind == "ring" else 1), width
+
+
+def layers_y(field, i, side, plane):
+    _, _, kind, _, width, direction = field
+    if kind in ("stream", "strip"):
+        return 0, reach(VEL[i][1], side, width, direction)
+    if kind == "next":
+        return width - 1, width if VEL[i][1] == -side * direction else 0
+    return (width - 1 if kind == "ring" and -width < plane < NX + width - 1 else 0), width
+
+
+def strip_rows(field, i):
+    return {1: (NY - 2, NY - 1), 0: (0, NY - 1), -1: (0, 1)}[VEL[i][1] * field[5]]
 
 
 def plan_x(fields, side):
-    places = {}
+    places, strips, tile = {}, [], 0
     for field in fields:
-        for layer in range(first_layer(field), field[2] + 1):
+        for layer in range(1, NX):
             for i in range(field[1]):
-                if member_reach(field, i, 0, side) >= layer:
-                    places[field[0], i, layer] = len(places)
-    return places, len(places)
+                first, last = layers_x(field, i, side)
+                if not first <= layer <= last:
+                    continue
+                if field[2] == "strip":
+                    strips.append((field, i, layer))
+                else:
+                    places[field, i, layer] = tile, 0
+                    tile += 1
+    for n, key in enumerate(strips):
+        places[key] = tile + n // (NY // 2), n % (NY // 2) * 2
+    return places, tile - (-len(strips) // (NY // 2))
 
 
 def plan_y(fields, side):
     entries, start = [], 0
     for field in fields:
-        for plane in range(-field[2], NX + field[2]):
+        for plane in range(1 - NX, 2 * NX - 1):
             for i in range(field[1]):
-                if plane < 0 and member_reach(field, i, 0, -1) < -plane:
+                if plane < 0 or plane >= NX:
+                    first, last = layers_x(field, i, -1 if plane < 0 else 1)
+                    inner = field[2] == "ring" and -field[3] < plane < NX + field[3] - 1
+                    if not inner and not first <= (-plane if plane < 0 else plane - NX + 1) <= last:
+                        continue
+                elif field[2] in ("strip", "next"):
                     continue
-                if plane >= NX and member_reach(field, i, 0, 1) < plane - NX + 1:
-                    continue
-                rows = member_reach(field, i, 1, side)
-                skip = first_layer(field) - 1 if -field[2] < plane < NX + field[2] - 1 else 0
-                if rows > skip:
-                    entries.append((field[0], i, plane, start, skip, rows - skip))
-                    start += rows - skip
+                skip, last = layers_y(field, i, side, plane)
+                if last > skip:
+                    entries.append((field, i, plane, start, skip, last - skip))
+                    start += last - skip
     return entries, -(-start // 8) * 8
 
 
-FIRST = (("post", 27, 3, 1), ("adjoint", 27, 1, -1), ("cell", 2, 2, 0))
-SECOND = (("adjoint", 27, 3, -1), ("post", 27, 1, 1), ("speed", 4, 2, 2))
+FIRST = (
+    ("post", 27, "stream", 2, 3, 1), ("strip", 27, "strip", 3, 2, 1), ("next", 27, "next", 2, 2, 1),
+    ("adjoint", 27, "stream", 1, 1, -1), ("cell", 2, "plain", 2, 2, 0),
+)
+SECOND = (
+    ("adjoint", 27, "stream", 2, 3, -1), ("strip", 27, "strip", 3, 2, -1), ("next", 27, "next", 2, 2, -1),
+    ("post", 27, "stream", 1, 1, 1), ("speed", 4, "ring", 2, 2, 0),
+)
 PLAN_X = {(f, s): plan_x(f, s) for f in (FIRST, SECOND) for s in (-1, 1)}
 PLAN_Y = {(f, s): plan_y(f, s) for f in (FIRST, SECOND) for s in (-1, 1)}
 
 
 def pack_x(fields, side, read, out):
-    for (name, i, layer), place in PLAN_X[fields, side][0].items():
-        out[place] = read(name, i, layer - 1 if side > 0 else NX - layer)
-
-
-def halo_tile(fields, from_low, from_high, name, i, plane):
-    if plane < 0:
-        return from_low, PLAN_X[fields, -1][0][name, i, -plane]
-    return from_high, PLAN_X[fields, 1][0][name, i, plane - NX + 1]
+    for (field, i, layer), (tile, row) in PLAN_X[fields, side][0].items():
+        value = read(field[0], i, layer - 1 if side > 0 else NX - layer)
+        if field[2] == "strip":
+            low, high = strip_rows(field, i)
+            out[tile, row : row + 1] = value[low : low + 1]
+            out[tile, row + 1 : row + 2] = value[high : high + 1]
+        else:
+            out[tile] = value
+
+
+def halo_rows(fields, from_low, from_high, field, i, plane, first, rows):
+    ref, side, layer = (from_low, -1, -plane) if plane < 0 else (from_high, 1, plane - NX + 1)
+    tile, row = PLAN_X[fields, side][0][field, i, layer]
+    if field[2] == "strip":
+        first = strip_rows(field, i).index(first)
+    return ref[tile, row + first : row + first + rows]
 
 
 def pack_y(fields, side, own, from_low, from_high, out):
-    for name, i, plane, start, skip, rows in PLAN_Y[fields, side][0]:
+    for field, i, plane, start, skip, rows in PLAN_Y[fields, side][0]:
         first = skip if side > 0 else NY - skip - rows
-        if 0 <= plane < NX or (name == "speed" and -2 < plane < NX + 1):
-            out[start : start + rows] = own(name, i, plane, first, rows)
+        if 0 <= plane < NX or (field[2] == "ring" and -field[3] < plane < NX + field[3] - 1):
+            out[start : start + rows] = own(field[0], i, plane, first, rows)
         else:
-            ref, place = halo_tile(fields, from_low, from_high, name, i, plane)
-            out[start : start + rows] = ref[place, first : first + rows]
+            out[start : start + rows] = halo_rows(fields, from_low, from_high, field, i, plane, first, rows)
 
 
 def by_parity(axis, run, from_odd, from_even):
@@ -111,16 +147,20 @@
 
 def unpack_x(fields, wide, *from_x):
     for side, ref in zip((-1, 1), from_x):
-        for (name, i, layer), place in PLAN_X[fields, side][0].items():
-            plane = NX - 1 + layer if side > 0 else -layer
-            wide[name][i, plane + HALO, NY : 2 * NY] = ref[place]
+        for (field, i, layer), (tile, row) in PLAN_X[fields, side][0].items():
+            plane = (NX - 1 + layer if side > 0 else -layer) + HALO
+            if field[2] == "strip":
+                for n, at in enumerate(strip_rows(field, i)):
+                    wide[field[0]][i, plane, NY + at : NY + at + 1] = ref[tile, row + n : row + n + 1]
+            else:
+                wide[field[0]][i, plane, NY : 2 * NY] = ref[tile]
 
 
 def unpack_y(fields, wide, *from_y):
     for side, ref in zip((-1, 1), from_y):
-        for name, i, plane, start, skip, rows in PLAN_Y[fields, side][0]:
+        for field, i, plane, start, skip, rows in PLAN_Y[fields, side][0]:
             first = 2 * NY + skip if side > 0 else NY - skip - rows
-            wide[name][i, plane + HALO, first : first + rows] = ref[start : start + rows]
+            wide[field[0]][i, plane + HALO, first : first + rows] = ref[start : start + rows]
 
 
 def receive_x(fields, wide, odd_x, even_x):
@@ -272,8 +312,15 @@
     ref[place + (slice(NY, 2 * NY),)] = value
 
 
+def put_narrow_edge_rows(ref, place, value):
+    ref[place + (slice(NY - 1, NY + 1),)] = value[1:3]
+    ref[place + (slice(2 * NY - 1, 2 * NY + 1),)] = value[5:7]
+
+
 OWN = (own_rows, put_own_rows)
+OUTER = (HALO - 2, HALO + NX + 1)
 EDGE = (edge_rows, put_edge_rows)
+NARROW_EDGE = (edge_rows, put_narrow_edge_rows)
 
 
 def shifted(wide, shift):
@@ -292,11 +339,11 @@
     return tiles
 
 
-def planes_loop(first, last, load, work, store):
+def planes_loop(first, last, load, work, store, step=1):
     together = TOGETHER[last - first]
 
     def body(n, carry):
-        planes = [first + together * n + k for k in range(together)]
+        planes = [first + together * n + k * step for k in range(together)]
         loaded = [load(plane) for plane in planes]
         results = [work(*values) for values in loaded]
         for plane, result in zip(planes, results):
@@ -306,7 +353,15 @@
     lax.fori_loop(0, (last - first) // together, body, 0)
 
 
-def forward(where, source, target, cell, speed, rates, inlet, width):
+def put_inner(ahead, direction, load, work):
+    results = [work(*values) for values in [load(1), load(NX - 2)]]
+    for n, out in enumerate(results):
+        for i in range(27):
+            if VEL[i][0] == (direction if n else -direction):
+                ahead[n, i] = out[i]
+
+
+def forward(where, source, target, cell, speed, rates, inlet, outer=False):
     get, put = where
 
     def load(plane):
@@ -319,13 +374,17 @@
         out, values = result
         for i in range(27):
             put(target, (i, plane), out[i])
-        for i in range(5):
-            put(speed, (i, plane), values[i])
-
-    planes_loop(HALO - width, HALO + NX + width, load, work, store)
-
-
-def backward(where, source, target, cell, speed, gain, rates, width):
+        if not outer:
+            for i in range(5):
+                put(speed, (i, plane), values[i])
+
+    if outer:
+        planes_loop(OUTER[0], OUTER[0] + 2, load, work, store, OUTER[1] - OUTER[0])
+    else:
+        planes_loop(HALO - 1, HALO + NX + 1, load, work, store)
+
+
+def backward(where, source, target, cell, speed, gain, rates, outer=False):
     get, put = where
 
     def load(plane):
@@ -339,9 +398,13 @@
         out, grad = result
         for i in range(27):
             put(target, (i, plane), out[i])
-        put(gain, (plane,), grad)
-
-    planes_loop(HALO - width, HALO + NX + width, load, work, store)
+        if not outer:
+            put(gain, (plane,), grad)
+
+    if outer:
+        planes_loop(OUTER[0], OUTER[0] + 2, load, work, store, OUTER[1] - OUTER[0])
+    else:
+        planes_loop(HALO - 1, HALO + NX + 1, load, work, store)
 
 
 def inlet_speed(start, step):
@@ -359,7 +422,7 @@
 def first_kernel(
     rates_hbm, start_hbm, populations, cotangent, porosity, cell_type,
     post_hbm, cell_hbm, speed_hbm, to_odd_hbm, to_even_hbm,
-    rates, start, f, gamma, kinds, ends, post, cell, speed, to_odd, to_even, sems,
+    rates, start, f, gamma, kinds, ends, post, cell, speed, to_odd, to_even, ahead, sems,
 ):
     small = start_copies(
         sems, (rates_hbm, rates), (start_hbm, start), (porosity, gamma), (cell_type, kinds)
@@ -386,18 +449,26 @@
             results.append(collide([f[i, plane] for i in range(27)], kappa, kind, rates, inlet))
         for plane, (out, values) in zip(planes, results):
             for i in range(27):
-                post[i, plane] = out[i]
+                post[i, plane, NY : 2 * NY] = out[i]
             for i in range(5):
                 speed[i, plane] = values[i]
         part = slice(2 * n, 2 * n + 2)
-        done.append(start_copies(sems.at[4 + n : 5 + n], (post.at[:, part], post_hbm.at[:, part])))
+        done.append(start_copies(sems.at[4 + n : 5 + n], (post.at[:, part, NY : 2 * NY], post_hbm.at[:, part])))
     done.append(start_copies(sems, (cell, cell_hbm), (speed, speed_hbm)))
+    later = inlet_speed(start, 1)
+    put_inner(
+        ahead, 1,
+        lambda plane: (pulled(post, plane, own_rows, 1), cell[0, plane], cell[1, plane]),
+        lambda f, kappa, kind: collide(f, kappa, kind, rates, later)[0],
+    )
     tail()
 
     def read(name, i, plane):
         if name == "adjoint":
             return ends[0, i - 18] if plane == 0 else ends[1, i]
-        return {"post": post, "cell": cell}[name][i, plane]
+        if name == "next":
+            return ahead[plane - 1, i]
+        return cell[i, plane] if name == "cell" else post[i, plane, NY : 2 * NY]
 
     send_x(FIRST, read, to_odd, to_even)
     done.append(start_copies(sems.at[6:8], (to_odd, to_odd_hbm), (to_even, to_even_hbm)))
@@ -448,25 +519,27 @@
     put_block(post_zero, post, 27)
     put_block(wide_adjoint, cotangent, 27)
     put_block(wide_cell, cell, 2)
-    wide = {"post": post_zero, "adjoint": wide_adjoint, "cell": wide_cell}
+    wide = {"post": post_zero, "strip": post_zero, "next": post_one, "adjoint": wide_adjoint, "cell": wide_cell}
     receive_x(FIRST, wide, odd_x, even_x)
     wait()
-    forward(OWN, post_zero, post_one, wide_cell, speed_one, rates, inlet_speed(start, 1), 2)
-    forward(OWN, post_one, post_two, wide_cell, speed_two, rates, inlet_speed(start, 2), 1)
+    forward(OWN, post_zero, post_one, wide_cell, speed_one, rates, inlet_speed(start, 1))
+    forward(OWN, post_one, post_two, wide_cell, speed_two, rates, inlet_speed(start, 2))
 
 
 def third_late_kernel(
     rates_hbm, start_hbm, _0, _1, _2, _3, _4, _5, _6, odd_y, even_y,
     post_zero, post_one, post_two, wide_adjoint, wide_cell, speed_one, speed_two,
     last_post, adjoint, gain, to_odd, to_even,
-    rates, start, sems,
+    rates, start, inner, ahead, sems,
 ):
     wait = start_copies(sems, (rates_hbm, rates), (start_hbm, start))
-    wide = {"post": post_zero, "adjoint": wide_adjoint, "cell": wide_cell}
+    wide = {"post": post_zero, "strip": post_zero, "next": post_one, "adjoint": wide_adjoint, "cell": wide_cell}
     receive_y(FIRST, wide, odd_y, even_y)
     wait()
-    forward(EDGE, post_zero, post_one, wide_cell, speed_one, rates, inlet_speed(start, 1), 2)
-    forward(EDGE, post_one, post_two, wide_cell, speed_two, rates, inlet_speed(start, 2), 1)
+    inlet = inlet_speed(start, 1)
+    forward(NARROW_EDGE, post_zero, post_one, wide_cell, speed_one, rates, inlet, True)
+    forward(EDGE, post_zero, post_one, wide_cell, speed_one, rates, inlet)
+    forward(EDGE, post_one, post_two, wide_cell, speed_two, rates, inlet_speed(start, 2))
     inlet = inlet_speed(start, 3)
 
     def load(n):
@@ -485,14 +558,29 @@
         for i in range(27):
             last_post[i, n] = out[i]
             adjoint[i, n] = back[i]
+            inner[i, n, NY : 2 * NY] = back[i]
         gain[n] = grad
 
     planes_loop(0, NX, load, work, store)
+
+    def load_inner(n):
+        plane = n + HALO
+        values = [own_rows(speed_two, (i, plane)) for i in range(4)]
+        return (
+            pulled(inner, n, own_rows, -1), own_rows(wide_cell, (0, plane)), own_rows(wide_cell, (1, plane)), values
+        )
+
+    def work_inner(h, kappa, kind, values):
+        return collide_back(h, kappa, kind, rates, values)[0]
+
+    put_inner(ahead, -1, load_inner, work_inner)
 
     def read(name, i, plane):
         if name == "speed":
             return speed_two[i, plane + HALO, NY : 2 * NY]
-        return {"post": last_post, "adjoint": adjoint}[name][i, plane]
+        if name == "next":
+            return ahead[plane - 1, i]
+        return {"post": last_post, "adjoint": adjoint, "strip": adjoint}[name][i, plane]
 
     send_x(SECOND, read, to_odd, to_even)
 
@@ -514,11 +602,13 @@
     wait = start_copies(sems, (rates_hbm, rates))
     put_block(wide_post, post, 27)
     put_block(adjoint_three, adjoint, 27)
-    wide = {"post": wide_post, "adjoint": adjoint_three, "speed": speed_two}
+    wide = {
+        "post": wide_post, "adjoint": adjoint_three, "strip": adjoint_three, "next": adjoint_two, "speed": speed_two
+    }
     receive_x(SECOND, wide, odd_x, even_x)
     wait()
-    backward(OWN, adjoint_three, adjoint_two, wide_cell, speed_two, gain_two, rates, 2)
-    backward(OWN, adjoint_two, adjoint_one, wide_cell, speed_one, gain_one, rates, 1)
+    backward(OWN, adjoint_three, adjoint_two, wide_cell, speed_two, gain_two, rates)
+    backward(OWN, adjoint_two, adjoint_one, wide_cell, speed_one, gain_one, rates)
 
 
 def fifth_late_kernel(
@@ -528,7 +618,9 @@
     rates, flow_here, adjoint_here, sensitivity_here, sems,
 ):
     wait = start_copies(sems, (rates_hbm, rates))
-    wide = {"post": wide_post, "adjoint": adjoint_three, "speed": speed_two}
+    wide = {
+        "post": wide_post, "adjoint": adjoint_three, "strip": adjoint_three, "next": adjoint_two, "speed": speed_two
+    }
     receive_y(SECOND, wide, odd_y, even_y)
 
     def run(n, carry):
@@ -540,8 +632,9 @@
     lax.fori_loop(0, NX, run, 0)
     wait()
     wait = start_copies(sems, (flow_here, flow))
-    backward(EDGE, adjoint_three, adjoint_two, wide_cell, speed_two, gain_two, rates, 2)
-    backward(EDGE, adjoint_two, adjoint_one, wide_cell, speed_one, gain_one, rates, 1)
+    backward(NARROW_EDGE, adjoint_three, adjoint_two, wide_cell, speed_two, gain_two, rates, True)
+    backward(EDGE, adjoint_three, adjoint_two, wide_cell, speed_two, gain_two, rates)
+    backward(EDGE, adjoint_two, adjoint_one, wide_cell, speed_one, gain_one, rates)
 
     def load(n):
         plane = n + HALO
@@ -609,6 +702,7 @@
 def body(populations, cotangent, porosity, cell_type, rates, start_step):
     block = (27, NX, NY, LANES)
     wide = (27, PLANES, ROWS, LANES)
+    inner, ahead = (27, NX, ROWS, LANES), (2, 27, NY, LANES)
     tiles = (PLAN_X[FIRST, 1][1], NY, LANES), (PLAN_X[FIRST, -1][1], NY, LANES)
     rows = (PLAN_Y[FIRST, 1][1], LANES), (PLAN_Y[FIRST, -1][1], LANES)
     rates_here, start_here = pltpu.SMEM((27,), jnp.float32), pltpu.SMEM((1,), jnp.int32)
@@ -617,7 +711,7 @@
         (block, (2, NX, NY, LANES), (5, NX, NY, LANES)) + tiles,
         (
             rates_here, start_here, block, (NX, NY, LANES), pltpu.VMEM((NX, NY, LANES), jnp.int32),
-            (2, 9, NY, LANES), block, (2, NX, NY, LANES), (5, NX, NY, LANES), *tiles,
+            (2, 9, NY, LANES), inner, (2, NX, NY, LANES), (5, NX, NY, LANES), *tiles, ahead,
             pltpu.SemaphoreType.DMA((8,)),
         ),
         FIRST_LIMIT,
@@ -641,7 +735,7 @@
     *wides, post, adjoint, gain, to_odd, to_even = call(
         third_late_kernel, (rates, start_step), tuple(wides) + y_halos,
         tuple(a.shape for a in wides) + (block, block, (NX, NY, LANES)) + tiles,
-        scalars, aliases={2 + n: n for n in range(len(wides))},
+        scalars[:2] + (inner, ahead) + scalars[2:], aliases={2 + n: n for n in range(len(wides))},
     )
     wide_cell, speed_one, speed_two = wides[4:]
     x_halos = exchange_x(to_odd, to_even)

time: 82 us -> 76.6 us (0.934)
  starting transfers between devices: 36 us -> 32.9 us
  waiting for transfers between devices: 23.9 us -> 21.7 us
    ppermute x6, starting transfers between devices: 36 us -> 32.9 us  [swap(): lax.ppermute(value, axis, [(a, b) for a, b in pairs] + [(b, a) for a, b i...]
    ppermute x6, waiting for transfers between devices: 23.9 us -> 21.7 us  [swap(): lax.ppermute(value, axis, [(a, b) for a, b in pairs] + [(b, a) for a, b i...]
    unnamed x12 -> x14, local copies, waits for them, and re-layouts: 3.44 us -> 3.44 us
  transfers between devices with their start and end apart: 6 -> 6, of which waited for: 4 -> 5; matrix products, arithmetic and copies ran while one was open for 0% -> 0% of each run, Pallas kernels for 5% -> 5%
where the time goes in v7:
time: 76.6 us; the launch traced here: 76.1 us
  starting transfers between devices  32.9 us (43%)
  waiting for transfers between devices  21.7 us (28%)
  Pallas kernels  12.4 us (16%)
  blocking collectives  4.3 us (6%)
  local copies, waits for them, and re-layouts  3.44 us (4%)
  between operations  1.43 us (2%)
    ppermute x6, starting transfers between devices, swap(): lax.ppermute(value, axis, [(a, b) for a, b in pairs] + [(b, a) for a, b i...  32.9 us
    ppermute x6, waiting for transfers between devices, swap(): lax.ppermute(value, axis, [(a, b) for a, b in pairs] + [(b, a) for a, b i...  21.7 us
    pallas_call x8, Pallas kernels, call(): pl.pallas_call(kernel, out_shape=tuple((f32(*s) for s in outs)), in_specs...  12.4 us
    all_gather x2, blocking collectives, exchange_y(): lax.all_gather(to_even, 'gy', axis_index_groups=partners('gy', 0))  4.3 us
    unnamed x14, local copies, waits for them, and re-layouts  3.44 us
  transfers between devices with their start and end apart: 6, of which 5 were waited for; matrix products, arithmetic and copies ran while one was open for 0% of the time, Pallas kernels for 5%

profile of v7, /device:TPU:6, one launch (start us, length us, event | category | flops | bytes accessed | tf_op | source)
XLA Modules:
  0.0 76.1 jit_solution(4832635598534161195)
XLA Ops:
  1.3 2.4 %first_kernel.1 = (f32[27,4,8,128]{3,2,1,0:T(8,128)}, f32[2,4,8,128]{3,2,1,0:T(8,128)}, f32[5,4,8,128]{3,2,1,0:T(8,128)}, f32[56,8,128]{2,1,0:T(8,128)}, f32[56,8,128]{2,1,0:T(8,128)}) custom-call(f32[27]{0:T(128)} %rates_hbm.9, s32[1]{0:T(128)S(6)} %copy.39.start_hbm, f32[27,4,8,128]{3,2,1,0:T(8,128)} %populations.1, f32[27,4,8,128]{3,2,1,0:T(8,128)} %refs_1_.1, ...), custom_call_target="tpu_custom_call" | custom-call | tf_op jit(solution)/shard_map/first_kernel/pallas_call | solution.py:671
  3.6 13.8 %collective-permute-start = (f32[56,8,128]{2,1,0:T(8,128)}, f32[56,8,128]{2,1,0:T(8,128)S(1)}, u32[]{:S(2)}, u32[]{:S(2)}) collective-permute-start(f32[56,8,128]{2,1,0:T(8,128)} %get-tuple-element.45), channel_id=1, source_target_pairs={{32,64},{96,128},{160,192},{224,256},{288,320},{352,384},{416,448}... | collective-permute-start | bytes 688136 | tf_op jit(solution)/shard_map/ppermute | solution.py:690
  17.5 1.9 %collective-permute-start.1 = (f32[56,8,128]{2,1,0:T(8,128)}, f32[56,8,128]{2,1,0:T(8,128)S(1)}, u32[]{:S(2)}, u32[]{:S(2)}) collective-permute-start(f32[56,8,128]{2,1,0:T(8,128)} %get-tuple-element.46), channel_id=1, source_target_pairs={{0,32},{64,96},{128,160},{192,224},{256,288},{320,352},{384,416},{... | collective-permute-start | bytes 688136 | tf_op jit(solution)/shard_map/ppermute | solution.py:690
  19.4 0.0 copy-start
  19.4 1.0 %copy-done = f32[27,4,8,128]{3,2,1,0:T(8,128)S(1)} copy-done((f32[27,4,8,128]{3,2,1,0:T(8,128)S(1)}, f32[27,4,8,128]{3,2,1,0:T(8,128)}, u32[]{:S(2)}) %copy-start) | copy-done | bytes 442392
  20.4 0.0 copy-start.1
  20.4 1.0 %copy-done.1 = f32[27,4,8,128]{3,2,1,0:T(8,128)S(1)} copy-done((f32[27,4,8,128]{3,2,1,0:T(8,128)S(1)}, f32[27,4,8,128]{3,2,1,0:T(8,128)}, u32[]{:S(2)}) %copy-start.1) | copy-done | bytes 442392
  21.4 0.0 copy-start.4
  21.4 0.8 copy-done.4
  22.2 0.6 holding_kernel.1
  22.8 5.4 %collective-permute-done.odd_x = f32[56,8,128]{2,1,0:T(8,128)S(1)} collective-permute-done((f32[56,8,128]{2,1,0:T(8,128)}, f32[56,8,128]{2,1,0:T(8,128)S(1)}, u32[]{:S(2)}, u32[]{:S(2)}) %collective-permute-start) | collective-permute-done | bytes 229408 | tf_op jit(solution)/shard_map/ppermute | solution.py:690
  28.1 0.0 collective-permute-done.1.even_x
  28.1 0.2 second_kernel.1
  28.3 2.7 %collective-permute-start.2 = (f32[464,128]{1,0:T(8,128)S(1)}, f32[464,128]{1,0:T(8,128)S(1)}, u32[]{:S(2)}, u32[]{:S(2)}) collective-permute-start(f32[464,128]{1,0:T(8,128)S(1)} %get-tuple-element.54), channel_id=1, source_target_pairs={{1,2},{3,4},{5,6},{7,8},{9,10},{11,12},{13,14},{15,16},{17,18},{19... | collective-permute-start | bytes 712712 | tf_op jit(solution)/shard_map/ppermute | solution.py:690
  31.0 0.0 copy-start.5
  31.0 0.6 copy-done.5
  31.7 1.7 %third_early_kernel.1 = (f32[27,10,24,128]{3,2,1,0:T(8,128)S(1)}, f32[27,10,24,128]{3,2,1,0:T(8,128)S(1)}, f32[27,10,24,128]{3,2,1,0:T(8,128)S(1)}, f32[27,10,24...) custom-call(f32[27]{0:T(128)S(1)} %copy-done.5, ...), custom_call_target="tpu_custom_call" | custom-call | tf_op jit(solution)/shard_map/third_early_kernel/pallas_call | solution.py:671
  33.4 2.1 %all-gather = f32[928,128]{1,0:T(8,128)S(1)} all-gather(f32[464,128]{1,0:T(8,128)S(1)} %get-tuple-element.55), channel_id=2, replica_groups={{0,1},{2,3},{4,5},{6,7},{8,9},{10,11},{12,13},{14,15},{16,17},{18,19},{..., dimensions={0}, use_global_device_ids=true | all-gather | bytes 712704 | tf_op jit(solution)/shard_map/all_gather | solution.py:699
  35.6 4.5 %collective-permute-done.2.odd_y = f32[464,128]{1,0:T(8,128)S(1)} collective-permute-done((f32[464,128]{1,0:T(8,128)S(1)}, f32[464,128]{1,0:T(8,128)S(1)}, u32[]{:S(2)}, u32[]{:S(2)}) %collective-permute-start.2) | collective-permute-done | bytes 237600 | tf_op jit(solution)/shard_map/ppermute | solution.py:690
  40.1 0.0 copy-start.6
  40.1 2.7 %third_late_kernel.1 = (f32[27,10,24,128]{3,2,1,0:T(8,128)S(1)}, f32[27,10,24,128]{3,2,1,0:T(8,128)S(1)}, f32[27,10,24,128]{3,2,1,0:T(8,128)S(1)}, f32[27,10,24,...) custom-call(f32[27]{0:T(128)S(1)} %copy-done.5, ...), custom_call_target="tpu_custom_call", output_to_operand_aliasing={{0}: (2, {}), {1}: (3, {}), {2}: (4, {}), {3}: (5, {}), {4}... | custom-call | tf_op jit(solution)/shard_map/third_late_kernel/pallas_call | solution.py:671
  42.9 0.0 copy-start.2
  42.9 0.0 copy-start.3
  42.9 9.4 %collective-permute-start.3 = (f32[56,8,128]{2,1,0:T(8,128)S(1)}, f32[56,8,128]{2,1,0:T(8,128)S(1)}, u32[]{:S(2)}, u32[]{:S(2)}) collective-permute-start(f32[56,8,128]{2,1,0:T(8,128)S(1)} %get-tuple-element.63), channel_id=1, source_target_pairs={{32,64},{96,128},{160,192},{224,256},{288,320},{352,384},{416,448}... | collective-permute-start | bytes 688136 | tf_op jit(solution)/shard_map/ppermute | solution.py:690
  52.3 1.9 %collective-permute-start.4 = (f32[56,8,128]{2,1,0:T(8,128)S(1)}, f32[56,8,128]{2,1,0:T(8,128)S(1)}, u32[]{:S(2)}, u32[]{:S(2)}) collective-permute-start(f32[56,8,128]{2,1,0:T(8,128)S(1)} %get-tuple-element.64), channel_id=1, source_target_pairs={{0,32},{64,96},{128,160},{192,224},{256,288},{320,352},{384,416},{... | collective-permute-start | bytes 688136 | tf_op jit(solution)/shard_map/ppermute | solution.py:690
  54.2 5.2 %collective-permute-done.3.odd_x = f32[56,8,128]{2,1,0:T(8,128)S(1)} collective-permute-done((f32[56,8,128]{2,1,0:T(8,128)S(1)}, f32[56,8,128]{2,1,0:T(8,128)S(1)}, u32[]{:S(2)}, u32[]{:S(2)}) %collective-permute-start.3) | collective-permute-done | bytes 229408 | tf_op jit(solution)/shard_map/ppermute | solution.py:690
  59.4 0.8 %collective-permute-done.4.even_x = f32[56,8,128]{2,1,0:T(8,128)S(1)} collective-permute-done((f32[56,8,128]{2,1,0:T(8,128)S(1)}, f32[56,8,128]{2,1,0:T(8,128)S(1)}, u32[]{:S(2)}, u32[]{:S(2)}) %collective-permute-start.4) | collective-permute-done | bytes 229408 | tf_op jit(solution)/shard_map/ppermute | solution.py:690
  60.2 0.2 fourth_kernel.1
  60.4 3.1 %collective-permute-start.5 = (f32[472,128]{1,0:T(8,128)S(1)}, f32[472,128]{1,0:T(8,128)S(1)}, u32[]{:S(2)}, u32[]{:S(2)}) collective-permute-start(f32[472,128]{1,0:T(8,128)S(1)} %get-tuple-element.65), channel_id=1, source_target_pairs={{1,2},{3,4},{5,6},{7,8},{9,10},{11,12},{13,14},{15,16},{17,18},{19... | collective-permute-start | bytes 725000 | tf_op jit(solution)/shard_map/ppermute | solution.py:690
  63.6 0.0 copy-done.6
  63.6 1.6 %fifth_early_kernel.1 = (f32[5,10,24,128]{3,2,1,0:T(8,128)S(1)}, f32[27,10,24,128]{3,2,1,0:T(8,128)S(1)}, f32[27,10,24,128]{3,2,1,0:T(8,128)S(1)}, f32[27,10,24,...) custom-call(f32[27]{0:T(128)S(1)} %copy-done.6, ...), custom_call_target="tpu_custom_call", output_to_operand_aliasing={{0}: (5, {})} | custom-call | tf_op jit(solution)/shard_map/fifth_early_kernel/pallas_call | solution.py:671
  65.2 2.2 %all-gather.1 = f32[944,128]{1,0:T(8,128)S(1)} all-gather(f32[472,128]{1,0:T(8,128)S(1)} %get-tuple-element.66), channel_id=3, replica_groups={{0,1},{2,3},{4,5},{6,7},{8,9},{10,11},{12,13},{14,15},{16,17},{18,19},{..., dimensions={0}, use_global_device_ids=true | all-gather | bytes 724992 | tf_op jit(solution)/shard_map/all_gather | solution.py:699
  67.3 5.8 %collective-permute-done.5.odd_y = f32[472,128]{1,0:T(8,128)S(1)} collective-permute-done((f32[472,128]{1,0:T(8,128)S(1)}, f32[472,128]{1,0:T(8,128)S(1)}, u32[]{:S(2)}, u32[]{:S(2)}) %collective-permute-start.5) | collective-permute-done | bytes 241696 | tf_op jit(solution)/shard_map/ppermute | solution.py:690
  73.1 0.0 copy-done.2
  73.1 0.0 copy-done.3
  73.1 3.0 %fifth_late_kernel.1 = (f32[27,4,8,128]{3,2,1,0:T(8,128)}, f32[27,4,8,128]{3,2,1,0:T(8,128)}, f32[4,8,128]{2,1,0:T(8,128)}, f32[5,10,24,128]{3,2,1,0:T(8,128)S(1...) custom-call(f32[27]{0:T(128)S(1)} %copy-done.6, ...), custom_call_target="tpu_custom_call", output_to_operand_aliasing={{3}: (8, {}), {4}: (9, {}), {5}: (10, {}), {6}: (11, {}), {... | custom-call | tf_op jit(solution)/shard_map/fifth_late_kernel/pallas_call | solution.py:671
Async XLA Ops:
  3.6 24.5 %collective-permute-start = (f32[56,8,128]{2,1,0:T(8,128)}, f32[56,8,128]{2,1,0:T(8,128)S(1)}, u32[]{:S(2)}, u32[]{:S(2)}) collective-permute-start(f32[56,8,128]{2,1,0:T(8,128)} %get-tuple-element.45), channel_id=1, source_target_pairs={{32,64},{96,128},{160,192},{224,256},{288,320},{352,384},{416,448}... | collective-permute-start | bytes 688136 | tf_op jit(solution)/shard_map/ppermute | solution.py:690
  17.5 10.7 %collective-permute-start.1 = (f32[56,8,128]{2,1,0:T(8,128)}, f32[56,8,128]{2,1,0:T(8,128)S(1)}, u32[]{:S(2)}, u32[]{:S(2)}) collective-permute-start(f32[56,8,128]{2,1,0:T(8,128)} %get-tuple-element.46), channel_id=1, source_target_pairs={{0,32},{64,96},{128,160},{192,224},{256,288},{320,352},{384,416},{... | collective-permute-start | bytes 688136 | tf_op jit(solution)/shard_map/ppermute | solution.py:690
  19.4 1.0 %copy-start = (f32[27,4,8,128]{3,2,1,0:T(8,128)S(1)}, f32[27,4,8,128]{3,2,1,0:T(8,128)}, u32[]{:S(2)}) copy-start(f32[27,4,8,128]{3,2,1,0:T(8,128)} %refs_1_.1) | copy-start | bytes 1327108
  20.4 1.0 %copy-start.1 = (f32[27,4,8,128]{3,2,1,0:T(8,128)S(1)}, f32[27,4,8,128]{3,2,1,0:T(8,128)}, u32[]{:S(2)}) copy-start(f32[27,4,8,128]{3,2,1,0:T(8,128)} %get-tuple-element.40.refs_0_) | copy-start | bytes 1327108
  21.4 0.8 copy-start.4
  28.3 11.8 %collective-permute-start.2 = (f32[464,128]{1,0:T(8,128)S(1)}, f32[464,128]{1,0:T(8,128)S(1)}, u32[]{:S(2)}, u32[]{:S(2)}) collective-permute-start(f32[464,128]{1,0:T(8,128)S(1)} %get-tuple-element.54), channel_id=1, source_target_pairs={{1,2},{3,4},{5,6},{7,8},{9,10},{11,12},{13,14},{15,16},{17,18},{19... | collective-permute-start | bytes 712712 | tf_op jit(solution)/shard_map/ppermute | solution.py:690
  31.0 0.7 copy-start.5
  40.1 23.5 %copy-start.6 = (f32[27]{0:T(128)S(1)}, f32[27]{0:T(128)}, u32[]{:S(2)}) copy-start(f32[27]{0:T(128)} %rates_hbm.9) | copy-start | bytes 328
  42.9 30.3 %copy-start.2 = (f32[5,4,8,128]{3,2,1,0:T(8,128)S(1)}, f32[5,4,8,128]{3,2,1,0:T(8,128)}, u32[]{:S(2)}) copy-start(f32[5,4,8,128]{3,2,1,0:T(8,128)} %get-tuple-element.57.speed_zero) | copy-start | bytes 245764
  42.9 30.3 %copy-start.3 = (f32[4,8,128]{2,1,0:T(8,128)S(1)}, f32[4,8,128]{2,1,0:T(8,128)}, u32[]{:S(2)}) copy-start(f32[4,8,128]{2,1,0:T(8,128)} %porosity.3) | copy-start | bytes 49156
  42.9 16.6 %collective-permute-start.3 = (f32[56,8,128]{2,1,0:T(8,128)S(1)}, f32[56,8,128]{2,1,0:T(8,128)S(1)}, u32[]{:S(2)}, u32[]{:S(2)}) collective-permute-start(f32[56,8,128]{2,1,0:T(8,128)S(1)} %get-tuple-element.63), channel_id=1, source_target_pairs={{32,64},{96,128},{160,192},{224,256},{288,320},{352,384},{416,448}... | collective-permute-start | bytes 688136 | tf_op jit(solution)/shard_map/ppermute | solution.py:690
  52.3 7.9 %collective-permute-start.4 = (f32[56,8,128]{2,1,0:T(8,128)S(1)}, f32[56,8,128]{2,1,0:T(8,128)S(1)}, u32[]{:S(2)}, u32[]{:S(2)}) collective-permute-start(f32[56,8,128]{2,1,0:T(8,128)S(1)} %get-tuple-element.64), channel_id=1, source_target_pairs={{0,32},{64,96},{128,160},{192,224},{256,288},{320,352},{384,416},{... | collective-permute-start | bytes 688136 | tf_op jit(solution)/shard_map/ppermute | solution.py:690
  60.4 12.7 %collective-permute-start.5 = (f32[472,128]{1,0:T(8,128)S(1)}, f32[472,128]{1,0:T(8,128)S(1)}, u32[]{:S(2)}, u32[]{:S(2)}) collective-permute-start(f32[472,128]{1,0:T(8,128)S(1)} %get-tuple-element.65), channel_id=1, source_target_pairs={{1,2},{3,4},{5,6},{7,8},{9,10},{11,12},{13,14},{15,16},{17,18},{19... | collective-permute-start | bytes 725000 | tf_op jit(solution)/shard_map/ppermute | solution.py:690

commit v8 on v7

--- a/solution.py
+++ b/solution.py
@@ -13,7 +13,6 @@
 
 NX, NY, LANES = 4, 8, 128
 HALO = 3
-TOGETHER = {6: 3, 4: 4, 2: 2}
 PLANES = NX + 2 * HALO
 ROWS = 3 * NY
 VMEM_LIMIT = 16 * 1024 * 1024
@@ -40,7 +39,7 @@
         return (reach(VEL[i][0], side, width, direction),) * 2
     if kind == "next":
         return width, width if VEL[i][0] == -side * direction else 0
-    return (width if kind == "ring" else 1), width
+    return (width if kind == "corner" else 1), 0 if kind == "ring" else width
 
 
 def layers_y(field, i, side, plane):
@@ -49,7 +48,7 @@
         return 0, reach(VEL[i][1], side, width, direction)
     if kind == "next":
         return width - 1, width if VEL[i][1] == -side * direction else 0
-    return (width - 1 if kind == "ring" and -width < plane < NX + width - 1 else 0), width
+    return (width - 1 if kind == "ring" else 0), width
 
 
 def strip_rows(field, i):
@@ -64,7 +63,7 @@
                 first, last = layers_x(field, i, side)
                 if not first <= layer <= last:
                     continue
-                if field[2] == "strip":
+                if field[2] in ("strip", "corner"):
                     strips.append((field, i, layer))
                 else:
                     places[field, i, layer] = tile, 0
@@ -84,7 +83,7 @@
                     inner = field[2] == "ring" and -field[3] < plane < NX + field[3] - 1
                     if not inner and not first <= (-plane if plane < 0 else plane - NX + 1) <= last:
                         continue
-                elif field[2] in ("strip", "next"):
+                elif field[2] in ("strip", "next", "corner"):
                     continue
                 skip, last = layers_y(field, i, side, plane)
                 if last > skip:
@@ -95,11 +94,11 @@
 
 FIRST = (
     ("post", 27, "stream", 2, 3, 1), ("strip", 27, "strip", 3, 2, 1), ("next", 27, "next", 2, 2, 1),
-    ("adjoint", 27, "stream", 1, 1, -1), ("cell", 2, "plain", 2, 2, 0),
+    ("adjoint", 27, "stream", 1, 1, -1), ("cell", 2, "plain", 1, 2, 0), ("corner", 2, "corner", 2, 1, 0),
 )
 SECOND = (
     ("adjoint", 27, "stream", 2, 3, -1), ("strip", 27, "strip", 3, 2, -1), ("next", 27, "next", 2, 2, -1),
-    ("post", 27, "stream", 1, 1, 1), ("speed", 4, "ring", 2, 2, 0),
+    ("post", 27, "stream", 1, 1, 1), ("speed", 4, "ring", 2, 2, 0), ("corner", 4, "corner", 2, 1, 0),
 )
 PLAN_X = {(f, s): plan_x(f, s) for f in (FIRST, SECOND) for s in (-1, 1)}
 PLAN_Y = {(f, s): plan_y(f, s) for f in (FIRST, SECOND) for s in (-1, 1)}
@@ -108,7 +107,7 @@
 def pack_x(fields, side, read, out):
     for (field, i, layer), (tile, row) in PLAN_X[fields, side][0].items():
         value = read(field[0], i, layer - 1 if side > 0 else NX - layer)
-        if field[2] == "strip":
+        if field[2] in ("strip", "corner"):
             low, high = strip_rows(field, i)
             out[tile, row : row + 1] = value[low : low + 1]
             out[tile, row + 1 : row + 2] = value[high : high + 1]
@@ -119,7 +118,7 @@
 def halo_rows(fields, from_low, from_high, field, i, plane, first, rows):
     ref, side, layer = (from_low, -1, -plane) if plane < 0 else (from_high, 1, plane - NX + 1)
     tile, row = PLAN_X[fields, side][0][field, i, layer]
-    if field[2] == "strip":
+    if field[2] in ("strip", "corner"):
         first = strip_rows(field, i).index(first)
     return ref[tile, row + first : row + first + rows]
 
@@ -149,27 +148,34 @@
     for side, ref in zip((-1, 1), from_x):
         for (field, i, layer), (tile, row) in PLAN_X[fields, side][0].items():
             plane = (NX - 1 + layer if side > 0 else -layer) + HALO
-            if field[2] == "strip":
+            if field[2] in ("strip", "corner"):
                 for n, at in enumerate(strip_rows(field, i)):
                     wide[field[0]][i, plane, NY + at : NY + at + 1] = ref[tile, row + n : row + n + 1]
             else:
                 wide[field[0]][i, plane, NY : 2 * NY] = ref[tile]
 
 
-def unpack_y(fields, wide, *from_y):
-    for side, ref in zip((-1, 1), from_y):
-        for field, i, plane, start, skip, rows in PLAN_Y[fields, side][0]:
-            first = 2 * NY + skip if side > 0 else NY - skip - rows
-            wide[field[0]][i, plane + HALO, first : first + rows] = ref[start : start + rows]
+def unpack_y(fields, wide, side, ref):
+    for field, i, plane, start, skip, rows in PLAN_Y[fields, side][0]:
+        first = 2 * NY + skip if side > 0 else NY - skip - rows
+        wide[field[0]][i, plane + HALO, first : first + rows] = ref[start : start + rows]
 
 
 def receive_x(fields, wide, odd_x, even_x):
     by_parity("gx", lambda low, high: unpack_x(fields, wide, low, high), odd_x, even_x)
 
 
-def receive_y(fields, wide, odd_y, even_y):
-    partner = even_y.at[1 - lax.axis_index("gy") % 2]
-    by_parity("gy", lambda low, high: unpack_y(fields, wide, low, high), odd_y, partner)
+def receive_y(fields, wide, from_partner, even):
+    parity = lax.axis_index("gy") % 2
+    ref = from_partner.at[1 - parity] if even else from_partner
+
+    @pl.when(parity == 0)
+    def _():
+        unpack_y(fields, wide, 1 if even else -1, ref)
+
+    @pl.when(parity == 1)
+    def _():
+        unpack_y(fields, wide, -1 if even else 1, ref)
 
 
 def send_x(fields, read, to_odd, to_even):
@@ -294,63 +300,73 @@
     return value if shift == 0 else pltpu.roll(value, shift % LANES, axis=1)
 
 
-def own_rows(ref, place):
-    return ref[place + (slice(NY, 2 * NY),)]
-
-
-def edge_rows(ref, place):
-    low, high = ref[place + (slice(NY - 2, 2 * NY - 2),)], ref[place + (slice(NY + 2, 2 * NY + 2),)]
-    return jnp.where(lax.broadcasted_iota(jnp.int32, (NY, LANES), 0) < NY // 2, low, high)
-
-
-def put_edge_rows(ref, place, value):
-    ref[place + (slice(NY - 2, NY + 2),)] = value[: NY // 2]
-    ref[place + (slice(2 * NY - 2, 2 * NY + 2),)] = value[NY // 2 :]
-
-
-def put_own_rows(ref, place, value):
-    ref[place + (slice(NY, 2 * NY),)] = value
-
-
-def put_narrow_edge_rows(ref, place, value):
-    ref[place + (slice(NY - 1, NY + 1),)] = value[1:3]
-    ref[place + (slice(2 * NY - 1, 2 * NY + 1),)] = value[5:7]
-
-
-OWN = (own_rows, put_own_rows)
-OUTER = (HALO - 2, HALO + NX + 1)
-EDGE = (edge_rows, put_edge_rows)
-NARROW_EDGE = (edge_rows, put_narrow_edge_rows)
-
-
-def shifted(wide, shift):
-    class View:
-        def __getitem__(self, place):
-            return wide[place[:-1] + (slice(place[-1].start + shift, place[-1].stop + shift),)]
-
-    return View()
+class Own:
+    items = tuple(range(HALO - 1, HALO + NX + 1))
+
+    def get(self, ref, place, shift=0):
+        return ref[place + (slice(NY + shift, 2 * NY + shift),)]
+
+    def put(self, ref, place, value, halves=(True, True)):
+        ref[place + (slice(NY, 2 * NY),)] = value
+
+
+class Edge:
+    items = tuple((plane, plane + 1) for plane in range(HALO - 1, HALO + NX + 1, 2))
+
+    def __init__(self, high, narrow=False):
+        self.first = NY - 2 + NY * high
+        self.skip = 1 if narrow else 0
+        if narrow:
+            self.items = ((HALO - 2, HALO + NX + 1),)
+
+    def get(self, ref, place, shift=0):
+        upper, lower = (
+            ref[place[:-1] + (plane, pl.ds(self.first + shift - half * (NY // 2), NY))]
+            for half, plane in enumerate(place[-1])
+        )
+        return jnp.where(lax.broadcasted_iota(jnp.int32, (NY, LANES), 0) < NY // 2, upper, lower)
+
+    def put(self, ref, place, value, halves=(True, True)):
+        rows = NY // 2 - 2 * self.skip
+        for half, plane in enumerate(place[-1]):
+            if halves[half]:
+                start = half * (NY // 2) + self.skip
+                ref[place[:-1] + (plane, pl.ds(self.first + self.skip, rows))] = value[start : start + rows]
+
+
+OWN = Own()
+
+
+def edges(even):
+    parity = lax.axis_index("gy") % 2
+    high = 1 - parity if even else parity
+    return Edge(high), Edge(high, True)
 
 
 def pulled(wide, plane, rows, direction):
     tiles = []
     for i, (cx, cy, cz) in enumerate(VEL):
-        tile = rows(shifted(wide, -direction * cy), (i, plane - direction * cx))
-        tiles.append(turned(tile, direction * cz))
+        moved = (
+            tuple(p - direction * cx for p in plane) if isinstance(plane, tuple) else plane - direction * cx
+        )
+        tiles.append(turned(rows.get(wide, (i, moved), -direction * cy), direction * cz))
     return tiles
 
 
-def planes_loop(first, last, load, work, store, step=1):
-    together = TOGETHER[last - first]
+def planes_loop(items, load, work, store):
+    together = 3 if len(items) == 6 else len(items)
 
     def body(n, carry):
-        planes = [first + together * n + k * step for k in range(together)]
-        loaded = [load(plane) for plane in planes]
-        results = [work(*values) for values in loaded]
+        planes = items if together == len(items) else [items[0] + together * n + k for k in range(together)]
+        results = [work(*values) for values in [load(plane) for plane in planes]]
         for plane, result in zip(planes, results):
             store(plane, result)
         return carry
 
-    lax.fori_loop(0, (last - first) // together, body, 0)
+    if together == len(items):
+        body(0, 0)
+    else:
+        lax.fori_loop(0, len(items) // together, body, 0)
 
 
 def put_inner(ahead, direction, load, work):
@@ -361,50 +377,45 @@
                 ahead[n, i] = out[i]
 
 
-def forward(where, source, target, cell, speed, rates, inlet, outer=False):
-    get, put = where
-
+def put_all(rows, target, plane, out, direction, outer):
+    for i in range(27):
+        halves = (VEL[i][0] == direction, VEL[i][0] == -direction) if outer else (True, True)
+        rows.put(target, (i, plane), out[i], halves)
+
+
+def forward(rows, source, target, cell, speed, rates, inlet, outer=False):
     def load(plane):
-        return pulled(source, plane, get, 1), get(cell, (0, plane)), get(cell, (1, plane))
+        return pulled(source, plane, rows, 1), rows.get(cell, (0, plane)), rows.get(cell, (1, plane))
 
     def work(f, kappa, kind):
         return collide(f, kappa, kind, rates, inlet)
 
     def store(plane, result):
         out, values = result
-        for i in range(27):
-            put(target, (i, plane), out[i])
+        put_all(rows, target, plane, out, 1, outer)
         if not outer:
             for i in range(5):
-                put(speed, (i, plane), values[i])
-
-    if outer:
-        planes_loop(OUTER[0], OUTER[0] + 2, load, work, store, OUTER[1] - OUTER[0])
-    else:
-        planes_loop(HALO - 1, HALO + NX + 1, load, work, store)
-
-
-def backward(where, source, target, cell, speed, gain, rates, outer=False):
-    get, put = where
-
+                rows.put(speed, (i, plane), values[i])
+
+    planes_loop(rows.items, load, work, store)
+
+
+def backward(rows, source, target, cell, speed, gain, rates, outer=False):
     def load(plane):
-        values = [get(speed, (i, plane)) for i in range(5)]
-        return pulled(source, plane, get, -1), get(cell, (0, plane)), get(cell, (1, plane)), values
+        values = [rows.get(speed, (i, plane)) for i in range(5)]
+        h = pulled(source, plane, rows, -1)
+        return h, rows.get(cell, (0, plane)), rows.get(cell, (1, plane)), values
 
     def work(h, kappa, kind, values):
         return collide_back(h, kappa, kind, rates, values[:4], values[4])
 
     def store(plane, result):
         out, grad = result
-        for i in range(27):
-            put(target, (i, plane), out[i])
+        put_all(rows, target, plane, out, -1, outer)
         if not outer:
-            put(gain, (plane,), grad)
-
-    if outer:
-        planes_loop(OUTER[0], OUTER[0] + 2, load, work, store, OUTER[1] - OUTER[0])
-    else:
-        planes_loop(HALO - 1, HALO + NX + 1, load, work, store)
+            rows.put(gain, (plane,), grad)
+
+    planes_loop(rows.items, load, work, store)
 
 
 def inlet_speed(start, step):
@@ -458,7 +469,7 @@
     later = inlet_speed(start, 1)
     put_inner(
         ahead, 1,
-        lambda plane: (pulled(post, plane, own_rows, 1), cell[0, plane], cell[1, plane]),
+        lambda plane: (pulled(post, plane, OWN, 1), cell[0, plane], cell[1, plane]),
         lambda f, kappa, kind: collide(f, kappa, kind, rates, later)[0],
     )
     tail()
@@ -468,7 +479,7 @@
             return ends[0, i - 18] if plane == 0 else ends[1, i]
         if name == "next":
             return ahead[plane - 1, i]
-        return cell[i, plane] if name == "cell" else post[i, plane, NY : 2 * NY]
+        return cell[i, plane] if name in ("cell", "corner") else post[i, plane, NY : 2 * NY]
 
     send_x(FIRST, read, to_odd, to_even)
     done.append(start_copies(sems.at[6:8], (to_odd, to_odd_hbm), (to_even, to_even_hbm)))
@@ -519,34 +530,56 @@
     put_block(post_zero, post, 27)
     put_block(wide_adjoint, cotangent, 27)
     put_block(wide_cell, cell, 2)
-    wide = {"post": post_zero, "strip": post_zero, "next": post_one, "adjoint": wide_adjoint, "cell": wide_cell}
+    wide = {
+        "post": post_zero, "strip": post_zero, "next": post_one, "adjoint": wide_adjoint, "cell": wide_cell,
+        "corner": wide_cell,
+    }
     receive_x(FIRST, wide, odd_x, even_x)
     wait()
     forward(OWN, post_zero, post_one, wide_cell, speed_one, rates, inlet_speed(start, 1))
     forward(OWN, post_one, post_two, wide_cell, speed_two, rates, inlet_speed(start, 2))
 
 
+def third_edges(
+    rates_hbm, start_hbm, from_partner, even,
+    post_zero, post_one, post_two, wide_adjoint, wide_cell, speed_one, speed_two,
+    rates, start, sems,
+):
+    wait = start_copies(sems, (rates_hbm, rates), (start_hbm, start))
+    wide = {
+        "post": post_zero, "strip": post_zero, "next": post_one, "adjoint": wide_adjoint, "cell": wide_cell,
+        "corner": wide_cell,
+    }
+    receive_y(FIRST, wide, from_partner, even)
+    wait()
+    rows, narrow = edges(even)
+    inlet = inlet_speed(start, 1)
+    forward(narrow, post_zero, post_one, wide_cell, speed_one, rates, inlet, True)
+    forward(rows, post_zero, post_one, wide_cell, speed_one, rates, inlet)
+    forward(rows, post_one, post_two, wide_cell, speed_two, rates, inlet_speed(start, 2))
+
+
+def third_middle_kernel(rates_hbm, start_hbm, _0, _1, _2, _3, _4, _5, _6, even_y, *refs):
+    third_edges(rates_hbm, start_hbm, even_y, True, *refs)
+
+
 def third_late_kernel(
-    rates_hbm, start_hbm, _0, _1, _2, _3, _4, _5, _6, odd_y, even_y,
+    rates_hbm, start_hbm, _0, _1, _2, _3, _4, _5, _6, odd_y,
     post_zero, post_one, post_two, wide_adjoint, wide_cell, speed_one, speed_two,
     last_post, adjoint, gain, to_odd, to_even,
     rates, start, inner, ahead, sems,
 ):
-    wait = start_copies(sems, (rates_hbm, rates), (start_hbm, start))
-    wide = {"post": post_zero, "strip": post_zero, "next": post_one, "adjoint": wide_adjoint, "cell": wide_cell}
-    receive_y(FIRST, wide, odd_y, even_y)
-    wait()
-    inlet = inlet_speed(start, 1)
-    forward(NARROW_EDGE, post_zero, post_one, wide_cell, speed_one, rates, inlet, True)
-    forward(EDGE, post_zero, post_one, wide_cell, speed_one, rates, inlet)
-    forward(EDGE, post_one, post_two, wide_cell, speed_two, rates, inlet_speed(start, 2))
+    third_edges(
+        rates_hbm, start_hbm, odd_y, False, post_zero, post_one, post_two, wide_adjoint, wide_cell, speed_one,
+        speed_two, rates, start, sems,
+    )
     inlet = inlet_speed(start, 3)
 
     def load(n):
         plane = n + HALO
         return (
-            pulled(post_two, plane, own_rows, 1), pulled(wide_adjoint, plane, own_rows, -1),
-            own_rows(wide_cell, (0, plane)), own_rows(wide_cell, (1, plane)),
+            pulled(post_two, plane, OWN, 1), pulled(wide_adjoint, plane, OWN, -1),
+            OWN.get(wide_cell, (0, plane)), OWN.get(wide_cell, (1, plane)),
         )
 
     def work(f, h, kappa, kind):
@@ -561,13 +594,13 @@
             inner[i, n, NY : 2 * NY] = back[i]
         gain[n] = grad
 
-    planes_loop(0, NX, load, work, store)
+    planes_loop(range(NX), load, work, store)
 
     def load_inner(n):
         plane = n + HALO
-        values = [own_rows(speed_two, (i, plane)) for i in range(4)]
+        values = [OWN.get(speed_two, (i, plane)) for i in range(4)]
         return (
-            pulled(inner, n, own_rows, -1), own_rows(wide_cell, (0, plane)), own_rows(wide_cell, (1, plane)), values
+            pulled(inner, n, OWN, -1), OWN.get(wide_cell, (0, plane)), OWN.get(wide_cell, (1, plane)), values
         )
 
     def work_inner(h, kappa, kind, values):
@@ -576,7 +609,7 @@
     put_inner(ahead, -1, load_inner, work_inner)
 
     def read(name, i, plane):
-        if name == "speed":
+        if name == "corner":
             return speed_two[i, plane + HALO, NY : 2 * NY]
         if name == "next":
             return ahead[plane - 1, i]
@@ -603,7 +636,8 @@
     put_block(wide_post, post, 27)
     put_block(adjoint_three, adjoint, 27)
     wide = {
-        "post": wide_post, "adjoint": adjoint_three, "strip": adjoint_three, "next": adjoint_two, "speed": speed_two
+        "post": wide_post, "adjoint": adjoint_three, "strip": adjoint_three, "next": adjoint_two, "speed": speed_two,
+        "corner": speed_two,
     }
     receive_x(SECOND, wide, odd_x, even_x)
     wait()
@@ -611,39 +645,55 @@
     backward(OWN, adjoint_two, adjoint_one, wide_cell, speed_one, gain_one, rates)
 
 
+def fifth_edges(
+    rates_hbm, wide_cell, speed_one, from_partner, even,
+    speed_two, adjoint_three, adjoint_two, adjoint_one, wide_post, gain_two, gain_one,
+    rates, sems,
+):
+    wait = start_copies(sems, (rates_hbm, rates))
+    wide = {
+        "post": wide_post, "adjoint": adjoint_three, "strip": adjoint_three, "next": adjoint_two, "speed": speed_two,
+        "corner": speed_two,
+    }
+    receive_y(SECOND, wide, from_partner, even)
+    wait()
+    rows, narrow = edges(even)
+    backward(narrow, adjoint_three, adjoint_two, wide_cell, speed_two, gain_two, rates, True)
+    backward(rows, adjoint_three, adjoint_two, wide_cell, speed_two, gain_two, rates)
+    backward(rows, adjoint_two, adjoint_one, wide_cell, speed_one, gain_one, rates)
+
+
+def fifth_middle_kernel(rates_hbm, wide_cell, speed_one, even_y, _0, _1, _2, _3, _4, _5, _6, *refs):
+    fifth_edges(rates_hbm, wide_cell, speed_one, even_y, True, *refs)
+
+
 def fifth_late_kernel(
-    rates_hbm, wide_cell, speed_zero, speed_one, gain, porosity, odd_y, even_y, _0, _1, _2, _3, _4, _5, _6,
+    rates_hbm, wide_cell, speed_zero, speed_one, gain, porosity, odd_y, _0, _1, _2, _3, _4, _5, _6,
     flow, first_adjoint, sensitivity,
     speed_two, adjoint_three, adjoint_two, adjoint_one, wide_post, gain_two, gain_one,
     rates, flow_here, adjoint_here, sensitivity_here, sems,
 ):
-    wait = start_copies(sems, (rates_hbm, rates))
-    wide = {
-        "post": wide_post, "adjoint": adjoint_three, "strip": adjoint_three, "next": adjoint_two, "speed": speed_two
-    }
-    receive_y(SECOND, wide, odd_y, even_y)
+    fifth_edges(
+        rates_hbm, wide_cell, speed_one, odd_y, False, speed_two, adjoint_three, adjoint_two, adjoint_one, wide_post,
+        gain_two, gain_one, rates, sems,
+    )
 
     def run(n, carry):
-        tiles = pulled(wide_post, n + HALO, own_rows, 1)
+        tiles = pulled(wide_post, n + HALO, OWN, 1)
         for i in range(27):
             flow_here[i, n] = tiles[i]
         return carry
 
     lax.fori_loop(0, NX, run, 0)
-    wait()
     wait = start_copies(sems, (flow_here, flow))
-    backward(NARROW_EDGE, adjoint_three, adjoint_two, wide_cell, speed_two, gain_two, rates, True)
-    backward(EDGE, adjoint_three, adjoint_two, wide_cell, speed_two, gain_two, rates)
-    backward(EDGE, adjoint_two, adjoint_one, wide_cell, speed_one, gain_one, rates)
-
     def load(n):
         plane = n + HALO
-        total = (gain[n] + own_rows(gain_two, (plane,))) + own_rows(gain_one, (plane,))
+        total = (gain[n] + OWN.get(gain_two, (plane,))) + OWN.get(gain_one, (plane,))
         ramp = RAMP_Q * (1.0 + DRAG_MAX) + (1.0 - DRAG_MAX * RAMP_Q) * porosity[n]
         slope = (DRAG_MAX * RAMP_Q * (1.0 + RAMP_Q)) / (ramp * ramp)
-        kappa, kind = own_rows(wide_cell, (0, plane)), own_rows(wide_cell, (1, plane))
+        kappa, kind = OWN.get(wide_cell, (0, plane)), OWN.get(wide_cell, (1, plane))
         values = [speed_zero[i, n] for i in range(5)]
-        return pulled(adjoint_one, plane, own_rows, -1), kappa, kind, values, total, slope
+        return pulled(adjoint_one, plane, OWN, -1), kappa, kind, values, total, slope
 
     def work(h, kappa, kind, values, total, slope):
         out, grad = collide_back(h, kappa, kind, rates, values[:4], values[4])
@@ -655,7 +705,7 @@
             adjoint_here[i, n] = out[i]
         sensitivity_here[n] = gradient
 
-    planes_loop(0, NX, load, work, store)
+    planes_loop(range(NX), load, work, store)
     last = start_copies(sems.at[1:3], (adjoint_here, first_adjoint), (sensitivity_here, sensitivity))
     wait()
     last()
@@ -730,11 +780,17 @@
     wides = call(
         third_early_kernel, (rates, start_step), (post, held, cell) + x_halos, wides, scalars
     )
+    odd_y, even_y = y_halos
+    kept = tuple(a.shape for a in wides)
+    wides = call(
+        third_middle_kernel, (rates, start_step), tuple(wides) + (even_y,), kept, scalars,
+        aliases={2 + n: n for n in range(len(wides))},
+    )
     tiles = (PLAN_X[SECOND, 1][1], NY, LANES), (PLAN_X[SECOND, -1][1], NY, LANES)
     rows = (PLAN_Y[SECOND, 1][1], LANES), (PLAN_Y[SECOND, -1][1], LANES)
     *wides, post, adjoint, gain, to_odd, to_even = call(
-        third_late_kernel, (rates, start_step), tuple(wides) + y_halos,
-        tuple(a.shape for a in wides) + (block, block, (NX, NY, LANES)) + tiles,
+        third_late_kernel, (rates, start_step), tuple(wides) + (odd_y,),
+        kept + (block, block, (NX, NY, LANES)) + tiles,
         scalars[:2] + (inner, ahead) + scalars[2:], aliases={2 + n: n for n in range(len(wides))},
     )
     wide_cell, speed_one, speed_two = wides[4:]
@@ -747,12 +803,18 @@
         fifth_early_kernel, (rates,), (post, adjoint, wide_cell, speed_one, speed_two) + x_halos,
         (wide_values, wide, wide, wide, wide, wide_gain, wide_gain), scalars, aliases={5: 0},
     )
+    odd_y, even_y = y_halos
+    kept = tuple(a.shape for a in wides)
+    wides = call(
+        fifth_middle_kernel, (rates,), (wide_cell, speed_one, even_y) + tuple(wides), kept, scalars,
+        aliases={4 + n: n for n in range(len(wides))},
+    )
     return call(
         fifth_late_kernel, (rates,),
-        (wide_cell, speed_zero, speed_one, gain, porosity) + y_halos + tuple(wides),
-        (block, block, (NX, NY, LANES)) + tuple(a.shape for a in wides),
+        (wide_cell, speed_zero, speed_one, gain, porosity, odd_y) + tuple(wides),
+        (block, block, (NX, NY, LANES)) + kept,
         (rates_here, block, block, (NX, NY, LANES), pltpu.SemaphoreType.DMA((3,))),
-        aliases={8 + n: 3 + n for n in range(len(wides))}, far_outs=3,
+        aliases={7 + n: 3 + n for n in range(len(wides))}, far_outs=3,
     )[:3]
 
 

time: 76.6 us -> 74 us (0.966)
  waiting for transfers between devices: 21.7 us -> 18.7 us
  Pallas kernels: 12.4 us -> 13.4 us
    ppermute x6, waiting for transfers between devices: 21.7 us -> 18.7 us  [swap(): lax.ppermute(value, axis, [(a, b) for a, b in pairs] + [(b, a) for a, b i...]
    pallas_call x8 -> x10, Pallas kernels: 12.4 us -> 13.4 us  [call(): pl.pallas_call(kernel, out_shape=tuple((f32(*s) for s in outs)), in_specs...]
    unnamed x14 -> x12, local copies, waits for them, and re-layouts: 3.44 us -> 3.44 us
  transfers between devices with their start and end apart: 6 -> 6, of which waited for: 5 -> 5; matrix products, arithmetic and copies ran while one was open for 0% -> 0% of each run, Pallas kernels for 5% -> 8%
where the time goes in v8:
time: 74 us; the launch traced here: 73.4 us
  starting transfers between devices  32.2 us (44%)
  waiting for transfers between devices  18.7 us (25%)
  Pallas kernels  13.4 us (18%)
  blocking collectives  4.29 us (6%)
  local copies, waits for them, and re-layouts  3.44 us (5%)
  between operations  1.42 us (2%)
    ppermute x6, starting transfers between devices, swap(): lax.ppermute(value, axis, [(a, b) for a, b in pairs] + [(b, a) for a, b i...  32.2 us
    ppermute x6, waiting for transfers between devices, swap(): lax.ppermute(value, axis, [(a, b) for a, b in pairs] + [(b, a) for a, b i...  18.7 us
    pallas_call x10, Pallas kernels, call(): pl.pallas_call(kernel, out_shape=tuple((f32(*s) for s in outs)), in_specs...  13.4 us
    all_gather x2, blocking collectives, exchange_y(): lax.all_gather(to_even, 'gy', axis_index_groups=partners('gy', 0))  4.29 us
    unnamed x12, local copies, waits for them, and re-layouts  3.44 us
  transfers between devices with their start and end apart: 6, of which 5 were waited for; matrix products, arithmetic and copies ran while one was open for 0% of the time, Pallas kernels for 8%

profile of v8, /device:TPU:6, one launch (start us, length us, event | category | flops | bytes accessed | tf_op | source)
XLA Modules:
  0.0 73.4 jit_solution(6469676612332231755)
XLA Ops:
  1.3 2.4 %first_kernel.1 = (f32[27,4,8,128]{3,2,1,0:T(8,128)}, f32[2,4,8,128]{3,2,1,0:T(8,128)}, f32[5,4,8,128]{3,2,1,0:T(8,128)}, f32[55,8,128]{2,1,0:T(8,128)}, f32[55,8,128]{2,1,0:T(8,128)}) custom-call(f32[27]{0:T(128)} %rates_hbm.13, s32[1]{0:T(128)S(6)} %copy.67.start_hbm, f32[27,4,8,128]{3,2,1,0:T(8,128)} %populations.1, f32[27,4,8,128]{3,2,1,0:T(8,128)} %refs_1_.1, ...), custom_call_target="tpu_custom_call" | custom-call | tf_op jit(solution)/shard_map/first_kernel/pallas_call | solution.py:721
  3.6 13.8 %collective-permute-start = (f32[55,8,128]{2,1,0:T(8,128)}, f32[55,8,128]{2,1,0:T(8,128)S(1)}, u32[]{:S(2)}, u32[]{:S(2)}) collective-permute-start(f32[55,8,128]{2,1,0:T(8,128)} %get-tuple-element.59), channel_id=1, source_target_pairs={{32,64},{96,128},{160,192},{224,256},{288,320},{352,384},{416,448}... | collective-permute-start | bytes 675848 | tf_op jit(solution)/shard_map/ppermute | solution.py:740
  17.5 1.9 %collective-permute-start.1 = (f32[55,8,128]{2,1,0:T(8,128)}, f32[55,8,128]{2,1,0:T(8,128)S(1)}, u32[]{:S(2)}, u32[]{:S(2)}) collective-permute-start(f32[55,8,128]{2,1,0:T(8,128)} %get-tuple-element.60), channel_id=1, source_target_pairs={{0,32},{64,96},{128,160},{192,224},{256,288},{320,352},{384,416},{... | collective-permute-start | bytes 675848 | tf_op jit(solution)/shard_map/ppermute | solution.py:740
  19.4 0.0 copy-start
  19.4 1.0 %copy-done = f32[27,4,8,128]{3,2,1,0:T(8,128)S(1)} copy-done((f32[27,4,8,128]{3,2,1,0:T(8,128)S(1)}, f32[27,4,8,128]{3,2,1,0:T(8,128)}, u32[]{:S(2)}) %copy-start) | copy-done | bytes 442392
  20.4 0.0 copy-start.1
  20.4 1.0 %copy-done.1 = f32[27,4,8,128]{3,2,1,0:T(8,128)S(1)} copy-done((f32[27,4,8,128]{3,2,1,0:T(8,128)S(1)}, f32[27,4,8,128]{3,2,1,0:T(8,128)}, u32[]{:S(2)}) %copy-start.1) | copy-done | bytes 442392
  21.4 0.0 copy-start.4
  21.4 0.8 %copy-done.4 = f32[2,4,8,128]{3,2,1,0:T(8,128)S(1)} copy-done((f32[2,4,8,128]{3,2,1,0:T(8,128)S(1)}, f32[2,4,8,128]{3,2,1,0:T(8,128)}, u32[]{:S(2)}) %copy-start.4) | copy-done | bytes 32792
  22.2 0.6 holding_kernel.1
  22.8 5.2 %collective-permute-done.odd_x = f32[55,8,128]{2,1,0:T(8,128)S(1)} collective-permute-done((f32[55,8,128]{2,1,0:T(8,128)}, f32[55,8,128]{2,1,0:T(8,128)S(1)}, u32[]{:S(2)}, u32[]{:S(2)}) %collective-permute-start) | collective-permute-done | bytes 225312 | tf_op jit(solution)/shard_map/ppermute | solution.py:740
  28.0 0.0 collective-permute-done.1.even_x
  28.0 0.2 second_kernel.1
  28.2 2.6 %collective-permute-start.2 = (f32[456,128]{1,0:T(8,128)S(1)}, f32[456,128]{1,0:T(8,128)S(1)}, u32[]{:S(2)}, u32[]{:S(2)}) collective-permute-start(f32[456,128]{1,0:T(8,128)S(1)} %get-tuple-element.76), channel_id=1, source_target_pairs={{1,2},{3,4},{5,6},{7,8},{9,10},{11,12},{13,14},{15,16},{17,18},{19... | collective-permute-start | bytes 700424 | tf_op jit(solution)/shard_map/ppermute | solution.py:740
  30.8 0.0 copy-start.5
  30.8 0.6 copy-done.5
  31.5 1.8 %third_early_kernel.1 = (f32[27,10,24,128]{3,2,1,0:T(8,128)S(1)}, f32[27,10,24,128]{3,2,1,0:T(8,128)S(1)}, f32[27,10,24,128]{3,2,1,0:T(8,128)S(1)}, f32[27,10,24...) custom-call(f32[27]{0:T(128)S(1)} %copy-done.5, ...), custom_call_target="tpu_custom_call" | custom-call | tf_op jit(solution)/shard_map/third_early_kernel/pallas_call | solution.py:721
  33.2 2.1 %all-gather = f32[912,128]{1,0:T(8,128)S(1)} all-gather(f32[456,128]{1,0:T(8,128)S(1)} %get-tuple-element.68), channel_id=2, replica_groups={{0,1},{2,3},{4,5},{6,7},{8,9},{10,11},{12,13},{14,15},{16,17},{18,19},{..., dimensions={0}, use_global_device_ids=true | all-gather | bytes 700416 | tf_op jit(solution)/shard_map/all_gather | solution.py:749
  35.4 1.1 %third_middle_kernel.1 = (f32[27,10,24,128]{3,2,1,0:T(8,128)S(1)}, f32[27,10,24,128]{3,2,1,0:T(8,128)S(1)}, f32[27,10,24,128]{3,2,1,0:T(8,128)S(1)}, f32[27,10,2...) custom-call(f32[27]{0:T(128)S(1)} %copy-done.5, ...), custom_call_target="tpu_custom_call", output_to_operand_aliasing={{0}: (2, {}), {1}: (3, {}), {2}: (4, {}), {3}: (5, {}), {4}... | custom-call | tf_op jit(solution)/shard_map/third_middle_kernel/pallas_call | solution.py:721
  36.5 3.3 %collective-permute-done.2.odd_y = f32[456,128]{1,0:T(8,128)S(1)} collective-permute-done((f32[456,128]{1,0:T(8,128)S(1)}, f32[456,128]{1,0:T(8,128)S(1)}, u32[]{:S(2)}, u32[]{:S(2)}) %collective-permute-start.2) | collective-permute-done | bytes 233504 | tf_op jit(solution)/shard_map/ppermute | solution.py:740
  39.8 1.9 %third_late_kernel.1 = (f32[27,10,24,128]{3,2,1,0:T(8,128)S(1)}, f32[27,10,24,128]{3,2,1,0:T(8,128)S(1)}, f32[27,10,24,128]{3,2,1,0:T(8,128)S(1)}, f32[27,10,24,...) custom-call(f32[27]{0:T(128)S(1)} %copy-done.5, ...), custom_call_target="tpu_custom_call", output_to_operand_aliasing={{0}: (2, {}), {1}: (3, {}), {2}: (4, {}), {3}: (5, {}), {4}... | custom-call | tf_op jit(solution)/shard_map/third_late_kernel/pallas_call | solution.py:721
  41.7 9.2 %collective-permute-start.3 = (f32[53,8,128]{2,1,0:T(8,128)S(1)}, f32[53,8,128]{2,1,0:T(8,128)S(1)}, u32[]{:S(2)}, u32[]{:S(2)}) collective-permute-start(f32[53,8,128]{2,1,0:T(8,128)S(1)} %get-tuple-element.84), channel_id=1, source_target_pairs={{32,64},{96,128},{160,192},{224,256},{288,320},{352,384},{416,448}... | collective-permute-start | bytes 651272 | tf_op jit(solution)/shard_map/ppermute | solution.py:740
  50.9 1.9 %collective-permute-start.4 = (f32[53,8,128]{2,1,0:T(8,128)S(1)}, f32[53,8,128]{2,1,0:T(8,128)S(1)}, u32[]{:S(2)}, u32[]{:S(2)}) collective-permute-start(f32[53,8,128]{2,1,0:T(8,128)S(1)} %get-tuple-element.85), channel_id=1, source_target_pairs={{0,32},{64,96},{128,160},{192,224},{256,288},{320,352},{384,416},{... | collective-permute-start | bytes 651272 | tf_op jit(solution)/shard_map/ppermute | solution.py:740
  52.9 5.7 %collective-permute-done.3.odd_x = f32[53,8,128]{2,1,0:T(8,128)S(1)} collective-permute-done((f32[53,8,128]{2,1,0:T(8,128)S(1)}, f32[53,8,128]{2,1,0:T(8,128)S(1)}, u32[]{:S(2)}, u32[]{:S(2)}) %collective-permute-start.3) | collective-permute-done | bytes 217120 | tf_op jit(solution)/shard_map/ppermute | solution.py:740
  58.6 0.1 collective-permute-done.4.even_x
  58.7 0.2 fourth_kernel.1
  58.9 2.6 %collective-permute-start.5 = (f32[464,128]{1,0:T(8,128)S(1)}, f32[464,128]{1,0:T(8,128)S(1)}, u32[]{:S(2)}, u32[]{:S(2)}) collective-permute-start(f32[464,128]{1,0:T(8,128)S(1)} %get-tuple-element.86), channel_id=1, source_target_pairs={{1,2},{3,4},{5,6},{7,8},{9,10},{11,12},{13,14},{15,16},{17,18},{19... | collective-permute-start | bytes 712712 | tf_op jit(solution)/shard_map/ppermute | solution.py:740
  61.5 1.6 %fifth_early_kernel.1 = (f32[5,10,24,128]{3,2,1,0:T(8,128)S(1)}, f32[27,10,24,128]{3,2,1,0:T(8,128)S(1)}, f32[27,10,24,128]{3,2,1,0:T(8,128)S(1)}, f32[27,10,24,...) custom-call(f32[27]{0:T(128)S(1)} %copy-done.5, ...), custom_call_target="tpu_custom_call", output_to_operand_aliasing={{0}: (5, {})} | custom-call | tf_op jit(solution)/shard_map/fifth_early_kernel/pallas_call | solution.py:721
  63.2 2.1 %all-gather.1 = f32[928,128]{1,0:T(8,128)S(1)} all-gather(f32[464,128]{1,0:T(8,128)S(1)} %get-tuple-element.87), channel_id=3, replica_groups={{0,1},{2,3},{4,5},{6,7},{8,9},{10,11},{12,13},{14,15},{16,17},{18,19},{..., dimensions={0}, use_global_device_ids=true | all-gather | bytes 712704 | tf_op jit(solution)/shard_map/all_gather | solution.py:749
  65.3 0.0 copy-start.2
  65.3 0.0 copy-start.3
  65.3 1.1 %fifth_middle_kernel.1 = (f32[5,10,24,128]{3,2,1,0:T(8,128)S(1)}, f32[27,10,24,128]{3,2,1,0:T(8,128)S(1)}, f32[27,10,24,128]{3,2,1,0:T(8,128)S(1)}, f32[27,10,24...) custom-call(f32[27]{0:T(128)S(1)} %copy-done.5, ...), custom_call_target="tpu_custom_call", output_to_operand_aliasing={{0}: (4, {}), {1}: (5, {}), {2}: (6, {}), {3}: (7, {}), {4}... | custom-call | tf_op jit(solution)/shard_map/fifth_middle_kernel/pallas_call | solution.py:721
  66.5 4.3 %collective-permute-done.5.odd_y = f32[464,128]{1,0:T(8,128)S(1)} collective-permute-done((f32[464,128]{1,0:T(8,128)S(1)}, f32[464,128]{1,0:T(8,128)S(1)}, u32[]{:S(2)}, u32[]{:S(2)}) %collective-permute-start.5) | collective-permute-done | bytes 237600 | tf_op jit(solution)/shard_map/ppermute | solution.py:740
  70.8 0.0 copy-done.2
  70.8 0.0 copy-done.3
  70.8 2.6 %fifth_late_kernel.1 = (f32[27,4,8,128]{3,2,1,0:T(8,128)}, f32[27,4,8,128]{3,2,1,0:T(8,128)}, f32[4,8,128]{2,1,0:T(8,128)}, f32[5,10,24,128]{3,2,1,0:T(8,128)S(1...) custom-call(f32[27]{0:T(128)S(1)} %copy-done.5, ...), custom_call_target="tpu_custom_call", output_to_operand_aliasing={{3}: (7, {}), {4}: (8, {}), {5}: (9, {}), {6}: (10, {}), {7... | custom-call | tf_op jit(solution)/shard_map/fifth_late_kernel/pallas_call | solution.py:721
Async XLA Ops:
  3.6 24.3 %collective-permute-start = (f32[55,8,128]{2,1,0:T(8,128)}, f32[55,8,128]{2,1,0:T(8,128)S(1)}, u32[]{:S(2)}, u32[]{:S(2)}) collective-permute-start(f32[55,8,128]{2,1,0:T(8,128)} %get-tuple-element.59), channel_id=1, source_target_pairs={{32,64},{96,128},{160,192},{224,256},{288,320},{352,384},{416,448}... | collective-permute-start | bytes 675848 | tf_op jit(solution)/shard_map/ppermute | solution.py:740
  17.5 10.5 %collective-permute-start.1 = (f32[55,8,128]{2,1,0:T(8,128)}, f32[55,8,128]{2,1,0:T(8,128)S(1)}, u32[]{:S(2)}, u32[]{:S(2)}) collective-permute-start(f32[55,8,128]{2,1,0:T(8,128)} %get-tuple-element.60), channel_id=1, source_target_pairs={{0,32},{64,96},{128,160},{192,224},{256,288},{320,352},{384,416},{... | collective-permute-start | bytes 675848 | tf_op jit(solution)/shard_map/ppermute | solution.py:740
  19.4 1.0 %copy-start = (f32[27,4,8,128]{3,2,1,0:T(8,128)S(1)}, f32[27,4,8,128]{3,2,1,0:T(8,128)}, u32[]{:S(2)}) copy-start(f32[27,4,8,128]{3,2,1,0:T(8,128)} %refs_1_.1) | copy-start | bytes 1327108
  20.4 1.0 %copy-start.1 = (f32[27,4,8,128]{3,2,1,0:T(8,128)S(1)}, f32[27,4,8,128]{3,2,1,0:T(8,128)}, u32[]{:S(2)}) copy-start(f32[27,4,8,128]{3,2,1,0:T(8,128)} %get-tuple-element.54.refs_0_) | copy-start | bytes 1327108
  21.4 0.8 %copy-start.4 = (f32[2,4,8,128]{3,2,1,0:T(8,128)S(1)}, f32[2,4,8,128]{3,2,1,0:T(8,128)}, u32[]{:S(2)}) copy-start(f32[2,4,8,128]{3,2,1,0:T(8,128)} %get-tuple-element.55.refs_2_) | copy-start | bytes 98308
  28.2 11.6 %collective-permute-start.2 = (f32[456,128]{1,0:T(8,128)S(1)}, f32[456,128]{1,0:T(8,128)S(1)}, u32[]{:S(2)}, u32[]{:S(2)}) collective-permute-start(f32[456,128]{1,0:T(8,128)S(1)} %get-tuple-element.76), channel_id=1, source_target_pairs={{1,2},{3,4},{5,6},{7,8},{9,10},{11,12},{13,14},{15,16},{17,18},{19... | collective-permute-start | bytes 700424 | tf_op jit(solution)/shard_map/ppermute | solution.py:740
  30.8 0.7 copy-start.5
  41.7 16.9 %collective-permute-start.3 = (f32[53,8,128]{2,1,0:T(8,128)S(1)}, f32[53,8,128]{2,1,0:T(8,128)S(1)}, u32[]{:S(2)}, u32[]{:S(2)}) collective-permute-start(f32[53,8,128]{2,1,0:T(8,128)S(1)} %get-tuple-element.84), channel_id=1, source_target_pairs={{32,64},{96,128},{160,192},{224,256},{288,320},{352,384},{416,448}... | collective-permute-start | bytes 651272 | tf_op jit(solution)/shard_map/ppermute | solution.py:740
  50.9 7.8 %collective-permute-start.4 = (f32[53,8,128]{2,1,0:T(8,128)S(1)}, f32[53,8,128]{2,1,0:T(8,128)S(1)}, u32[]{:S(2)}, u32[]{:S(2)}) collective-permute-start(f32[53,8,128]{2,1,0:T(8,128)S(1)} %get-tuple-element.85), channel_id=1, source_target_pairs={{0,32},{64,96},{128,160},{192,224},{256,288},{320,352},{384,416},{... | collective-permute-start | bytes 651272 | tf_op jit(solution)/shard_map/ppermute | solution.py:740
  58.9 11.9 %collective-permute-start.5 = (f32[464,128]{1,0:T(8,128)S(1)}, f32[464,128]{1,0:T(8,128)S(1)}, u32[]{:S(2)}, u32[]{:S(2)}) collective-permute-start(f32[464,128]{1,0:T(8,128)S(1)} %get-tuple-element.86), channel_id=1, source_target_pairs={{1,2},{3,4},{5,6},{7,8},{9,10},{11,12},{13,14},{15,16},{17,18},{19... | collective-permute-start | bytes 712712 | tf_op jit(solution)/shard_map/ppermute | solution.py:740
  65.3 5.5 %copy-start.2 = (f32[5,4,8,128]{3,2,1,0:T(8,128)S(1)}, f32[5,4,8,128]{3,2,1,0:T(8,128)}, u32[]{:S(2)}) copy-start(f32[5,4,8,128]{3,2,1,0:T(8,128)} %get-tuple-element.78.speed_zero) | copy-start | bytes 245764
  65.3 5.5 %copy-start.3 = (f32[4,8,128]{2,1,0:T(8,128)S(1)}, f32[4,8,128]{2,1,0:T(8,128)}, u32[]{:S(2)}) copy-start(f32[4,8,128]{2,1,0:T(8,128)} %porosity.3) | copy-start | bytes 49156

commit v9 on v8

--- a/solution.py
+++ b/solution.py
@@ -578,12 +578,13 @@
     def load(n):
         plane = n + HALO
         return (
-            pulled(post_two, plane, OWN, 1), pulled(wide_adjoint, plane, OWN, -1),
+            plane, pulled(post_two, plane, OWN, 1),
             OWN.get(wide_cell, (0, plane)), OWN.get(wide_cell, (1, plane)),
         )
 
-    def work(f, h, kappa, kind):
+    def work(plane, f, kappa, kind):
         out, values = collide(f, kappa, kind, rates, inlet)
+        h = pulled(wide_adjoint, plane, OWN, -1)
         return out, collide_back(h, kappa, kind, rates, values[:4], values[4])
 
     def store(n, result):

time: 74 us -> 74.1 us (level)
  no operation moved by 1% of the time
where the time goes in v9:
time: 74.1 us; the launch traced here: 73.4 us
  starting transfers between devices  32.2 us (43%)
  waiting for transfers between devices  18.7 us (25%)
  Pallas kernels  13.4 us (18%)
  blocking collectives  4.29 us (6%)
  local copies, waits for them, and re-layouts  3.44 us (5%)
  between operations  1.42 us (2%)
    ppermute x6, starting transfers between devices, swap(): lax.ppermute(value, axis, [(a, b) for a, b in pairs] + [(b, a) for a, b i...  32.2 us
    ppermute x6, waiting for transfers between devices, swap(): lax.ppermute(value, axis, [(a, b) for a, b in pairs] + [(b, a) for a, b i...  18.7 us
    pallas_call x10, Pallas kernels, call(): pl.pallas_call(kernel, out_shape=tuple((f32(*s) for s in outs)), in_specs...  13.4 us
    all_gather x2, blocking collectives, exchange_y(): lax.all_gather(to_even, 'gy', axis_index_groups=partners('gy', 0))  4.29 us
    unnamed x12, local copies, waits for them, and re-layouts  3.44 us
  transfers between devices with their start and end apart: 6, of which 5 were waited for; matrix products, arithmetic and copies ran while one was open for 0% of the time, Pallas kernels for 8%

profile of v9, /device:TPU:6, one launch (start us, length us, event | category | flops | bytes accessed | tf_op | source)
XLA Modules:
  0.0 73.4 jit_solution(2423748260312412096)
XLA Ops:
  1.3 2.4 %first_kernel.1 = (f32[27,4,8,128]{3,2,1,0:T(8,128)}, f32[2,4,8,128]{3,2,1,0:T(8,128)}, f32[5,4,8,128]{3,2,1,0:T(8,128)}, f32[55,8,128]{2,1,0:T(8,128)}, f32[55,8,128]{2,1,0:T(8,128)}) custom-call(f32[27]{0:T(128)} %rates_hbm.13, s32[1]{0:T(128)S(6)} %copy.67.start_hbm, f32[27,4,8,128]{3,2,1,0:T(8,128)} %populations.1, f32[27,4,8,128]{3,2,1,0:T(8,128)} %refs_1_.1, ...), custom_call_target="tpu_custom_call" | custom-call | tf_op jit(solution)/shard_map/first_kernel/pallas_call | solution.py:722
  3.6 13.8 %collective-permute-start = (f32[55,8,128]{2,1,0:T(8,128)}, f32[55,8,128]{2,1,0:T(8,128)S(1)}, u32[]{:S(2)}, u32[]{:S(2)}) collective-permute-start(f32[55,8,128]{2,1,0:T(8,128)} %get-tuple-element.59), channel_id=1, source_target_pairs={{32,64},{96,128},{160,192},{224,256},{288,320},{352,384},{416,448}... | collective-permute-start | bytes 675848 | tf_op jit(solution)/shard_map/ppermute | solution.py:741
  17.5 1.9 %collective-permute-start.1 = (f32[55,8,128]{2,1,0:T(8,128)}, f32[55,8,128]{2,1,0:T(8,128)S(1)}, u32[]{:S(2)}, u32[]{:S(2)}) collective-permute-start(f32[55,8,128]{2,1,0:T(8,128)} %get-tuple-element.60), channel_id=1, source_target_pairs={{0,32},{64,96},{128,160},{192,224},{256,288},{320,352},{384,416},{... | collective-permute-start | bytes 675848 | tf_op jit(solution)/shard_map/ppermute | solution.py:741
  19.4 0.0 copy-start
  19.4 1.0 %copy-done = f32[27,4,8,128]{3,2,1,0:T(8,128)S(1)} copy-done((f32[27,4,8,128]{3,2,1,0:T(8,128)S(1)}, f32[27,4,8,128]{3,2,1,0:T(8,128)}, u32[]{:S(2)}) %copy-start) | copy-done | bytes 442392
  20.4 0.0 copy-start.1
  20.4 1.0 %copy-done.1 = f32[27,4,8,128]{3,2,1,0:T(8,128)S(1)} copy-done((f32[27,4,8,128]{3,2,1,0:T(8,128)S(1)}, f32[27,4,8,128]{3,2,1,0:T(8,128)}, u32[]{:S(2)}) %copy-start.1) | copy-done | bytes 442392
  21.4 0.0 copy-start.4
  21.4 0.8 %copy-done.4 = f32[2,4,8,128]{3,2,1,0:T(8,128)S(1)} copy-done((f32[2,4,8,128]{3,2,1,0:T(8,128)S(1)}, f32[2,4,8,128]{3,2,1,0:T(8,128)}, u32[]{:S(2)}) %copy-start.4) | copy-done | bytes 32792
  22.2 0.6 holding_kernel.1
  22.8 5.2 %collective-permute-done.odd_x = f32[55,8,128]{2,1,0:T(8,128)S(1)} collective-permute-done((f32[55,8,128]{2,1,0:T(8,128)}, f32[55,8,128]{2,1,0:T(8,128)S(1)}, u32[]{:S(2)}, u32[]{:S(2)}) %collective-permute-start) | collective-permute-done | bytes 225312 | tf_op jit(solution)/shard_map/ppermute | solution.py:741
  28.0 0.0 collective-permute-done.1.even_x
  28.0 0.2 second_kernel.1
  28.2 2.6 %collective-permute-start.2 = (f32[456,128]{1,0:T(8,128)S(1)}, f32[456,128]{1,0:T(8,128)S(1)}, u32[]{:S(2)}, u32[]{:S(2)}) collective-permute-start(f32[456,128]{1,0:T(8,128)S(1)} %get-tuple-element.76), channel_id=1, source_target_pairs={{1,2},{3,4},{5,6},{7,8},{9,10},{11,12},{13,14},{15,16},{17,18},{19... | collective-permute-start | bytes 700424 | tf_op jit(solution)/shard_map/ppermute | solution.py:741
  30.8 0.0 copy-start.5
  30.8 0.6 copy-done.5
  31.5 1.8 %third_early_kernel.1 = (f32[27,10,24,128]{3,2,1,0:T(8,128)S(1)}, f32[27,10,24,128]{3,2,1,0:T(8,128)S(1)}, f32[27,10,24,128]{3,2,1,0:T(8,128)S(1)}, f32[27,10,24...) custom-call(f32[27]{0:T(128)S(1)} %copy-done.5, ...), custom_call_target="tpu_custom_call" | custom-call | tf_op jit(solution)/shard_map/third_early_kernel/pallas_call | solution.py:722
  33.2 2.1 %all-gather = f32[912,128]{1,0:T(8,128)S(1)} all-gather(f32[456,128]{1,0:T(8,128)S(1)} %get-tuple-element.68), channel_id=2, replica_groups={{0,1},{2,3},{4,5},{6,7},{8,9},{10,11},{12,13},{14,15},{16,17},{18,19},{..., dimensions={0}, use_global_device_ids=true | all-gather | bytes 700416 | tf_op jit(solution)/shard_map/all_gather | solution.py:750
  35.4 1.1 %third_middle_kernel.1 = (f32[27,10,24,128]{3,2,1,0:T(8,128)S(1)}, f32[27,10,24,128]{3,2,1,0:T(8,128)S(1)}, f32[27,10,24,128]{3,2,1,0:T(8,128)S(1)}, f32[27,10,2...) custom-call(f32[27]{0:T(128)S(1)} %copy-done.5, ...), custom_call_target="tpu_custom_call", output_to_operand_aliasing={{0}: (2, {}), {1}: (3, {}), {2}: (4, {}), {3}: (5, {}), {4}... | custom-call | tf_op jit(solution)/shard_map/third_middle_kernel/pallas_call | solution.py:722
  36.5 3.3 %collective-permute-done.2.odd_y = f32[456,128]{1,0:T(8,128)S(1)} collective-permute-done((f32[456,128]{1,0:T(8,128)S(1)}, f32[456,128]{1,0:T(8,128)S(1)}, u32[]{:S(2)}, u32[]{:S(2)}) %collective-permute-start.2) | collective-permute-done | bytes 233504 | tf_op jit(solution)/shard_map/ppermute | solution.py:741
  39.8 1.9 %third_late_kernel.1 = (f32[27,10,24,128]{3,2,1,0:T(8,128)S(1)}, f32[27,10,24,128]{3,2,1,0:T(8,128)S(1)}, f32[27,10,24,128]{3,2,1,0:T(8,128)S(1)}, f32[27,10,24,...) custom-call(f32[27]{0:T(128)S(1)} %copy-done.5, ...), custom_call_target="tpu_custom_call", output_to_operand_aliasing={{0}: (2, {}), {1}: (3, {}), {2}: (4, {}), {3}: (5, {}), {4}... | custom-call | tf_op jit(solution)/shard_map/third_late_kernel/pallas_call | solution.py:722
  41.7 9.2 %collective-permute-start.3 = (f32[53,8,128]{2,1,0:T(8,128)S(1)}, f32[53,8,128]{2,1,0:T(8,128)S(1)}, u32[]{:S(2)}, u32[]{:S(2)}) collective-permute-start(f32[53,8,128]{2,1,0:T(8,128)S(1)} %get-tuple-element.84), channel_id=1, source_target_pairs={{32,64},{96,128},{160,192},{224,256},{288,320},{352,384},{416,448}... | collective-permute-start | bytes 651272 | tf_op jit(solution)/shard_map/ppermute | solution.py:741
  50.9 1.9 %collective-permute-start.4 = (f32[53,8,128]{2,1,0:T(8,128)S(1)}, f32[53,8,128]{2,1,0:T(8,128)S(1)}, u32[]{:S(2)}, u32[]{:S(2)}) collective-permute-start(f32[53,8,128]{2,1,0:T(8,128)S(1)} %get-tuple-element.85), channel_id=1, source_target_pairs={{0,32},{64,96},{128,160},{192,224},{256,288},{320,352},{384,416},{... | collective-permute-start | bytes 651272 | tf_op jit(solution)/shard_map/ppermute | solution.py:741
  52.9 5.7 %collective-permute-done.3.odd_x = f32[53,8,128]{2,1,0:T(8,128)S(1)} collective-permute-done((f32[53,8,128]{2,1,0:T(8,128)S(1)}, f32[53,8,128]{2,1,0:T(8,128)S(1)}, u32[]{:S(2)}, u32[]{:S(2)}) %collective-permute-start.3) | collective-permute-done | bytes 217120 | tf_op jit(solution)/shard_map/ppermute | solution.py:741
  58.6 0.1 collective-permute-done.4.even_x
  58.7 0.2 fourth_kernel.1
  58.9 2.6 %collective-permute-start.5 = (f32[464,128]{1,0:T(8,128)S(1)}, f32[464,128]{1,0:T(8,128)S(1)}, u32[]{:S(2)}, u32[]{:S(2)}) collective-permute-start(f32[464,128]{1,0:T(8,128)S(1)} %get-tuple-element.86), channel_id=1, source_target_pairs={{1,2},{3,4},{5,6},{7,8},{9,10},{11,12},{13,14},{15,16},{17,18},{19... | collective-permute-start | bytes 712712 | tf_op jit(solution)/shard_map/ppermute | solution.py:741
  61.5 1.6 %fifth_early_kernel.1 = (f32[5,10,24,128]{3,2,1,0:T(8,128)S(1)}, f32[27,10,24,128]{3,2,1,0:T(8,128)S(1)}, f32[27,10,24,128]{3,2,1,0:T(8,128)S(1)}, f32[27,10,24,...) custom-call(f32[27]{0:T(128)S(1)} %copy-done.5, ...), custom_call_target="tpu_custom_call", output_to_operand_aliasing={{0}: (5, {})} | custom-call | tf_op jit(solution)/shard_map/fifth_early_kernel/pallas_call | solution.py:722
  63.2 2.1 %all-gather.1 = f32[928,128]{1,0:T(8,128)S(1)} all-gather(f32[464,128]{1,0:T(8,128)S(1)} %get-tuple-element.87), channel_id=3, replica_groups={{0,1},{2,3},{4,5},{6,7},{8,9},{10,11},{12,13},{14,15},{16,17},{18,19},{..., dimensions={0}, use_global_device_ids=true | all-gather | bytes 712704 | tf_op jit(solution)/shard_map/all_gather | solution.py:750
  65.3 0.0 copy-start.2
  65.3 0.0 copy-start.3
  65.3 1.1 %fifth_middle_kernel.1 = (f32[5,10,24,128]{3,2,1,0:T(8,128)S(1)}, f32[27,10,24,128]{3,2,1,0:T(8,128)S(1)}, f32[27,10,24,128]{3,2,1,0:T(8,128)S(1)}, f32[27,10,24...) custom-call(f32[27]{0:T(128)S(1)} %copy-done.5, ...), custom_call_target="tpu_custom_call", output_to_operand_aliasing={{0}: (4, {}), {1}: (5, {}), {2}: (6, {}), {3}: (7, {}), {4}... | custom-call | tf_op jit(solution)/shard_map/fifth_middle_kernel/pallas_call | solution.py:722
  66.5 4.3 %collective-permute-done.5.odd_y = f32[464,128]{1,0:T(8,128)S(1)} collective-permute-done((f32[464,128]{1,0:T(8,128)S(1)}, f32[464,128]{1,0:T(8,128)S(1)}, u32[]{:S(2)}, u32[]{:S(2)}) %collective-permute-start.5) | collective-permute-done | bytes 237600 | tf_op jit(solution)/shard_map/ppermute | solution.py:741
  70.8 0.0 copy-done.2
  70.8 0.0 copy-done.3
  70.8 2.6 %fifth_late_kernel.1 = (f32[27,4,8,128]{3,2,1,0:T(8,128)}, f32[27,4,8,128]{3,2,1,0:T(8,128)}, f32[4,8,128]{2,1,0:T(8,128)}, f32[5,10,24,128]{3,2,1,0:T(8,128)S(1...) custom-call(f32[27]{0:T(128)S(1)} %copy-done.5, ...), custom_call_target="tpu_custom_call", output_to_operand_aliasing={{3}: (7, {}), {4}: (8, {}), {5}: (9, {}), {6}: (10, {}), {7... | custom-call | tf_op jit(solution)/shard_map/fifth_late_kernel/pallas_call | solution.py:722
Async XLA Ops:
  3.6 24.3 %collective-permute-start = (f32[55,8,128]{2,1,0:T(8,128)}, f32[55,8,128]{2,1,0:T(8,128)S(1)}, u32[]{:S(2)}, u32[]{:S(2)}) collective-permute-start(f32[55,8,128]{2,1,0:T(8,128)} %get-tuple-element.59), channel_id=1, source_target_pairs={{32,64},{96,128},{160,192},{224,256},{288,320},{352,384},{416,448}... | collective-permute-start | bytes 675848 | tf_op jit(solution)/shard_map/ppermute | solution.py:741
  17.5 10.5 %collective-permute-start.1 = (f32[55,8,128]{2,1,0:T(8,128)}, f32[55,8,128]{2,1,0:T(8,128)S(1)}, u32[]{:S(2)}, u32[]{:S(2)}) collective-permute-start(f32[55,8,128]{2,1,0:T(8,128)} %get-tuple-element.60), channel_id=1, source_target_pairs={{0,32},{64,96},{128,160},{192,224},{256,288},{320,352},{384,416},{... | collective-permute-start | bytes 675848 | tf_op jit(solution)/shard_map/ppermute | solution.py:741
  19.4 1.0 %copy-start = (f32[27,4,8,128]{3,2,1,0:T(8,128)S(1)}, f32[27,4,8,128]{3,2,1,0:T(8,128)}, u32[]{:S(2)}) copy-start(f32[27,4,8,128]{3,2,1,0:T(8,128)} %refs_1_.1) | copy-start | bytes 1327108
  20.4 1.0 %copy-start.1 = (f32[27,4,8,128]{3,2,1,0:T(8,128)S(1)}, f32[27,4,8,128]{3,2,1,0:T(8,128)}, u32[]{:S(2)}) copy-start(f32[27,4,8,128]{3,2,1,0:T(8,128)} %get-tuple-element.54.refs_0_) | copy-start | bytes 1327108
  21.4 0.8 %copy-start.4 = (f32[2,4,8,128]{3,2,1,0:T(8,128)S(1)}, f32[2,4,8,128]{3,2,1,0:T(8,128)}, u32[]{:S(2)}) copy-start(f32[2,4,8,128]{3,2,1,0:T(8,128)} %get-tuple-element.55.refs_2_) | copy-start | bytes 98308
  28.2 11.6 %collective-permute-start.2 = (f32[456,128]{1,0:T(8,128)S(1)}, f32[456,128]{1,0:T(8,128)S(1)}, u32[]{:S(2)}, u32[]{:S(2)}) collective-permute-start(f32[456,128]{1,0:T(8,128)S(1)} %get-tuple-element.76), channel_id=1, source_target_pairs={{1,2},{3,4},{5,6},{7,8},{9,10},{11,12},{13,14},{15,16},{17,18},{19... | collective-permute-start | bytes 700424 | tf_op jit(solution)/shard_map/ppermute | solution.py:741
  30.8 0.7 copy-start.5
  41.7 16.9 %collective-permute-start.3 = (f32[53,8,128]{2,1,0:T(8,128)S(1)}, f32[53,8,128]{2,1,0:T(8,128)S(1)}, u32[]{:S(2)}, u32[]{:S(2)}) collective-permute-start(f32[53,8,128]{2,1,0:T(8,128)S(1)} %get-tuple-element.84), channel_id=1, source_target_pairs={{32,64},{96,128},{160,192},{224,256},{288,320},{352,384},{416,448}... | collective-permute-start | bytes 651272 | tf_op jit(solution)/shard_map/ppermute | solution.py:741
  50.9 7.8 %collective-permute-start.4 = (f32[53,8,128]{2,1,0:T(8,128)S(1)}, f32[53,8,128]{2,1,0:T(8,128)S(1)}, u32[]{:S(2)}, u32[]{:S(2)}) collective-permute-start(f32[53,8,128]{2,1,0:T(8,128)S(1)} %get-tuple-element.85), channel_id=1, source_target_pairs={{0,32},{64,96},{128,160},{192,224},{256,288},{320,352},{384,416},{... | collective-permute-start | bytes 651272 | tf_op jit(solution)/shard_map/ppermute | solution.py:741
  58.9 11.9 %collective-permute-start.5 = (f32[464,128]{1,0:T(8,128)S(1)}, f32[464,128]{1,0:T(8,128)S(1)}, u32[]{:S(2)}, u32[]{:S(2)}) collective-permute-start(f32[464,128]{1,0:T(8,128)S(1)} %get-tuple-element.86), channel_id=1, source_target_pairs={{1,2},{3,4},{5,6},{7,8},{9,10},{11,12},{13,14},{15,16},{17,18},{19... | collective-permute-start | bytes 712712 | tf_op jit(solution)/shard_map/ppermute | solution.py:741
  65.3 5.5 %copy-start.2 = (f32[5,4,8,128]{3,2,1,0:T(8,128)S(1)}, f32[5,4,8,128]{3,2,1,0:T(8,128)}, u32[]{:S(2)}) copy-start(f32[5,4,8,128]{3,2,1,0:T(8,128)} %get-tuple-element.78.speed_zero) | copy-start | bytes 245764
  65.3 5.5 %copy-start.3 = (f32[4,8,128]{2,1,0:T(8,128)S(1)}, f32[4,8,128]{2,1,0:T(8,128)}, u32[]{:S(2)}) copy-start(f32[4,8,128]{2,1,0:T(8,128)} %porosity.3) | copy-start | bytes 49156
